TPU v7x, 768 devices: a whole 4x8x12 slice. The times are simulated.
768 devices in a mesh: seg: 64 (over x, y, core), sub: 12 (over z).
Axes of the slice: x: 4, y: 8, z: 12, core: 2. Of those that a mesh axis runs over, the one named last changes fastest.
Arguments:
- fields: float32 [7, 2048, 1536], P(None, 'seg', 'sub'), may hold values from -1.5 to 3, as said below
- region_levels: int32 [64, 12], replicated, may hold values from 0 to 2, as said below
Outputs:
- new_fields: float32 [7, 2048, 1536], P(None, 'seg', 'sub')
Inputs may be any that keep to these rules, and one draw needn't show every extreme that they name: `region_levels`: root regions sharing a side or a corner differ by at most one level; some root region is at level 2. `fields`: component 0 (density) lies between 1 and 3; tile entries in a tile's unused room are not read.
All inputs are finite; a program needn't handle non-finite values.
Results may differ from a plain program's by a relative error of at most 0.0003.
Values sent between devices are 32-bit elements; how exact they have to be, the bound alone decides.
No kernel may reach another device: no remote copies, remote signals or barrier semaphores. Data moves between devices by JAX's collectives and lax.ppermute only.
A program may use at most 64 MiB of HBM per device.

v0:
```python
from functools import partial

import jax
import jax.numpy as jnp
from jax import lax
from jax.experimental import pallas as pl
from jax.experimental.pallas import tpu as pltpu
from jax.sharding import PartitionSpec as P

STEP_SIZE = 0.08
ROWS, COLS = 32, 128
F32 = jnp.float32
VMEM = pl.BlockSpec(memory_space=pltpu.VMEM)
SMEM = pl.BlockSpec(memory_space=pltpu.SMEM)

PAD = 8


def lane(rows):
    return lax.broadcasted_iota(jnp.int32, (rows, COLS), 1)


def gather_lanes(value, index):
    return jnp.take_along_axis(value, index, axis=1, mode="promise_in_bounds")


def near_level(levels_ref, row, col):
    seg_count, sub_count = levels_ref.shape
    s = lax.rem(lax.axis_index("seg") + (row + seg_count), seg_count)
    u = lax.rem(lax.axis_index("sub") + (col + sub_count), sub_count)
    return levels_ref[s, u]


def rows_kernel(levels_ref, fields_ref, low_ref, high_ref):
    start = 8 * (1 << near_level(levels_ref, 0, 0)) - 8
    for f in range(7):
        low_ref[f] = fields_ref[f, 0:8, :]
        high_ref[f] = fields_ref[f, pl.ds(pl.multiple_of(start, 8), 8), :]


def cols_kernel(levels_ref, fields_ref, below_ref, above_ref, out_ref):
    def pack(read, rows, level):
        p = lane(rows)
        first = 32 * (1 << level) - 8
        index = (p & 7) + jnp.where((p & 15) < 8, first, 0)
        packed = gather_lanes(read(0), index)
        for f in range(1, 7):
            packed = jnp.where((p >> 4) == f, gather_lanes(read(f), index), packed)
        return packed

    out_ref[0:8, :] = pack(lambda f: below_ref[f], 8, near_level(levels_ref, -1, 0))
    out_ref[8:40, :] = pack(lambda f: fields_ref[f], 32, near_level(levels_ref, 0, 0))
    out_ref[40:48, :] = pack(lambda f: above_ref[f], 8, near_level(levels_ref, 1, 0))


def minmod(a, b):
    return jnp.maximum(jnp.minimum(a, b), 0.0) + jnp.minimum(jnp.maximum(a, b), 0.0)


def side(state, normal):
    density, speed_n, speed_t, speed_z, field_t, field_z = state
    normal_square = normal * normal
    field_square = normal_square + field_t * field_t + field_z * field_z
    moment = density * speed_n
    fluxes = [
        moment,
        moment * speed_n + (density + 0.5 * field_square) - normal_square,
        moment * speed_t - normal * field_t,
        moment * speed_z - normal * field_z,
        field_t * speed_n - normal * speed_t,
        field_z * speed_n - normal * speed_z,
    ]
    conserved = [density, moment, density * speed_t, density * speed_z, field_t, field_z]
    signal = jnp.abs(speed_n) + jnp.sqrt(1.0 + field_square / density)
    return fluxes, conserved, signal


def riemann(left, right, normal):
    flux_left, cons_left, signal_left = side(left, normal)
    flux_right, cons_right, signal_right = side(right, normal)
    fastest = jnp.maximum(signal_left, signal_right)
    return [
        0.5 * ((a + b) - fastest * (d - c))
        for a, b, c, d in zip(flux_left, flux_right, cons_left, cons_right)
    ]


def main_kernel(
    levels_ref,
    fields_ref,
    below_ref,
    above_ref,
    left_ref,
    right_ref,
    out_ref,
    win,
    prim,
    lefty,
    diffx,
    fluxy,
    gx,
    edge,
    lev,
    corner,
    tmp,
):
    near = [[near_level(levels_ref, i, j) for j in (-1, 0, 1)] for i in (-1, 0, 1)]
    own_level = near[1][1]
    p32 = lane(32)
    p24 = lane(24)
    p16 = lane(16)
    p8 = lane(8)
    coarse32 = (p32 >= 72) & (p32 < 120)

    def by_cols(row, rows, kind):
        p = lane(rows)
        first, middle, last = near[row]
        if kind == 0:
            return jnp.full((rows, COLS), middle, jnp.int32)
        if kind == 1:
            return jnp.where(p < 64, last, first)
        inner = (p < 64) | ((p >= 80) & (p < 112))
        outer = ((p >= 64) & (p < 72)) | ((p >= 112) & (p < 120))
        return jnp.where(inner, middle, jnp.where(outer, last, first))

    for kind in range(2):
        lev[kind, 0:8, :] = by_cols(0, 8, kind)
        lev[kind, 8:40, :] = by_cols(1, 32, kind)
        lev[kind, 40:48, :] = by_cols(2, 8, kind)
    is_coarse = (p8 >= 72) & (p8 < 120)
    centre_row = by_cols(1, 8, 2)
    top_row = by_cols(2, 8, 2)
    lev[2, 0:8, :] = by_cols(0, 8, 2)
    lev[2, 8:16, :] = centre_row
    lev[2, 16:24, :] = jnp.where(is_coarse, top_row, centre_row)
    lev[2, 24:32, :] = top_row
    beside = lev[2, 0:32, :]
    beside = jnp.maximum(beside, pltpu.roll(beside, 1, 1))
    corner[...] = jnp.maximum(beside, pltpu.roll(beside, 1, 0))

    p48 = lane(48)
    strips = jnp.where((p48 & 15) < 8, left_ref[...], right_ref[...])
    strip = ((p8 >= 64) & (p8 < 80)) | (p8 >= 112)
    right_strip = ((p8 >= 64) & (p8 < 72)) | ((p8 >= 112) & (p8 < 120))
    strip_index = (p8 & 7) + jnp.where(right_strip, 8, 0)
    for f in range(7):
        win[f, 0, PAD : PAD + 8, :] = below_ref[f]
        win[f, 0, PAD + 8 : PAD + 40, :] = fields_ref[f]
        win[f, 0, PAD + 40 : PAD + 48, :] = above_ref[f]
        win[f, 1, PAD : PAD + 48, :] = pltpu.roll(strips, (120 - 16 * f) % 128, 1)
        index = strip_index + 16 * f
        packed = [gather_lanes(strips[r : r + 8], index) for r in (0, 8, 16, 40)]

        def joined(fine, coarse):
            return jnp.where(p8 < 72, fine, pltpu.roll(coarse, 80, 1))

        below, above = below_ref[f], above_ref[f]
        near_rows, next_rows = fields_ref[f, 0:8, :], fields_ref[f, 8:16, :]
        win[f, 2, PAD : PAD + 8, :] = jnp.where(strip, packed[0], joined(below, below))
        win[f, 2, PAD + 8 : PAD + 16, :] = jnp.where(
            strip, packed[1], joined(near_rows, near_rows)
        )
        win[f, 2, PAD + 16 : PAD + 24, :] = jnp.where(
            strip, jnp.where(is_coarse, packed[3], packed[2]), joined(next_rows, above)
        )
        win[f, 2, PAD + 24 : PAD + 32, :] = jnp.where(strip, packed[3], above)

    index_up_one = jnp.where(p32 < 72, 80 + (p32 >> 1), jnp.where(p32 >= 120, 16 + (p32 >> 1), p32))
    index_up_two = (p32 >> 1, 64 + (p32 >> 1))
    index_down_two = (2 * p24) & 127
    index_down_one = (2 * (p16 - 80)) & 127

    def doubled(value, first, count, slot):
        tmp[slot, 0:32, :] = value
        part = tmp[slot, pl.ds(first, count), :]
        tmp[slot + 1, pl.ds(0, count, stride=2), :] = part
        tmp[slot + 1, pl.ds(1, count, stride=2), :] = part
        return tmp[slot + 1, 0 : 2 * count, :]

    def rows_halved(ref, first, count, by_rows):
        initial = ref[pl.ds(first, count, stride=2), :]
        if not by_rows:
            return initial
        return 0.5 * (initial + ref[pl.ds(first + 1, count, stride=2), :])

    def cols_halved(value, by_cols):
        return 0.5 * (value + pltpu.roll(value, 127, 1)) if by_cols else value

    def down_two(ref0, ref1, first, by_rows, by_cols, slot):
        parts = [cols_halved(rows_halved(ref, first, 24, by_rows), by_cols) for ref in (ref0, ref1)]
        parts = [gather_lanes(part, index_down_two) for part in parts]
        tmp[slot, 4:28, :] = jnp.where(p24 < 64, parts[0], parts[1])
        return tmp[slot, 0:32, :]

    def down_one(ref, first, by_rows, by_cols, slot):
        part = cols_halved(rows_halved(ref, first, 16, by_rows), by_cols)
        tmp[slot, 4:20, :] = gather_lanes(part, index_down_one)
        return tmp[slot, 0:32, :]

    def share():
        level_b = lev[2, 0:32, :]
        fine_a = [lev[k, 0:48, :] == 2 for k in range(2)]
        for f in range(7):
            by_rows, by_cols = f != 6, f != 5
            value = win[f, 2, PAD : PAD + 32, :]
            injected = doubled(gather_lanes(value, index_up_one), 4, 16, 0)
            value = jnp.where((level_b == 0) & ~coarse32, injected, value)
            for k in range(2):
                injected = doubled(gather_lanes(value, index_up_two[k]), 4, 24, 2 + 2 * k)
                win[f, k, PAD : PAD + 48, :] = jnp.where(
                    fine_a[k], win[f, k, PAD : PAD + 48, :], injected
                )
            halved = down_two(win.at[f, 0], win.at[f, 1], PAD, by_rows, by_cols, 6)
            value = jnp.where((level_b == 2) & ~coarse32, halved, value)
            win[f, 2, PAD : PAD + 32, :] = value
            halved = down_one(win.at[f, 2], PAD, by_rows, by_cols, 7)
            win[f, 2, PAD : PAD + 32, :] = jnp.where((level_b >= 1) & coarse32, halved, value)

    def load(ref, fields, wide, row):
        if wide:
            return jnp.concatenate([ref[*fields, k, pl.ds(row, 8), :] for k in range(2)], axis=0)
        return ref[*fields, 2, pl.ds(row, 16), :]

    def store(ref, fields, wide, row, value):
        if wide:
            for k in range(2):
                ref[*fields, k, pl.ds(row, 8), :] = value[8 * k : 8 * k + 8]
        else:
            ref[*fields, 2, pl.ds(row, 16), :] = value

    def shifted(value, wide, back):
        moved = pltpu.roll(value, 1 if back else 127, 1)
        if not wide:
            return moved
        other = jnp.concatenate([moved[8:], moved[:8]], axis=0)
        return jnp.where(p16 == (0 if back else 127), other, moved)

    def over_chunks(body):
        for c in range(6):
            body(True, PAD + 8 * c)
        for c in range(2):
            body(False, PAD + 16 * c)

    def primitives(wide, row):
        inverse = 1.0 / load(win, (0,), wide, row)
        for i in range(3):
            store(prim, (i,), wide, row, load(win, (1 + i,), wide, row) * inverse)
        face_x = load(win, (5,), wide, row)
        store(prim, (3,), wide, row, 0.5 * (face_x + shifted(face_x, wide, False)))
        face_y = load(win, (6,), wide, row)
        store(prim, (4,), wide, row, 0.5 * (face_y + load(win, (6,), wide, row + 1)))

    RHO, VX, VY, VZ, CX, CY, BZ = (
        (win, 0),
        (prim, 0),
        (prim, 1),
        (prim, 2),
        (prim, 3),
        (prim, 4),
        (win, 4),
    )

    def sweeps(wide, row):
        def at(item, step=0):
            return load(item[0], (item[1],), wide, row + step)

        left, right = [], []
        for item in (RHO, VX, VY, VZ, CY, BZ):
            value = at(item)
            before = value - shifted(value, wide, True)
            slope = 0.5 * minmod(before, shifted(before, wide, False))
            left.append(shifted(value + slope, wide, True))
            right.append(value - slope)
        flux = riemann(left, right, at((win, 5)))
        for i, n in enumerate((0, 1, 2, 3, 5)):
            store(diffx, (i,), wide, row, shifted(flux[n], wide, False) - flux[n])
        flux_by = flux[4]
        store(gx, (), wide, row, flux_by)
        left, right = [], []
        for i, item in enumerate((RHO, VY, VX, VZ, CX, BZ)):
            value = at(item)
            slope = 0.5 * minmod(value - at(item, -1), at(item, 1) - value)
            store(lefty, (i,), wide, row, value + slope)
            left.append(load(lefty, (i,), wide, row - 1))
            right.append(value - slope)
        flux = riemann(left, right, at((win, 6)))
        for i, n in enumerate((0, 2, 1, 3, 5)):
            store(fluxy, (i,), wide, row, flux[n])
        flux_bx = flux[4]
        value = (flux_bx + shifted(flux_bx, wide, True)) - (flux_by + load(gx, (), wide, row - 1))
        store(edge, (), wide, row, 0.25 * value)

    ratio_b = jnp.where((p16 >= 72) & (p16 < 120), STEP_SIZE / 4, STEP_SIZE / 2)

    def correct():
        value = edge[2, PAD : PAD + 32, :]
        finest = corner[...]
        halved_two = down_two(edge.at[0], edge.at[1], PAD, False, False, 6)
        halved_one = down_one(edge.at[2], PAD, False, False, 7)
        value = jnp.where((finest == 2) & ~coarse32, halved_two, value)
        edge[2, PAD : PAD + 32, :] = jnp.where((finest >= 1) & coarse32, halved_one, value)

    def update(wide, row):
        ratio = STEP_SIZE if wide else ratio_b
        for i in range(5):
            change = load(diffx, (i,), wide, row) + (
                load(fluxy, (i,), wide, row + 1) - load(fluxy, (i,), wide, row)
            )
            store(win, (i,), wide, row, load(win, (i,), wide, row) - ratio * change)
        value = load(edge, (), wide, row)
        diff_x = load(edge, (), wide, row + 1) - value
        diff_y = shifted(value, wide, False) - value
        store(win, (5,), wide, row, load(win, (5,), wide, row) - ratio * diff_x)
        store(win, (6,), wide, row, load(win, (6,), wide, row) + ratio * diff_y)

    for _ in range(2):
        share()
        over_chunks(primitives)
        over_chunks(sweeps)
        correct()
        over_chunks(update)

    zero = jnp.zeros((8, COLS), F32)
    for f in range(7):
        for c in range(4):
            value = win[f, 0, PAD + 8 + 8 * c : PAD + 16 + 8 * c, :]
            if c < 2:
                medium = win[f, 2, PAD + 8 + 8 * c : PAD + 16 + 8 * c, :]
                coarse = pltpu.roll(medium, 48, 1) if c == 0 else zero
                lower = jnp.where(own_level == 1, medium, coarse)
                value = jnp.where(own_level == 2, value, lower)
            rows = 8 << own_level
            used = (8 * c < rows) & (p8 < (32 << own_level))
            blend = 0.5 * (fields_ref[f, 8 * c : 8 * c + 8, :] + value)
            out_ref[f, 8 * c : 8 * c + 8, :] = jnp.where(used, blend, 0.0)


def moved(value, axis, step):
    size = lax.axis_size(axis)
    return lax.ppermute(value, axis, [(i, (i + step) % size) for i in range(size)])


def on_device(fields, region_levels):
    shape = jax.ShapeDtypeStruct
    params = pltpu.CompilerParams(vmem_limit_bytes=32 * 1024 * 1024)
    rows = shape((7, 8, COLS), F32)
    low, high = pl.pallas_call(
        rows_kernel, out_shape=(rows, rows), in_specs=[SMEM, VMEM], out_specs=(VMEM, VMEM)
    )(region_levels, fields)
    below = moved(high, "seg", 1)
    above = moved(low, "seg", -1)
    packed = pl.pallas_call(
        cols_kernel,
        out_shape=shape((48, COLS), F32),
        in_specs=[SMEM, VMEM, VMEM, VMEM],
        out_specs=VMEM,
        compiler_params=params,
    )(region_levels, fields, below, above)
    left = moved(packed, "sub", 1)
    right = moved(packed, "sub", -1)

    def window(*lead):
        return pltpu.VMEM((*lead, 3, PAD + 56, COLS), F32)

    return pl.pallas_call(
        main_kernel,
        out_shape=shape(fields.shape, F32),
        in_specs=[SMEM, VMEM, VMEM, VMEM, VMEM, VMEM],
        out_specs=VMEM,
        scratch_shapes=[
            window(7),
            window(5),
            window(6),
            window(5),
            window(5),
            window(),
            window(),
            pltpu.VMEM((3, 48, COLS), jnp.int32),
            pltpu.VMEM((32, COLS), jnp.int32),
            pltpu.VMEM((8, 48, COLS), F32),
        ],
        compiler_params=params,
    )(region_levels, fields, below, above, left, right)


def solution(mesh):
    placed = (P(None, "seg", "sub"), P())
    return jax.shard_map(
        on_device, mesh=mesh, in_specs=placed, out_specs=P(None, "seg", "sub"), check_vma=False
    )
```

profile of v0, /device:TPU:31, one launch (start us, length us, event | category | flops | bytes accessed | tf_op | source)
XLA Modules:
  0.0 47.1 jit_solution(3795300522090451802)
XLA Ops:
  0.0 0.0 copy-start
  0.0 1.4 %copy.5.levels_ref = s32[64,12]{1,0:T(8,128)} copy(s32[64,12]{0,1:T(8,128)} %param.3) | data formatting | bytes 6144 | tf_op args[1]
  1.4 0.0 copy-start.1
  1.4 2.0 %shard_map.28 = (f32[7,8,128]{2,1,0:T(8,128)}, f32[7,8,128]{2,1,0:T(8,128)}) custom-call(s32[64,12]{1,0:T(8,128)} %copy.5.levels_ref, f32[7,32,128]{2,1,0:T(8,128)} %fields_ref.5), custom_call_target="tpu_custom_call" | custom-call | tf_op jit(solution)/shard_map/pallas_call | solution.py:347
  3.4 5.0 %collective-permute-start = (f32[7,8,128]{2,1,0:T(8,128)}, f32[7,8,128]{2,1,0:T(8,128)S(1)}, u32[]{:S(2)}, u32[]{:S(2)}) collective-permute-start(f32[7,8,128]{2,1,0:T(8,128)} %get-tuple-element.7), channel_id=1, source_target_pairs={{0,12},{12,24},{24,36},{36,48},{48,60},{60,72},{72,84},{84,96},{96... | collective-permute-start | bytes 86024 | tf_op jit(solution)/shard_map/ppermute | solution.py:340
  8.4 1.9 %collective-permute-start.1 = (f32[7,8,128]{2,1,0:T(8,128)}, f32[7,8,128]{2,1,0:T(8,128)S(1)}, u32[]{:S(2)}, u32[]{:S(2)}) collective-permute-start(f32[7,8,128]{2,1,0:T(8,128)} %get-tuple-element.8), channel_id=1, source_target_pairs={{0,756},{12,0},{24,12},{36,24},{48,36},{60,48},{72,60},{84,72},{96... | collective-permute-start | bytes 86024 | tf_op jit(solution)/shard_map/ppermute | solution.py:340
  10.3 0.0 collective-permute-done.below_ref
  10.3 4.7 %collective-permute-done.1.above_ref = f32[7,8,128]{2,1,0:T(8,128)S(1)} collective-permute-done((f32[7,8,128]{2,1,0:T(8,128)}, f32[7,8,128]{2,1,0:T(8,128)S(1)}, u32[]{:S(2)}, u32[]{:S(2)}) %collective-permute-start.1) | collective-permute-done | bytes 28704 | tf_op jit(solution)/shard_map/ppermute | solution.py:340
  15.0 0.0 copy-done
  15.0 0.0 copy-done.1
  15.0 1.2 %shard_map.29 = f32[48,128]{1,0:T(8,128)S(1)} custom-call(s32[64,12]{1,0:T(8,128)S(1)} %copy-done.1, f32[7,32,128]{2,1,0:T(8,128)S(1)} %copy-done, f32[7,8,128]{2,1,0:T(8,128)S(1)} %collective-permute-done.below_ref, f32[7,8,128]{2,1,0:T(8,128)S(1)} %collective-permute-done.1.above_ref), custom_call_target="tpu_custom_call" | custom-call | tf_op jit(solution)/shard_map/pallas_call | solution.py:352
  16.2 14.3 %collective-permute-start.3 = (f32[48,128]{1,0:T(8,128)S(1)}, f32[48,128]{1,0:T(8,128)S(1)}, u32[]{:S(2)}, u32[]{:S(2)}) collective-permute-start(f32[48,128]{1,0:T(8,128)S(1)} %shard_map.29), channel_id=1, source_target_pairs={{0,11},{1,0},{2,1},{3,2},{4,3},{5,4},{6,5},{7,6},{8,7},{9,8},{10,9... | collective-permute-start | bytes 73736 | tf_op jit(solution)/shard_map/ppermute | solution.py:340
  30.5 1.9 %collective-permute-start.2 = (f32[48,128]{1,0:T(8,128)S(1)}, f32[48,128]{1,0:T(8,128)S(1)}, u32[]{:S(2)}, u32[]{:S(2)}) collective-permute-start(f32[48,128]{1,0:T(8,128)S(1)} %shard_map.29), channel_id=1, source_target_pairs={{0,1},{1,2},{2,3},{3,4},{4,5},{5,6},{6,7},{7,8},{8,9},{9,10},{10,1... | collective-permute-start | bytes 73736 | tf_op jit(solution)/shard_map/ppermute | solution.py:340
  32.5 0.0 collective-permute-done.3.right_ref
  32.5 3.8 %collective-permute-done.2.left_ref = f32[48,128]{1,0:T(8,128)S(1)} collective-permute-done((f32[48,128]{1,0:T(8,128)S(1)}, f32[48,128]{1,0:T(8,128)S(1)}, u32[]{:S(2)}, u32[]{:S(2)}) %collective-permute-start.2) | collective-permute-done | bytes 24608 | tf_op jit(solution)/shard_map/ppermute | solution.py:340
  36.3 10.7 %shard_map.30 = f32[7,32,128]{2,1,0:T(8,128)} custom-call(s32[64,12]{1,0:T(8,128)S(1)} %copy-done.1, f32[7,32,128]{2,1,0:T(8,128)S(1)} %copy-done, f32[7,8,128]{2,1,0:T(8,128)S(1)} %collective-permute-done.below_ref, f32[7,8,128]{2,1,0:T(8,128)S(1)} %collective-permute-done.1.above_ref, f32[48,128]{1,0:T(8,128)S(1)} %collective-permute-done.2.left_ref, ...), custom_call_target="tpu_custom_call" | custom-call | tf_op jit(solution)/shard_map/pallas_call | solution.py:365
Async XLA Ops:
  0.0 15.0 %copy-start = (f32[7,32,128]{2,1,0:T(8,128)S(1)}, f32[7,32,128]{2,1,0:T(8,128)}, u32[]{:S(2)}) copy-start(f32[7,32,128]{2,1,0:T(8,128)} %fields_ref.5) | copy-start | bytes 344068
  1.4 13.6 %copy-start.1 = (s32[64,12]{1,0:T(8,128)S(1)}, s32[64,12]{1,0:T(8,128)}, u32[]{:S(2)}) copy-start(s32[64,12]{1,0:T(8,128)} %copy.5.levels_ref) | copy-start | bytes 9220
  3.4 6.9 %collective-permute-start = (f32[7,8,128]{2,1,0:T(8,128)}, f32[7,8,128]{2,1,0:T(8,128)S(1)}, u32[]{:S(2)}, u32[]{:S(2)}) collective-permute-start(f32[7,8,128]{2,1,0:T(8,128)} %get-tuple-element.7), channel_id=1, source_target_pairs={{0,12},{12,24},{24,36},{36,48},{48,60},{60,72},{72,84},{84,96},{96... | collective-permute-start | bytes 86024 | tf_op jit(solution)/shard_map/ppermute | solution.py:340
  8.4 6.6 %collective-permute-start.1 = (f32[7,8,128]{2,1,0:T(8,128)}, f32[7,8,128]{2,1,0:T(8,128)S(1)}, u32[]{:S(2)}, u32[]{:S(2)}) collective-permute-start(f32[7,8,128]{2,1,0:T(8,128)} %get-tuple-element.8), channel_id=1, source_target_pairs={{0,756},{12,0},{24,12},{36,24},{48,36},{60,48},{72,60},{84,72},{96... | collective-permute-start | bytes 86024 | tf_op jit(solution)/shard_map/ppermute | solution.py:340
  16.2 16.2 %collective-permute-start.3 = (f32[48,128]{1,0:T(8,128)S(1)}, f32[48,128]{1,0:T(8,128)S(1)}, u32[]{:S(2)}, u32[]{:S(2)}) collective-permute-start(f32[48,128]{1,0:T(8,128)S(1)} %shard_map.29), channel_id=1, source_target_pairs={{0,11},{1,0},{2,1},{3,2},{4,3},{5,4},{6,5},{7,6},{8,7},{9,8},{10,9... | collective-permute-start | bytes 73736 | tf_op jit(solution)/shard_map/ppermute | solution.py:340
  30.5 5.8 %collective-permute-start.2 = (f32[48,128]{1,0:T(8,128)S(1)}, f32[48,128]{1,0:T(8,128)S(1)}, u32[]{:S(2)}, u32[]{:S(2)}) collective-permute-start(f32[48,128]{1,0:T(8,128)S(1)} %shard_map.29), channel_id=1, source_target_pairs={{0,1},{1,2},{2,3},{3,4},{4,5},{5,6},{6,7},{7,8},{8,9},{9,10},{10,1... | collective-permute-start | bytes 73736 | tf_op jit(solution)/shard_map/ppermute | solution.py:340
where the time goes:
time: 47.3 us; the launch traced here: 47.1 us
  starting transfers between devices  23.1 us (49%)
  Pallas kernels  13.9 us (29%)
  waiting for transfers between devices  8.52 us (18%)
  local copies, waits for them, and re-layouts  1.44 us (3%)
    ppermute x4, starting transfers between devices, moved(): lax.ppermute(value, axis, [(i, (i + step) % size) for i in range(size)])  23.1 us
    pallas_call x1, Pallas kernels, on_device(): pl.pallas_call(main_kernel, out_shape=shape(fields.shape, F32), in_specs=...  10.7 us
    ppermute x4, waiting for transfers between devices, moved(): lax.ppermute(value, axis, [(i, (i + step) % size) for i in range(size)])  8.52 us
    pallas_call x1, Pallas kernels, on_device(): pl.pallas_call(rows_kernel, out_shape=(rows, rows), in_specs=[SMEM, VMEM]...  1.96 us
    unnamed x5, local copies, waits for them, and re-layouts  1.44 us
    pallas_call x1, Pallas kernels, on_device(): pl.pallas_call(cols_kernel, out_shape=shape((48, COLS), F32), in_specs=[S...  1.22 us
  transfers between devices with their start and end apart: 4, of which 2 were waited for; matrix products, arithmetic and copies ran while one was open for 0% of the time, Pallas kernels for 0%

commit v1 on v0

--- a/solution.py
+++ b/solution.py
@@ -11,7 +11,6 @@
 ROWS, COLS = 32, 128
 F32 = jnp.float32
 VMEM = pl.BlockSpec(memory_space=pltpu.VMEM)
-SMEM = pl.BlockSpec(memory_space=pltpu.SMEM)
 
 PAD = 8
 
@@ -24,33 +23,47 @@
     return jnp.take_along_axis(value, index, axis=1, mode="promise_in_bounds")
 
 
-def near_level(levels_ref, row, col):
+def near_rows(levels_ref, held_ref):
     seg_count, sub_count = levels_ref.shape
-    s = lax.rem(lax.axis_index("seg") + (row + seg_count), seg_count)
-    u = lax.rem(lax.axis_index("sub") + (col + sub_count), sub_count)
-    return levels_ref[s, u]
-
-
-def rows_kernel(levels_ref, fields_ref, low_ref, high_ref):
-    start = 8 * (1 << near_level(levels_ref, 0, 0)) - 8
-    for f in range(7):
-        low_ref[f] = fields_ref[f, 0:8, :]
-        high_ref[f] = fields_ref[f, pl.ds(pl.multiple_of(start, 8), 8), :]
-
-
-def cols_kernel(levels_ref, fields_ref, below_ref, above_ref, out_ref):
-    def pack(read, rows, level):
-        p = lane(rows)
-        first = 32 * (1 << level) - 8
+    sub = lax.axis_index("sub")
+    for i in range(3):
+        s = lax.rem(lax.axis_index("seg") + (i - 1 + seg_count), seg_count)
+        held_ref[8 * i : 8 * i + 1, 0:sub_count] = levels_ref[pl.ds(s, 1), :]
+
+    def level_of(i, offset):
+        row = jnp.broadcast_to(held_ref[8 * i : 8 * i + 1, :], (8, COLS))
+        u = sub + offset
+        u = jnp.where(u < 0, u + sub_count, jnp.where(u >= sub_count, u - sub_count, u))
+        return gather_lanes(row, u)
+
+    return level_of
+
+
+def last_rows(ref, f, level):
+    return jnp.where(
+        level == 2, ref[f, 24:32, :], jnp.where(level == 1, ref[f, 8:16, :], ref[f, 0:8, :])
+    )
+
+
+def cols_kernel(levels_ref, fields_ref, below_ref, above_ref, out_ref, held):
+    level_of = near_rows(levels_ref, held)
+    p = lane(8)
+
+    def pack(read, level):
+        first = jnp.where(level == 2, 120, jnp.where(level == 1, 56, 24))
         index = (p & 7) + jnp.where((p & 15) < 8, first, 0)
         packed = gather_lanes(read(0), index)
         for f in range(1, 7):
             packed = jnp.where((p >> 4) == f, gather_lanes(read(f), index), packed)
         return packed
 
-    out_ref[0:8, :] = pack(lambda f: below_ref[f], 8, near_level(levels_ref, -1, 0))
-    out_ref[8:40, :] = pack(lambda f: fields_ref[f], 32, near_level(levels_ref, 0, 0))
-    out_ref[40:48, :] = pack(lambda f: above_ref[f], 8, near_level(levels_ref, 1, 0))
+    none = jnp.zeros((8, COLS), jnp.int32)
+    level = level_of(0, none)
+    out_ref[0:8, :] = pack(lambda f: last_rows(below_ref, f, level), level)
+    own = level_of(1, none)
+    for r in range(0, 32, 8):
+        out_ref[8 + r : 16 + r, :] = pack(lambda f: fields_ref[f, r : r + 8, :], own)
+    out_ref[40:48, :] = pack(lambda f: above_ref[f, 0:8, :], level_of(2, none))
 
 
 def minmod(a, b):
@@ -103,37 +116,33 @@
     lev,
     corner,
     tmp,
+    held,
 ):
-    near = [[near_level(levels_ref, i, j) for j in (-1, 0, 1)] for i in (-1, 0, 1)]
-    own_level = near[1][1]
+    level_of = near_rows(levels_ref, held)
     p32 = lane(32)
     p24 = lane(24)
     p16 = lane(16)
     p8 = lane(8)
     coarse32 = (p32 >= 72) & (p32 < 120)
 
-    def by_cols(row, rows, kind):
-        p = lane(rows)
-        first, middle, last = near[row]
-        if kind == 0:
-            return jnp.full((rows, COLS), middle, jnp.int32)
-        if kind == 1:
-            return jnp.where(p < 64, last, first)
-        inner = (p < 64) | ((p >= 80) & (p < 112))
-        outer = ((p >= 64) & (p < 72)) | ((p >= 112) & (p < 120))
-        return jnp.where(inner, middle, jnp.where(outer, last, first))
-
-    for kind in range(2):
-        lev[kind, 0:8, :] = by_cols(0, 8, kind)
-        lev[kind, 8:40, :] = by_cols(1, 32, kind)
-        lev[kind, 40:48, :] = by_cols(2, 8, kind)
+    inner = (p8 < 64) | ((p8 >= 80) & (p8 < 112))
+    outer = ((p8 >= 64) & (p8 < 72)) | ((p8 >= 112) & (p8 < 120))
+    middle = jnp.zeros((8, COLS), jnp.int32)
+    offsets = (middle, jnp.where(p8 < 64, 1, -1), jnp.where(inner, 0, jnp.where(outer, 1, -1)))
     is_coarse = (p8 >= 72) & (p8 < 120)
-    centre_row = by_cols(1, 8, 2)
-    top_row = by_cols(2, 8, 2)
-    lev[2, 0:8, :] = by_cols(0, 8, 2)
-    lev[2, 8:16, :] = centre_row
-    lev[2, 16:24, :] = jnp.where(is_coarse, top_row, centre_row)
-    lev[2, 24:32, :] = top_row
+    for kind in range(3):
+        below_row, centre_row, above_row = (level_of(i, offsets[kind]) for i in range(3))
+        lev[kind, 0:8, :] = below_row
+        lev[kind, 8:16, :] = centre_row
+        if kind == 2:
+            lev[kind, 16:24, :] = jnp.where(is_coarse, above_row, centre_row)
+            lev[kind, 24:32, :] = above_row
+        else:
+            for r in (16, 24, 32):
+                lev[kind, r : r + 8, :] = centre_row
+            lev[kind, 40:48, :] = above_row
+    own_level = lev[0, 8:16, :]
+    below_level = lev[0, 0:8, :]
     beside = lev[2, 0:32, :]
     beside = jnp.maximum(beside, pltpu.roll(beside, 1, 1))
     corner[...] = jnp.maximum(beside, pltpu.roll(beside, 1, 0))
@@ -144,9 +153,10 @@
     right_strip = ((p8 >= 64) & (p8 < 72)) | ((p8 >= 112) & (p8 < 120))
     strip_index = (p8 & 7) + jnp.where(right_strip, 8, 0)
     for f in range(7):
-        win[f, 0, PAD : PAD + 8, :] = below_ref[f]
+        below, above = last_rows(below_ref, f, below_level), above_ref[f, 0:8, :]
+        win[f, 0, PAD : PAD + 8, :] = below
         win[f, 0, PAD + 8 : PAD + 40, :] = fields_ref[f]
-        win[f, 0, PAD + 40 : PAD + 48, :] = above_ref[f]
+        win[f, 0, PAD + 40 : PAD + 48, :] = above
         win[f, 1, PAD : PAD + 48, :] = pltpu.roll(strips, (120 - 16 * f) % 128, 1)
         index = strip_index + 16 * f
         packed = [gather_lanes(strips[r : r + 8], index) for r in (0, 8, 16, 40)]
@@ -154,14 +164,13 @@
         def joined(fine, coarse):
             return jnp.where(p8 < 72, fine, pltpu.roll(coarse, 80, 1))
 
-        below, above = below_ref[f], above_ref[f]
-        near_rows, next_rows = fields_ref[f, 0:8, :], fields_ref[f, 8:16, :]
+        initial, second = fields_ref[f, 0:8, :], fields_ref[f, 8:16, :]
         win[f, 2, PAD : PAD + 8, :] = jnp.where(strip, packed[0], joined(below, below))
         win[f, 2, PAD + 8 : PAD + 16, :] = jnp.where(
-            strip, packed[1], joined(near_rows, near_rows)
+            strip, packed[1], joined(initial, initial)
         )
         win[f, 2, PAD + 16 : PAD + 24, :] = jnp.where(
-            strip, jnp.where(is_coarse, packed[3], packed[2]), joined(next_rows, above)
+            strip, jnp.where(is_coarse, packed[3], packed[2]), joined(second, above)
         )
         win[f, 2, PAD + 24 : PAD + 32, :] = jnp.where(strip, packed[3], above)
 
@@ -329,8 +338,8 @@
                 coarse = pltpu.roll(medium, 48, 1) if c == 0 else zero
                 lower = jnp.where(own_level == 1, medium, coarse)
                 value = jnp.where(own_level == 2, value, lower)
-            rows = 8 << own_level
-            used = (8 * c < rows) & (p8 < (32 << own_level))
+            used = p8 < jnp.where(own_level == 2, 128, jnp.where(own_level == 1, 64, 32))
+            used = used & (own_level >= (0, 1, 2, 2)[c])
             blend = 0.5 * (fields_ref[f, 8 * c : 8 * c + 8, :] + value)
             out_ref[f, 8 * c : 8 * c + 8, :] = jnp.where(used, blend, 0.0)
 
@@ -343,21 +352,18 @@
 def on_device(fields, region_levels):
     shape = jax.ShapeDtypeStruct
     params = pltpu.CompilerParams(vmem_limit_bytes=32 * 1024 * 1024)
-    rows = shape((7, 8, COLS), F32)
-    low, high = pl.pallas_call(
-        rows_kernel, out_shape=(rows, rows), in_specs=[SMEM, VMEM], out_specs=(VMEM, VMEM)
-    )(region_levels, fields)
-    below = moved(high, "seg", 1)
-    above = moved(low, "seg", -1)
+    below = moved(fields, "seg", 1)
+    above = moved(fields, "seg", -1)
     packed = pl.pallas_call(
         cols_kernel,
         out_shape=shape((48, COLS), F32),
-        in_specs=[SMEM, VMEM, VMEM, VMEM],
+        in_specs=[VMEM] * 4,
         out_specs=VMEM,
+        scratch_shapes=[pltpu.VMEM((24, COLS), jnp.int32)],
         compiler_params=params,
     )(region_levels, fields, below, above)
+    right = moved(packed, "sub", -1)
     left = moved(packed, "sub", 1)
-    right = moved(packed, "sub", -1)
 
     def window(*lead):
         return pltpu.VMEM((*lead, 3, PAD + 56, COLS), F32)
@@ -365,7 +371,7 @@
     return pl.pallas_call(
         main_kernel,
         out_shape=shape(fields.shape, F32),
-        in_specs=[SMEM, VMEM, VMEM, VMEM, VMEM, VMEM],
+        in_specs=[VMEM] * 6,
         out_specs=VMEM,
         scratch_shapes=[
             window(7),
@@ -378,6 +384,7 @@
             pltpu.VMEM((3, 48, COLS), jnp.int32),
             pltpu.VMEM((32, COLS), jnp.int32),
             pltpu.VMEM((8, 48, COLS), F32),
+            pltpu.VMEM((24, COLS), jnp.int32),
         ],
         compiler_params=params,
     )(region_levels, fields, below, above, left, right)

time: 47.3 us -> 43.4 us (0.918)
  the two profiles are of different devices: /device:TPU:31 before, /device:TPU:6 now
where the time goes in v1:
time: 43.4 us; the launch traced here: 43.2 us
  starting transfers between devices  23.5 us (54%)
  waiting for transfers between devices  10.7 us (25%)
  Pallas kernels  7.23 us (17%)
  local copies, waits for them, and re-layouts  1.68 us (4%)
    ppermute x4, starting transfers between devices, moved(): lax.ppermute(value, axis, [(i, (i + step) % size) for i in range(size)])  23.5 us
    ppermute x4, waiting for transfers between devices, moved(): lax.ppermute(value, axis, [(i, (i + step) % size) for i in range(size)])  10.7 us
    pallas_call x1, Pallas kernels, on_device(): pl.pallas_call(main_kernel, out_shape=shape(fields.shape, F32), in_specs=...  7.02 us
    unnamed x3, local copies, waits for them, and re-layouts  1.68 us
  transfers between devices with their start and end apart: 4, of which 2 were waited for; matrix products, arithmetic and copies ran while one was open for 2% of the time, Pallas kernels for 0%

profile of v1, /device:TPU:6, one launch (start us, length us, event | category | flops | bytes accessed | tf_op | source)
XLA Modules:
  0.0 43.2 jit_solution(8869140232920049324)
XLA Ops:
  0.0 5.1 %collective-permute-start.1 = (f32[7,32,128]{2,1,0:T(8,128)}, f32[7,32,128]{2,1,0:T(8,128)S(1)}, u32[]{:S(2)}, u32[]{:S(2)}) collective-permute-start(f32[7,32,128]{2,1,0:T(8,128)} %fields_ref.3), channel_id=1, source_target_pairs={{0,756},{12,0},{24,12},{36,24},{48,36},{60,48},{72,60},{84,72},{96... | collective-permute-start | bytes 344072 | tf_op jit(solution)/shard_map/ppermute | solution.py:349
  5.1 1.9 %collective-permute-start = (f32[7,32,128]{2,1,0:T(8,128)}, f32[7,32,128]{2,1,0:T(8,128)S(1)}, u32[]{:S(2)}, u32[]{:S(2)}) collective-permute-start(f32[7,32,128]{2,1,0:T(8,128)} %fields_ref.3), channel_id=1, source_target_pairs={{0,12},{12,24},{24,36},{36,48},{48,60},{60,72},{72,84},{84,96},{96... | collective-permute-start | bytes 344072 | tf_op jit(solution)/shard_map/ppermute | solution.py:349
  7.0 0.8 %copy.4.levels_ref = s32[64,12]{1,0:T(8,128)S(1)} copy(s32[64,12]{0,1:T(8,128)} %param.3) | data formatting | bytes 6144 | tf_op args[1]
  7.8 0.0 collective-permute-done.1.above_ref
  7.8 5.7 %collective-permute-done.below_ref = f32[7,32,128]{2,1,0:T(8,128)S(1)} collective-permute-done((f32[7,32,128]{2,1,0:T(8,128)}, f32[7,32,128]{2,1,0:T(8,128)S(1)}, u32[]{:S(2)}, u32[]{:S(2)}) %collective-permute-start) | collective-permute-done | bytes 114720 | tf_op jit(solution)/shard_map/ppermute | solution.py:349
  13.5 0.0 copy-start
  13.5 0.9 %copy-done = f32[7,32,128]{2,1,0:T(8,128)S(1)} copy-done((f32[7,32,128]{2,1,0:T(8,128)S(1)}, f32[7,32,128]{2,1,0:T(8,128)}, u32[]{:S(2)}) %copy-start) | copy-done | bytes 114712
  14.4 0.2 shard_map.28
  14.6 14.6 %collective-permute-start.3 = (f32[48,128]{1,0:T(8,128)S(1)}, f32[48,128]{1,0:T(8,128)S(1)}, u32[]{:S(2)}, u32[]{:S(2)}) collective-permute-start(f32[48,128]{1,0:T(8,128)S(1)} %shard_map.28), channel_id=1, source_target_pairs={{0,11},{1,0},{2,1},{3,2},{4,3},{5,4},{6,5},{7,6},{8,7},{9,8},{10,9... | collective-permute-start | bytes 73736 | tf_op jit(solution)/shard_map/ppermute | solution.py:349
  29.2 1.9 %collective-permute-start.2 = (f32[48,128]{1,0:T(8,128)S(1)}, f32[48,128]{1,0:T(8,128)S(1)}, u32[]{:S(2)}, u32[]{:S(2)}) collective-permute-start(f32[48,128]{1,0:T(8,128)S(1)} %shard_map.28), channel_id=1, source_target_pairs={{0,1},{1,2},{2,3},{3,4},{4,5},{5,6},{6,7},{7,8},{8,9},{9,10},{10,1... | collective-permute-start | bytes 73736 | tf_op jit(solution)/shard_map/ppermute | solution.py:349
  31.1 0.0 collective-permute-done.3.right_ref
  31.2 5.0 %collective-permute-done.2.left_ref = f32[48,128]{1,0:T(8,128)S(1)} collective-permute-done((f32[48,128]{1,0:T(8,128)S(1)}, f32[48,128]{1,0:T(8,128)S(1)}, u32[]{:S(2)}, u32[]{:S(2)}) %collective-permute-start.2) | collective-permute-done | bytes 24608 | tf_op jit(solution)/shard_map/ppermute | solution.py:349
  36.2 7.0 %shard_map.29 = f32[7,32,128]{2,1,0:T(8,128)} custom-call(s32[64,12]{1,0:T(8,128)S(1)} %copy.4.levels_ref, f32[7,32,128]{2,1,0:T(8,128)S(1)} %copy-done, f32[7,32,128]{2,1,0:T(8,128)S(1)} %collective-permute-done.below_ref, f32[7,32,128]{2,1,0:T(8,128)S(1)} %collective-permute-done.1.above_ref, f32[48,128]{1,0:T(8,128)S(1)} %collective-permute-done.2.left_ref, ...), custom_call_target="tpu_custom_call" | custom-call | tf_op jit(solution)/shard_map/pallas_call | solution.py:371
Async XLA Ops:
  0.0 7.8 %collective-permute-start.1 = (f32[7,32,128]{2,1,0:T(8,128)}, f32[7,32,128]{2,1,0:T(8,128)S(1)}, u32[]{:S(2)}, u32[]{:S(2)}) collective-permute-start(f32[7,32,128]{2,1,0:T(8,128)} %fields_ref.3), channel_id=1, source_target_pairs={{0,756},{12,0},{24,12},{36,24},{48,36},{60,48},{72,60},{84,72},{96... | collective-permute-start | bytes 344072 | tf_op jit(solution)/shard_map/ppermute | solution.py:349
  5.1 8.4 %collective-permute-start = (f32[7,32,128]{2,1,0:T(8,128)}, f32[7,32,128]{2,1,0:T(8,128)S(1)}, u32[]{:S(2)}, u32[]{:S(2)}) collective-permute-start(f32[7,32,128]{2,1,0:T(8,128)} %fields_ref.3), channel_id=1, source_target_pairs={{0,12},{12,24},{24,36},{36,48},{48,60},{60,72},{72,84},{84,96},{96... | collective-permute-start | bytes 344072 | tf_op jit(solution)/shard_map/ppermute | solution.py:349
  13.5 0.9 %copy-start = (f32[7,32,128]{2,1,0:T(8,128)S(1)}, f32[7,32,128]{2,1,0:T(8,128)}, u32[]{:S(2)}) copy-start(f32[7,32,128]{2,1,0:T(8,128)} %fields_ref.3) | copy-start | bytes 344068
  14.6 16.5 %collective-permute-start.3 = (f32[48,128]{1,0:T(8,128)S(1)}, f32[48,128]{1,0:T(8,128)S(1)}, u32[]{:S(2)}, u32[]{:S(2)}) collective-permute-start(f32[48,128]{1,0:T(8,128)S(1)} %shard_map.28), channel_id=1, source_target_pairs={{0,11},{1,0},{2,1},{3,2},{4,3},{5,4},{6,5},{7,6},{8,7},{9,8},{10,9... | collective-permute-start | bytes 73736 | tf_op jit(solution)/shard_map/ppermute | solution.py:349
  29.2 6.9 %collective-permute-start.2 = (f32[48,128]{1,0:T(8,128)S(1)}, f32[48,128]{1,0:T(8,128)S(1)}, u32[]{:S(2)}, u32[]{:S(2)}) collective-permute-start(f32[48,128]{1,0:T(8,128)S(1)} %shard_map.28), channel_id=1, source_target_pairs={{0,1},{1,2},{2,3},{3,4},{4,5},{5,6},{6,7},{7,8},{8,9},{9,10},{10,1... | collective-permute-start | bytes 73736 | tf_op jit(solution)/shard_map/ppermute | solution.py:349

commit v2 on v1

v2 whole, which is shorter than its diff:
```python
from functools import partial

import jax
import jax.numpy as jnp
from jax import lax
from jax.experimental import pallas as pl
from jax.experimental.pallas import tpu as pltpu
from jax.sharding import PartitionSpec as P

STEP_SIZE = 0.08
ROWS, COLS = 32, 128
F32 = jnp.float32
VMEM = pl.BlockSpec(memory_space=pltpu.VMEM)

PAD = 8
TPAD = 16
MID, SIDE = PAD + 48, PAD + 80


def lane(rows):
    return lax.broadcasted_iota(jnp.int32, (rows, COLS), 1)


def gather_lanes(value, index):
    return jnp.take_along_axis(value, index, axis=1, mode="promise_in_bounds")


def near_rows(levels_ref, held_ref):
    seg_count, sub_count = levels_ref.shape
    sub = lax.axis_index("sub")
    for i in range(3):
        s = lax.rem(lax.axis_index("seg") + (i - 1 + seg_count), seg_count)
        held_ref[8 * i : 8 * i + 1, 0:sub_count] = levels_ref[pl.ds(s, 1), :]

    def level_of(i, offset):
        row = jnp.broadcast_to(held_ref[8 * i : 8 * i + 1, :], (8, COLS))
        u = sub + offset
        u = jnp.where(u < 0, u + sub_count, jnp.where(u >= sub_count, u - sub_count, u))
        return gather_lanes(row, u)

    return level_of


def last_rows(ref, f, level):
    return jnp.where(
        level == 2, ref[f, 24:32, :], jnp.where(level == 1, ref[f, 8:16, :], ref[f, 0:8, :])
    )


def cols_kernel(levels_ref, fields_ref, below_ref, above_ref, out_ref, held):
    level_of = near_rows(levels_ref, held)
    p = lane(8)

    def pack(read, level):
        first = jnp.where(level == 2, 120, jnp.where(level == 1, 56, 24))
        index = (p & 7) + jnp.where((p & 15) < 8, first, 0)
        packed = gather_lanes(read(0), index)
        for f in range(1, 7):
            packed = jnp.where((p >> 4) == f, gather_lanes(read(f), index), packed)
        return packed

    none = jnp.zeros((8, COLS), jnp.int32)
    level = level_of(0, none)
    out_ref[0:8, :] = pack(lambda f: last_rows(below_ref, f, level), level)
    own = level_of(1, none)
    for r in range(0, 32, 8):
        out_ref[8 + r : 16 + r, :] = pack(lambda f: fields_ref[f, r : r + 8, :], own)
    out_ref[40:48, :] = pack(lambda f: above_ref[f, 0:8, :], level_of(2, none))


def minmod(a, b):
    return jnp.maximum(jnp.minimum(a, b), 0.0) + jnp.minimum(jnp.maximum(a, b), 0.0)


def side(state, normal):
    density, speed_n, speed_t, speed_z, field_t, field_z = state
    normal_square = normal * normal
    field_square = normal_square + field_t * field_t + field_z * field_z
    moment = density * speed_n
    fluxes = [
        moment,
        moment * speed_n + (density + 0.5 * field_square) - normal_square,
        moment * speed_t - normal * field_t,
        moment * speed_z - normal * field_z,
        field_t * speed_n - normal * speed_t,
        field_z * speed_n - normal * speed_z,
    ]
    conserved = [density, moment, density * speed_t, density * speed_z, field_t, field_z]
    signal = jnp.abs(speed_n) + jnp.sqrt(1.0 + field_square / density)
    return fluxes, conserved, signal


def riemann(left, right, normal):
    flux_left, cons_left, signal_left = side(left, normal)
    flux_right, cons_right, signal_right = side(right, normal)
    fastest = jnp.maximum(signal_left, signal_right)
    return [
        0.5 * ((a + b) - fastest * (d - c))
        for a, b, c, d in zip(flux_left, flux_right, cons_left, cons_right)
    ]


def main_kernel(
    levels_ref,
    fields_ref,
    below_ref,
    above_ref,
    right_ref,
    left_ref,
    out_ref,
    win,
    prim,
    lefty,
    fluxy,
    gx,
    diffx,
    edge,
    turned,
    leftx,
    fluxx,
    lev,
    corner,
    tmp,
    held,
):
    level_of = near_rows(levels_ref, held)
    p32, p24, p16, p8 = lane(32), lane(24), lane(16), lane(8)
    coarse32 = (p32 >= 72) & (p32 < 120)

    inner = (p8 < 64) | ((p8 >= 80) & (p8 < 112))
    outer = ((p8 >= 64) & (p8 < 72)) | ((p8 >= 112) & (p8 < 120))
    middle = jnp.zeros((8, COLS), jnp.int32)
    offsets = (middle, jnp.where(inner, 0, jnp.where(outer, 1, -1)), jnp.where(p8 < 64, 1, -1))
    is_coarse = (p8 >= 72) & (p8 < 120)
    for kind, first in enumerate((0, 48, 80)):
        below_row, centre_row, above_row = (level_of(i, offsets[kind]) for i in range(3))
        lev[first : first + 8, :] = below_row
        lev[first + 8 : first + 16, :] = centre_row
        if kind == 1:
            lev[first + 16 : first + 24, :] = jnp.where(is_coarse, above_row, centre_row)
            lev[first + 24 : first + 32, :] = above_row
        else:
            for r in (16, 24, 32):
                lev[first + r : first + r + 8, :] = centre_row
            lev[first + 40 : first + 48, :] = above_row
    own_level = lev[8:16, :]
    below_level = lev[0:8, :]
    beside = lev[48:80, :]
    beside = jnp.maximum(beside, pltpu.roll(beside, 1, 1))
    corner[...] = jnp.maximum(beside, pltpu.roll(beside, 1, 0))

    p48 = lane(48)
    strips = jnp.where((p48 & 15) < 8, left_ref[...], right_ref[...])
    strip = ((p8 >= 64) & (p8 < 80)) | (p8 >= 112)
    strip_index = (p8 & 7) + jnp.where(outer, 8, 0)
    for f in range(7):
        below, above = last_rows(below_ref, f, below_level), above_ref[f, 0:8, :]
        win[f, PAD : PAD + 8, :] = below
        win[f, PAD + 8 : PAD + 40, :] = fields_ref[f]
        win[f, PAD + 40 : PAD + 48, :] = above
        win[f, SIDE : SIDE + 48, :] = pltpu.roll(strips, (120 - 16 * f) % 128, 1)
        index = strip_index + 16 * f
        packed = [gather_lanes(strips[r : r + 8], index) for r in (0, 8, 16, 40)]

        def joined(fine, coarse):
            return jnp.where(p8 < 72, fine, pltpu.roll(coarse, 80, 1))

        initial, second = fields_ref[f, 0:8, :], fields_ref[f, 8:16, :]
        win[f, MID : MID + 8, :] = jnp.where(strip, packed[0], joined(below, below))
        win[f, MID + 8 : MID + 16, :] = jnp.where(strip, packed[1], joined(initial, initial))
        win[f, MID + 16 : MID + 24, :] = jnp.where(
            strip, jnp.where(is_coarse, packed[3], packed[2]), joined(second, above)
        )
        win[f, MID + 24 : MID + 32, :] = jnp.where(strip, packed[3], above)

    index_up_one = jnp.where(p32 < 72, 80 + (p32 >> 1), jnp.where(p32 >= 120, 16 + (p32 >> 1), p32))
    index_up_two = (p32 >> 1, 64 + (p32 >> 1))
    index_down_two = (2 * p24) & 127
    index_down_one = (2 * (p16 - 80)) & 127

    def doubled(value, first, count, slot):
        tmp[slot, 0:32, :] = value
        part = tmp[slot, pl.ds(first, count), :]
        tmp[slot + 1, pl.ds(0, count, stride=2), :] = part
        tmp[slot + 1, pl.ds(1, count, stride=2), :] = part
        return tmp[slot + 1, 0 : 2 * count, :]

    def rows_halved(ref, first, count, by_rows):
        initial = ref[pl.ds(first, count, stride=2), :]
        if not by_rows:
            return initial
        return 0.5 * (initial + ref[pl.ds(first + 1, count, stride=2), :])

    def cols_halved(value, by_cols):
        return 0.5 * (value + pltpu.roll(value, 127, 1)) if by_cols else value

    def down_two(ref, by_rows, by_cols, slot):
        parts = [
            cols_halved(rows_halved(ref, first, 24, by_rows), by_cols) for first in (PAD, SIDE)
        ]
        parts = [gather_lanes(part, index_down_two) for part in parts]
        tmp[slot, 4:28, :] = jnp.where(p24 < 64, parts[0], parts[1])
        return tmp[slot, 0:32, :]

    def down_one(ref, by_rows, by_cols, slot):
        part = cols_halved(rows_halved(ref, MID, 16, by_rows), by_cols)
        tmp[slot, 4:20, :] = gather_lanes(part, index_down_one)
        return tmp[slot, 0:32, :]

    def share():
        level_b = lev[48:80, :]
        for f in range(7):
            by_rows, by_cols = f != 6, f != 5
            value = win[f, MID : MID + 32, :]
            injected = doubled(gather_lanes(value, index_up_one), 4, 16, 0)
            value = jnp.where((level_b == 0) & ~coarse32, injected, value)
            for k, first in enumerate((0, 80)):
                injected = doubled(gather_lanes(value, index_up_two[k]), 4, 24, 2 + 2 * k)
                held_rows = slice(PAD + first, PAD + first + 48)
                win[f, held_rows, :] = jnp.where(
                    lev[first : first + 48, :] == 2, win[f, held_rows, :], injected
                )
            halved = down_two(win.at[f], by_rows, by_cols, 6)
            value = jnp.where((level_b == 2) & ~coarse32, halved, value)
            win[f, MID : MID + 32, :] = value
            halved = down_one(win.at[f], by_rows, by_cols, 7)
            win[f, MID : MID + 32, :] = jnp.where((level_b >= 1) & coarse32, halved, value)

    def swapped(value):
        outside = jnp.where(p8 < 48, pltpu.roll(value, 48, 1), pltpu.roll(value, 80, 1))
        return jnp.where((p8 >= 48) & (p8 < 80), value, outside)

    def turn(slot, value):
        value = value.T
        turned[slot, TPAD : TPAD + 128, :] = value
        turned[slot, TPAD - 8 : TPAD, :] = swapped(value[120:128])
        turned[slot, TPAD + 128 : TPAD + 136, :] = swapped(value[0:8])

    chunks = [PAD + 16 * c for c in range(8)]

    def primitives():
        for row in chunks:
            rows = slice(row, row + 16)
            inverse = 1.0 / win[0, rows, :]
            for i in range(3):
                prim[i, rows, :] = win[1 + i, rows, :] * inverse
            prim[3, rows, :] = 0.5 * (win[6, rows, :] + win[6, row + 1 : row + 17, :])
        sources = [(win, 0), (prim, 0), (prim, 1), (prim, 2), (prim, 3), (win, 4), (win, 5)]
        for slot, (ref, i) in enumerate(sources):
            turn(slot, ref[i, PAD : PAD + 128, :])
        face_x = turned.at[6]
        prim[4, PAD : PAD + 128, :] = (
            0.5 * (face_x[TPAD : TPAD + 128, :] + face_x[TPAD + 1 : TPAD + 129, :])
        ).T

    def sweep(items, lefts, row, count, normal):
        def at(item, step):
            ref, i = item
            return ref[i, row + step : row + step + count, :]

        left, right = [], []
        for i, item in enumerate(items):
            value = at(item, 0)
            slope = 0.5 * minmod(value - at(item, -1), at(item, 1) - value)
            lefts[i, row : row + count, :] = value + slope
            if normal is not None:
                left.append(lefts[i, row - 1 : row - 1 + count, :])
                right.append(value - slope)
        if normal is None:
            return None
        return riemann(left, right, at(normal, 0))

    def sweep_x():
        items = [(turned, i) for i in range(6)]
        sweep(items, leftx, TPAD - 8, 8, None)
        for row in [TPAD + 16 * c for c in range(9)]:
            count = 8 if row == TPAD + 128 else 16
            flux = sweep(items, leftx, row, count, (turned, 6))
            for i, value in enumerate(flux):
                fluxx[i, row : row + count, :] = value
        for i, n in enumerate((0, 1, 2, 3, 5)):
            value = fluxx[n, TPAD + 1 : TPAD + 129, :] - fluxx[n, TPAD : TPAD + 128, :]
            diffx[i, PAD : PAD + 128, :] = value.T
        gx[PAD : PAD + 128, :] = fluxx[4, TPAD : TPAD + 128, :].T

    def sweep_y():
        items = [(win, 0), (prim, 1), (prim, 0), (prim, 2), (prim, 4), (win, 4)]
        for row in chunks:
            flux = sweep(items, lefty, row, 16, (win, 6))
            for i, n in enumerate((0, 2, 1, 3, 5, 4)):
                fluxy[i, row : row + 16, :] = flux[n]

    def beside_cols(ref, row, back):
        parts = [ref[r : r + 8, :] for r in row]
        parts = [pltpu.roll(part, 1 if back else 127, 1) for part in parts]
        edge_lane = p8 == (0 if back else 127)
        return [
            jnp.where(edge_lane, parts[1], parts[0]),
            jnp.where(edge_lane, parts[0], parts[1]),
        ] + parts[2:]

    row_sets = [
        (PAD + 8 * c, SIDE + 8 * c) + ((MID + 8 * c,) if c < 4 else ()) for c in range(6)
    ]

    def edges():
        for rows in row_sets:
            shifted = beside_cols(fluxy.at[5], rows, True)
            for row, other in zip(rows, shifted):
                value = (fluxy[5, row : row + 8, :] + other) - (
                    gx[row : row + 8, :] + gx[row - 1 : row + 7, :]
                )
                edge[row : row + 8, :] = 0.25 * value

    def correct():
        value = edge[MID : MID + 32, :]
        finest = corner[...]
        halved_two = down_two(edge, False, False, 6)
        halved_one = down_one(edge, False, False, 7)
        value = jnp.where((finest == 2) & ~coarse32, halved_two, value)
        edge[MID : MID + 32, :] = jnp.where((finest >= 1) & coarse32, halved_one, value)

    def update():
        for rows in row_sets:
            shifted = beside_cols(edge, rows, False)
            for k, (row, other) in enumerate(zip(rows, shifted)):
                ratio = STEP_SIZE
                if k == 2:
                    ratio = jnp.where(is_coarse, STEP_SIZE / 4, STEP_SIZE / 2)
                part = slice(row, row + 8)
                for i in range(5):
                    change = diffx[i, part, :] + (fluxy[i, row + 1 : row + 9, :] - fluxy[i, part, :])
                    win[i, part, :] = win[i, part, :] - ratio * change
                value = edge[part, :]
                diff_x = edge[row + 1 : row + 9, :] - value
                win[5, part, :] = win[5, part, :] - ratio * diff_x
                win[6, part, :] = win[6, part, :] + ratio * (other - value)

    for _ in range(2):
        share()
        primitives()
        sweep_x()
        sweep_y()
        edges()
        correct()
        update()

    zero = jnp.zeros((8, COLS), F32)
    for f in range(7):
        for c in range(4):
            value = win[f, PAD + 8 + 8 * c : PAD + 16 + 8 * c, :]
            if c < 2:
                medium = win[f, MID + 8 + 8 * c : MID + 16 + 8 * c, :]
                coarse = pltpu.roll(medium, 48, 1) if c == 0 else zero
                lower = jnp.where(own_level == 1, medium, coarse)
                value = jnp.where(own_level == 2, value, lower)
            used = p8 < jnp.where(own_level == 2, 128, jnp.where(own_level == 1, 64, 32))
            used = used & (own_level >= (0, 1, 2, 2)[c])
            blend = 0.5 * (fields_ref[f, 8 * c : 8 * c + 8, :] + value)
            out_ref[f, 8 * c : 8 * c + 8, :] = jnp.where(used, blend, 0.0)


def moved(value, axis, step):
    size = lax.axis_size(axis)
    return lax.ppermute(value, axis, [(i, (i + step) % size) for i in range(size)])


def on_device(fields, region_levels):
    shape = jax.ShapeDtypeStruct
    params = pltpu.CompilerParams(vmem_limit_bytes=32 * 1024 * 1024)
    below = moved(fields, "seg", 1)
    above = moved(fields, "seg", -1)
    packed = pl.pallas_call(
        cols_kernel,
        out_shape=shape((48, COLS), F32),
        in_specs=[VMEM] * 4,
        out_specs=VMEM,
        scratch_shapes=[pltpu.VMEM((24, COLS), jnp.int32)],
        compiler_params=params,
    )(region_levels, fields, below, above)
    right = moved(packed, "sub", -1)
    left = moved(packed, "sub", 1)

    def window(*lead):
        return pltpu.VMEM((*lead, PAD + 136, COLS), F32)

    def across(*lead):
        return pltpu.VMEM((*lead, TPAD + 144, COLS), F32)

    return pl.pallas_call(
        main_kernel,
        out_shape=shape(fields.shape, F32),
        in_specs=[VMEM] * 6,
        out_specs=VMEM,
        scratch_shapes=[
            window(7),
            window(5),
            window(6),
            window(6),
            window(),
            window(5),
            window(),
            across(7),
            across(6),
            across(6),
            pltpu.VMEM((128, COLS), jnp.int32),
            pltpu.VMEM((32, COLS), jnp.int32),
            pltpu.VMEM((8, 48, COLS), F32),
            pltpu.VMEM((24, COLS), jnp.int32),
        ],
        compiler_params=params,
    )(region_levels, fields, below, above, right, left)


def solution(mesh):
    placed = (P(None, "seg", "sub"), P())
    return jax.shard_map(
        on_device, mesh=mesh, in_specs=placed, out_specs=P(None, "seg", "sub"), check_vma=False
    )
```

time: 43.4 us -> 37.5 us (0.86)
  waiting for transfers between devices: 10.7 us -> 7.21 us
  Pallas kernels: 7.23 us -> 4.75 us
    ppermute x4, waiting for transfers between devices: 10.7 us -> 7.21 us  [moved(): lax.ppermute(value, axis, [(i, (i + step) % size) for i in range(size)])]
    pallas_call x1, Pallas kernels: 7.02 us -> 4.54 us  [on_device(): pl.pallas_call(main_kernel, out_shape=shape(fields.shape, F32), in_specs=...]
where the time goes in v2:
time: 37.5 us; the launch traced here: 37.2 us
  starting transfers between devices  23.5 us (63%)
  waiting for transfers between devices  7.21 us (19%)
  Pallas kernels  4.75 us (13%)
  local copies, waits for them, and re-layouts  1.68 us (4%)
    ppermute x4, starting transfers between devices, moved(): lax.ppermute(value, axis, [(i, (i + step) % size) for i in range(size)])  23.5 us
    ppermute x4, waiting for transfers between devices, moved(): lax.ppermute(value, axis, [(i, (i + step) % size) for i in range(size)])  7.21 us
    pallas_call x1, Pallas kernels, on_device(): pl.pallas_call(main_kernel, out_shape=shape(fields.shape, F32), in_specs=...  4.54 us
    unnamed x3, local copies, waits for them, and re-layouts  1.68 us
  transfers between devices with their start and end apart: 4, of which 2 were waited for; matrix products, arithmetic and copies ran while one was open for 2% of the time, Pallas kernels for 0%

profile of v2, /device:TPU:6, one launch (start us, length us, event | category | flops | bytes accessed | tf_op | source)
XLA Modules:
  0.0 37.2 jit_solution(4776432216500125945)
XLA Ops:
  0.0 5.1 %collective-permute-start.1 = (f32[7,32,128]{2,1,0:T(8,128)}, f32[7,32,128]{2,1,0:T(8,128)S(1)}, u32[]{:S(2)}, u32[]{:S(2)}) collective-permute-start(f32[7,32,128]{2,1,0:T(8,128)} %fields_ref.3), channel_id=1, source_target_pairs={{0,756},{12,0},{24,12},{36,24},{48,36},{60,48},{72,60},{84,72},{96... | collective-permute-start | bytes 344072 | tf_op jit(solution)/shard_map/ppermute | solution.py:365
  5.1 1.9 %collective-permute-start = (f32[7,32,128]{2,1,0:T(8,128)}, f32[7,32,128]{2,1,0:T(8,128)S(1)}, u32[]{:S(2)}, u32[]{:S(2)}) collective-permute-start(f32[7,32,128]{2,1,0:T(8,128)} %fields_ref.3), channel_id=1, source_target_pairs={{0,12},{12,24},{24,36},{36,48},{48,60},{60,72},{72,84},{84,96},{96... | collective-permute-start | bytes 344072 | tf_op jit(solution)/shard_map/ppermute | solution.py:365
  7.0 0.8 %copy.4.levels_ref = s32[64,12]{1,0:T(8,128)S(1)} copy(s32[64,12]{0,1:T(8,128)} %param.3) | data formatting | bytes 6144 | tf_op args[1]
  7.8 0.0 collective-permute-done.1.above_ref
  7.8 5.7 %collective-permute-done.below_ref = f32[7,32,128]{2,1,0:T(8,128)S(1)} collective-permute-done((f32[7,32,128]{2,1,0:T(8,128)}, f32[7,32,128]{2,1,0:T(8,128)S(1)}, u32[]{:S(2)}, u32[]{:S(2)}) %collective-permute-start) | collective-permute-done | bytes 114720 | tf_op jit(solution)/shard_map/ppermute | solution.py:365
  13.5 0.0 copy-start
  13.5 0.9 %copy-done = f32[7,32,128]{2,1,0:T(8,128)S(1)} copy-done((f32[7,32,128]{2,1,0:T(8,128)S(1)}, f32[7,32,128]{2,1,0:T(8,128)}, u32[]{:S(2)}) %copy-start) | copy-done | bytes 114712
  14.4 0.2 shard_map.28
  14.6 4.3 %collective-permute-start.3 = (f32[48,128]{1,0:T(8,128)S(1)}, f32[48,128]{1,0:T(8,128)S(1)}, u32[]{:S(2)}, u32[]{:S(2)}) collective-permute-start(f32[48,128]{1,0:T(8,128)S(1)} %shard_map.28), channel_id=1, source_target_pairs={{0,1},{1,2},{2,3},{3,4},{4,5},{5,6},{6,7},{7,8},{8,9},{9,10},{10,1... | collective-permute-start | bytes 73736 | tf_op jit(solution)/shard_map/ppermute | solution.py:365
  18.9 12.2 %collective-permute-start.2 = (f32[48,128]{1,0:T(8,128)S(1)}, f32[48,128]{1,0:T(8,128)S(1)}, u32[]{:S(2)}, u32[]{:S(2)}) collective-permute-start(f32[48,128]{1,0:T(8,128)S(1)} %shard_map.28), channel_id=1, source_target_pairs={{0,11},{1,0},{2,1},{3,2},{4,3},{5,4},{6,5},{7,6},{8,7},{9,8},{10,9... | collective-permute-start | bytes 73736 | tf_op jit(solution)/shard_map/ppermute | solution.py:365
  31.1 0.0 collective-permute-done.3.left_ref
  31.2 1.5 %collective-permute-done.2.right_ref = f32[48,128]{1,0:T(8,128)S(1)} collective-permute-done((f32[48,128]{1,0:T(8,128)S(1)}, f32[48,128]{1,0:T(8,128)S(1)}, u32[]{:S(2)}, u32[]{:S(2)}) %collective-permute-start.2) | collective-permute-done | bytes 24608 | tf_op jit(solution)/shard_map/ppermute | solution.py:365
  32.6 4.5 %shard_map.29 = f32[7,32,128]{2,1,0:T(8,128)} custom-call(s32[64,12]{1,0:T(8,128)S(1)} %copy.4.levels_ref, f32[7,32,128]{2,1,0:T(8,128)S(1)} %copy-done, f32[7,32,128]{2,1,0:T(8,128)S(1)} %collective-permute-done.below_ref, f32[7,32,128]{2,1,0:T(8,128)S(1)} %collective-permute-done.1.above_ref, f32[48,128]{1,0:T(8,128)S(1)} %collective-permute-done.2.right_ref, ...), custom_call_target="tpu_custom_call" | custom-call | tf_op jit(solution)/shard_map/pallas_call | solution.py:390
Async XLA Ops:
  0.0 7.8 %collective-permute-start.1 = (f32[7,32,128]{2,1,0:T(8,128)}, f32[7,32,128]{2,1,0:T(8,128)S(1)}, u32[]{:S(2)}, u32[]{:S(2)}) collective-permute-start(f32[7,32,128]{2,1,0:T(8,128)} %fields_ref.3), channel_id=1, source_target_pairs={{0,756},{12,0},{24,12},{36,24},{48,36},{60,48},{72,60},{84,72},{96... | collective-permute-start | bytes 344072 | tf_op jit(solution)/shard_map/ppermute | solution.py:365
  5.1 8.4 %collective-permute-start = (f32[7,32,128]{2,1,0:T(8,128)}, f32[7,32,128]{2,1,0:T(8,128)S(1)}, u32[]{:S(2)}, u32[]{:S(2)}) collective-permute-start(f32[7,32,128]{2,1,0:T(8,128)} %fields_ref.3), channel_id=1, source_target_pairs={{0,12},{12,24},{24,36},{36,48},{48,60},{60,72},{72,84},{84,96},{96... | collective-permute-start | bytes 344072 | tf_op jit(solution)/shard_map/ppermute | solution.py:365
  13.5 0.9 %copy-start = (f32[7,32,128]{2,1,0:T(8,128)S(1)}, f32[7,32,128]{2,1,0:T(8,128)}, u32[]{:S(2)}) copy-start(f32[7,32,128]{2,1,0:T(8,128)} %fields_ref.3) | copy-start | bytes 344068
  14.6 16.5 %collective-permute-start.3 = (f32[48,128]{1,0:T(8,128)S(1)}, f32[48,128]{1,0:T(8,128)S(1)}, u32[]{:S(2)}, u32[]{:S(2)}) collective-permute-start(f32[48,128]{1,0:T(8,128)S(1)} %shard_map.28), channel_id=1, source_target_pairs={{0,1},{1,2},{2,3},{3,4},{4,5},{5,6},{6,7},{7,8},{8,9},{9,10},{10,1... | collective-permute-start | bytes 73736 | tf_op jit(solution)/shard_map/ppermute | solution.py:365
  18.9 13.7 %collective-permute-start.2 = (f32[48,128]{1,0:T(8,128)S(1)}, f32[48,128]{1,0:T(8,128)S(1)}, u32[]{:S(2)}, u32[]{:S(2)}) collective-permute-start(f32[48,128]{1,0:T(8,128)S(1)} %shard_map.28), channel_id=1, source_target_pairs={{0,11},{1,0},{2,1},{3,2},{4,3},{5,4},{6,5},{7,6},{8,7},{9,8},{10,9... | collective-permute-start | bytes 73736 | tf_op jit(solution)/shard_map/ppermute | solution.py:365

commit v3 on v2

--- a/solution.py
+++ b/solution.py
@@ -47,25 +47,53 @@
     )
 
 
-def cols_kernel(levels_ref, fields_ref, below_ref, above_ref, out_ref, held):
+def packed_cols(read, level):
+    p = lane(8)
+    first = jnp.where(level == 2, 120, jnp.where(level == 1, 56, 24))
+    index = (p & 7) + jnp.where((p & 15) < 8, first, 0)
+    packed = gather_lanes(read(0), index)
+    for f in range(1, 7):
+        packed = jnp.where((p >> 4) == f, gather_lanes(read(f), index), packed)
+    return packed
+
+
+def own_kernel(levels_ref, fields_ref, lev, corner, cols_ref, held):
     level_of = near_rows(levels_ref, held)
-    p = lane(8)
-
-    def pack(read, level):
-        first = jnp.where(level == 2, 120, jnp.where(level == 1, 56, 24))
-        index = (p & 7) + jnp.where((p & 15) < 8, first, 0)
-        packed = gather_lanes(read(0), index)
-        for f in range(1, 7):
-            packed = jnp.where((p >> 4) == f, gather_lanes(read(f), index), packed)
-        return packed
-
-    none = jnp.zeros((8, COLS), jnp.int32)
-    level = level_of(0, none)
-    out_ref[0:8, :] = pack(lambda f: last_rows(below_ref, f, level), level)
-    own = level_of(1, none)
+    p8 = lane(8)
+    inner = (p8 < 64) | ((p8 >= 80) & (p8 < 112))
+    outer = ((p8 >= 64) & (p8 < 72)) | ((p8 >= 112) & (p8 < 120))
+    middle = jnp.zeros((8, COLS), jnp.int32)
+    offsets = (middle, jnp.where(inner, 0, jnp.where(outer, 1, -1)), jnp.where(p8 < 64, 1, -1))
+    is_coarse = (p8 >= 72) & (p8 < 120)
+    for kind, first in enumerate((0, 48, 80)):
+        below_row, centre_row, above_row = (level_of(i, offsets[kind]) for i in range(3))
+        lev[first : first + 8, :] = below_row
+        lev[first + 8 : first + 16, :] = centre_row
+        if kind == 1:
+            lev[first + 16 : first + 24, :] = jnp.where(is_coarse, above_row, centre_row)
+            lev[first + 24 : first + 32, :] = above_row
+        else:
+            for r in (16, 24, 32):
+                lev[first + r : first + r + 8, :] = centre_row
+            lev[first + 40 : first + 48, :] = above_row
+    beside = lev[48:80, :]
+    beside = jnp.maximum(beside, pltpu.roll(beside, 1, 1))
+    corner[...] = jnp.maximum(beside, pltpu.roll(beside, 1, 0))
+    own = lev[8:16, :]
     for r in range(0, 32, 8):
-        out_ref[8 + r : 16 + r, :] = pack(lambda f: fields_ref[f, r : r + 8, :], own)
-    out_ref[40:48, :] = pack(lambda f: above_ref[f, 0:8, :], level_of(2, none))
+        cols_ref[r : r + 8, :] = packed_cols(lambda f: fields_ref[f, r : r + 8, :], own)
+
+
+def cols_kernel(lev, cols_ref, far_ref, close_ref, out_ref, below_ref, above_ref):
+    even = jnp.full((8, COLS), lax.rem(lax.axis_index("seg"), 2)) == 0
+    below_level, above_level = lev[0:8, :], lev[40:48, :]
+    for f in range(7):
+        far, close = (last_rows(ref, f, below_level) for ref in (far_ref, close_ref))
+        below_ref[f] = jnp.where(even, far, close)
+        above_ref[f] = jnp.where(even, close_ref[f, 0:8, :], far_ref[f, 0:8, :])
+    out_ref[0:8, :] = packed_cols(lambda f: below_ref[f], below_level)
+    out_ref[8:40, :] = cols_ref[...]
+    out_ref[40:48, :] = packed_cols(lambda f: above_ref[f], above_level)
 
 
 def minmod(a, b):
@@ -101,7 +129,8 @@
 
 
 def main_kernel(
-    levels_ref,
+    lev,
+    corner,
     fields_ref,
     below_ref,
     above_ref,
@@ -118,43 +147,21 @@
     turned,
     leftx,
     fluxx,
-    lev,
-    corner,
     tmp,
-    held,
 ):
-    level_of = near_rows(levels_ref, held)
     p32, p24, p16, p8 = lane(32), lane(24), lane(16), lane(8)
     coarse32 = (p32 >= 72) & (p32 < 120)
 
-    inner = (p8 < 64) | ((p8 >= 80) & (p8 < 112))
+    is_coarse = (p8 >= 72) & (p8 < 120)
     outer = ((p8 >= 64) & (p8 < 72)) | ((p8 >= 112) & (p8 < 120))
-    middle = jnp.zeros((8, COLS), jnp.int32)
-    offsets = (middle, jnp.where(inner, 0, jnp.where(outer, 1, -1)), jnp.where(p8 < 64, 1, -1))
-    is_coarse = (p8 >= 72) & (p8 < 120)
-    for kind, first in enumerate((0, 48, 80)):
-        below_row, centre_row, above_row = (level_of(i, offsets[kind]) for i in range(3))
-        lev[first : first + 8, :] = below_row
-        lev[first + 8 : first + 16, :] = centre_row
-        if kind == 1:
-            lev[first + 16 : first + 24, :] = jnp.where(is_coarse, above_row, centre_row)
-            lev[first + 24 : first + 32, :] = above_row
-        else:
-            for r in (16, 24, 32):
-                lev[first + r : first + r + 8, :] = centre_row
-            lev[first + 40 : first + 48, :] = above_row
     own_level = lev[8:16, :]
-    below_level = lev[0:8, :]
-    beside = lev[48:80, :]
-    beside = jnp.maximum(beside, pltpu.roll(beside, 1, 1))
-    corner[...] = jnp.maximum(beside, pltpu.roll(beside, 1, 0))
 
     p48 = lane(48)
     strips = jnp.where((p48 & 15) < 8, left_ref[...], right_ref[...])
     strip = ((p8 >= 64) & (p8 < 80)) | (p8 >= 112)
     strip_index = (p8 & 7) + jnp.where(outer, 8, 0)
     for f in range(7):
-        below, above = last_rows(below_ref, f, below_level), above_ref[f, 0:8, :]
+        below, above = below_ref[f], above_ref[f]
         win[f, PAD : PAD + 8, :] = below
         win[f, PAD + 8 : PAD + 40, :] = fields_ref[f]
         win[f, PAD + 40 : PAD + 48, :] = above
@@ -365,19 +372,37 @@
     return lax.ppermute(value, axis, [(i, (i + step) % size) for i in range(size)])
 
 
+def swapped_pairs(value, axis, first):
+    size = lax.axis_size(axis)
+    pairs = [(i, (i + 1) % size) for i in range(first, size, 2)]
+    return lax.ppermute(value, axis, pairs + [(j, i) for i, j in pairs])
+
+
 def on_device(fields, region_levels):
     shape = jax.ShapeDtypeStruct
     params = pltpu.CompilerParams(vmem_limit_bytes=32 * 1024 * 1024)
-    below = moved(fields, "seg", 1)
-    above = moved(fields, "seg", -1)
-    packed = pl.pallas_call(
-        cols_kernel,
-        out_shape=shape((48, COLS), F32),
-        in_specs=[VMEM] * 4,
-        out_specs=VMEM,
+    far = swapped_pairs(fields, "seg", 1)
+    close = swapped_pairs(fields, "seg", 0)
+    lev, corner, cols = pl.pallas_call(
+        own_kernel,
+        out_shape=(
+            shape((128, COLS), jnp.int32),
+            shape((32, COLS), jnp.int32),
+            shape((32, COLS), F32),
+        ),
+        in_specs=[VMEM] * 2,
+        out_specs=(VMEM,) * 3,
         scratch_shapes=[pltpu.VMEM((24, COLS), jnp.int32)],
         compiler_params=params,
-    )(region_levels, fields, below, above)
+    )(region_levels, fields)
+    rows = shape((7, 8, COLS), F32)
+    packed, below, above = pl.pallas_call(
+        cols_kernel,
+        out_shape=(shape((48, COLS), F32), rows, rows),
+        in_specs=[VMEM] * 4,
+        out_specs=(VMEM,) * 3,
+        compiler_params=params,
+    )(lev, cols, far, close)
     right = moved(packed, "sub", -1)
     left = moved(packed, "sub", 1)
 
@@ -390,7 +415,7 @@
     return pl.pallas_call(
         main_kernel,
         out_shape=shape(fields.shape, F32),
-        in_specs=[VMEM] * 6,
+        in_specs=[VMEM] * 7,
         out_specs=VMEM,
         scratch_shapes=[
             window(7),
@@ -403,13 +428,10 @@
             across(7),
             across(6),
             across(6),
-            pltpu.VMEM((128, COLS), jnp.int32),
-            pltpu.VMEM((32, COLS), jnp.int32),
             pltpu.VMEM((8, 48, COLS), F32),
-            pltpu.VMEM((24, COLS), jnp.int32),
         ],
         compiler_params=params,
-    )(region_levels, fields, below, above, right, left)
+    )(lev, corner, fields, below, above, right, left)
 
 
 def solution(mesh):

time: 37.5 us -> 34.5 us (0.920)
  the two profiles are of different devices: /device:TPU:6 before, /device:TPU:1 now
where the time goes in v3:
time: 34.5 us; the launch traced here: 34.2 us
  starting transfers between devices  26.6 us (77%)
  Pallas kernels  4.87 us (14%)
  local copies, waits for them, and re-layouts  1.69 us (5%)
  waiting for transfers between devices  0.92 us (3%)
    ppermute x2, starting transfers between devices, swapped_pairs(): return lax.ppermute(value, axis, pairs + [(j, i) for i, j in pairs])  14.3 us
    ppermute x2, starting transfers between devices, moved(): lax.ppermute(value, axis, [(i, (i + step) % size) for i in range(size)])  12.3 us
    pallas_call x1, Pallas kernels, on_device(): pl.pallas_call(main_kernel, out_shape=shape(fields.shape, F32), in_specs=...  4.6 us
    unnamed x5, local copies, waits for them, and re-layouts  1.69 us
    ppermute x2, waiting for transfers between devices, moved(): lax.ppermute(value, axis, [(i, (i + step) % size) for i in range(size)])  0.92 us
  transfers between devices with their start and end apart: 4, of which 1 were waited for; matrix products, arithmetic and copies ran while one was open for 2% of the time, Pallas kernels for 1%

profile of v3, /device:TPU:1, one launch (start us, length us, event | category | flops | bytes accessed | tf_op | source)
XLA Modules:
  0.0 34.2 jit_solution(9986942881678855036)
XLA Ops:
  0.0 4.6 %collective-permute-start = (f32[7,32,128]{2,1,0:T(8,128)}, f32[7,32,128]{2,1,0:T(8,128)S(1)}, u32[]{:S(2)}, u32[]{:S(2)}) collective-permute-start(f32[7,32,128]{2,1,0:T(8,128)} %fields_ref.3), channel_id=1, source_target_pairs={{12,24},{36,48},{60,72},{84,96},{108,120},{132,144},{156,168},{180... | collective-permute-start | bytes 344072 | tf_op jit(solution)/shard_map/ppermute | solution.py:378
  4.6 9.8 %collective-permute-start.1 = (f32[7,32,128]{2,1,0:T(8,128)}, f32[7,32,128]{2,1,0:T(8,128)S(1)}, u32[]{:S(2)}, u32[]{:S(2)}) collective-permute-start(f32[7,32,128]{2,1,0:T(8,128)} %fields_ref.3), channel_id=1, source_target_pairs={{0,12},{24,36},{48,60},{72,84},{96,108},{120,132},{144,156},{168,1... | collective-permute-start | bytes 344072 | tf_op jit(solution)/shard_map/ppermute | solution.py:378
  14.4 0.8 %copy.3.levels_ref = s32[64,12]{1,0:T(8,128)S(1)} copy(s32[64,12]{0,1:T(8,128)} %param.3) | data formatting | bytes 6144 | tf_op args[1]
  15.1 0.0 copy-start
  15.1 0.9 %copy-done = f32[7,32,128]{2,1,0:T(8,128)S(1)} copy-done((f32[7,32,128]{2,1,0:T(8,128)S(1)}, f32[7,32,128]{2,1,0:T(8,128)}, u32[]{:S(2)}) %copy-start) | copy-done | bytes 114712
  16.0 0.2 shard_map.28
  16.2 0.0 collective-permute-done.far_ref
  16.2 0.0 collective-permute-done.1.close_ref
  16.3 0.0 copy-start.1
  16.3 0.1 shard_map.29
  16.4 1.9 %collective-permute-start.3 = (f32[48,128]{1,0:T(8,128)S(1)}, f32[48,128]{1,0:T(8,128)S(1)}, u32[]{:S(2)}, u32[]{:S(2)}) collective-permute-start(f32[48,128]{1,0:T(8,128)S(1)} %get-tuple-element.16), channel_id=1, source_target_pairs={{0,1},{1,2},{2,3},{3,4},{4,5},{5,6},{6,7},{7,8},{8,9},{9,10},{10,1... | collective-permute-start | bytes 73736 | tf_op jit(solution)/shard_map/ppermute | solution.py:372
  18.3 10.4 %collective-permute-start.2 = (f32[48,128]{1,0:T(8,128)S(1)}, f32[48,128]{1,0:T(8,128)S(1)}, u32[]{:S(2)}, u32[]{:S(2)}) collective-permute-start(f32[48,128]{1,0:T(8,128)S(1)} %get-tuple-element.16), channel_id=1, source_target_pairs={{0,11},{1,0},{2,1},{3,2},{4,3},{5,4},{6,5},{7,6},{8,7},{9,8},{10,9... | collective-permute-start | bytes 73736 | tf_op jit(solution)/shard_map/ppermute | solution.py:372
  28.7 0.0 collective-permute-done.3.left_ref
  28.7 0.9 %collective-permute-done.2.right_ref = f32[48,128]{1,0:T(8,128)S(1)} collective-permute-done((f32[48,128]{1,0:T(8,128)S(1)}, f32[48,128]{1,0:T(8,128)S(1)}, u32[]{:S(2)}, u32[]{:S(2)}) %collective-permute-start.2) | collective-permute-done | bytes 24608 | tf_op jit(solution)/shard_map/ppermute | solution.py:372
  29.6 0.0 copy-done.1
  29.6 4.6 %shard_map.30 = f32[7,32,128]{2,1,0:T(8,128)} custom-call(s32[128,128]{1,0:T(8,128)S(1)} %get-tuple-element.11.lev, s32[32,128]{1,0:T(8,128)S(1)} %get-tuple-element.12.corner, f32[7,32,128]{2,1,0:T(8,128)S(1)} %copy-done.1, f32[7,8,128]{2,1,0:T(8,128)S(1)} %get-tuple-element.14.below_ref, f32[7,8,128]{2,1,0:T(8,128)S(1)} %get-tuple-element.15.above_ref, ...), custom_call_target="tpu_custom_call" | custom-call | tf_op jit(solution)/shard_map/pallas_call | solution.py:415
Async XLA Ops:
  0.0 16.2 %collective-permute-start = (f32[7,32,128]{2,1,0:T(8,128)}, f32[7,32,128]{2,1,0:T(8,128)S(1)}, u32[]{:S(2)}, u32[]{:S(2)}) collective-permute-start(f32[7,32,128]{2,1,0:T(8,128)} %fields_ref.3), channel_id=1, source_target_pairs={{12,24},{36,48},{60,72},{84,96},{108,120},{132,144},{156,168},{180... | collective-permute-start | bytes 344072 | tf_op jit(solution)/shard_map/ppermute | solution.py:378
  4.6 11.7 %collective-permute-start.1 = (f32[7,32,128]{2,1,0:T(8,128)}, f32[7,32,128]{2,1,0:T(8,128)S(1)}, u32[]{:S(2)}, u32[]{:S(2)}) collective-permute-start(f32[7,32,128]{2,1,0:T(8,128)} %fields_ref.3), channel_id=1, source_target_pairs={{0,12},{24,36},{48,60},{72,84},{96,108},{120,132},{144,156},{168,1... | collective-permute-start | bytes 344072 | tf_op jit(solution)/shard_map/ppermute | solution.py:378
  15.1 0.9 %copy-start = (f32[7,32,128]{2,1,0:T(8,128)S(1)}, f32[7,32,128]{2,1,0:T(8,128)}, u32[]{:S(2)}) copy-start(f32[7,32,128]{2,1,0:T(8,128)} %fields_ref.3) | copy-start | bytes 344068
  16.3 13.3 %copy-start.1 = (f32[7,32,128]{2,1,0:T(8,128)S(1)}, f32[7,32,128]{2,1,0:T(8,128)}, u32[]{:S(2)}) copy-start(f32[7,32,128]{2,1,0:T(8,128)} %fields_ref.3) | copy-start | bytes 344068
  16.4 12.3 %collective-permute-start.3 = (f32[48,128]{1,0:T(8,128)S(1)}, f32[48,128]{1,0:T(8,128)S(1)}, u32[]{:S(2)}, u32[]{:S(2)}) collective-permute-start(f32[48,128]{1,0:T(8,128)S(1)} %get-tuple-element.16), channel_id=1, source_target_pairs={{0,1},{1,2},{2,3},{3,4},{4,5},{5,6},{6,7},{7,8},{8,9},{9,10},{10,1... | collective-permute-start | bytes 73736 | tf_op jit(solution)/shard_map/ppermute | solution.py:372
  18.3 11.3 %collective-permute-start.2 = (f32[48,128]{1,0:T(8,128)S(1)}, f32[48,128]{1,0:T(8,128)S(1)}, u32[]{:S(2)}, u32[]{:S(2)}) collective-permute-start(f32[48,128]{1,0:T(8,128)S(1)} %get-tuple-element.16), channel_id=1, source_target_pairs={{0,11},{1,0},{2,1},{3,2},{4,3},{5,4},{6,5},{7,6},{8,7},{9,8},{10,9... | collective-permute-start | bytes 73736 | tf_op jit(solution)/shard_map/ppermute | solution.py:372

commit v4 on v3

--- a/solution.py
+++ b/solution.py
@@ -11,6 +11,7 @@
 ROWS, COLS = 32, 128
 F32 = jnp.float32
 VMEM = pl.BlockSpec(memory_space=pltpu.VMEM)
+HBM = pl.BlockSpec(memory_space=pltpu.HBM)
 
 PAD = 8
 TPAD = 16
@@ -26,17 +27,20 @@
 
 
 def near_rows(levels_ref, held_ref):
-    seg_count, sub_count = levels_ref.shape
-    sub = lax.axis_index("sub")
+    sub_count, seg_count = levels_ref.shape
+    for j in range(3):
+        u = lax.rem(lax.axis_index("sub") + (j - 1 + sub_count), sub_count)
+        held_ref[8 * j : 8 * j + 1, 0:seg_count] = levels_ref[pl.ds(u, 1), :]
+    table = []
     for i in range(3):
         s = lax.rem(lax.axis_index("seg") + (i - 1 + seg_count), seg_count)
-        held_ref[8 * i : 8 * i + 1, 0:sub_count] = levels_ref[pl.ds(s, 1), :]
+        s = jnp.full((8, COLS), s, jnp.int32)
+        rows = [jnp.broadcast_to(held_ref[8 * j : 8 * j + 1, :], (8, COLS)) for j in range(3)]
+        table.append([gather_lanes(row, s) for row in rows])
 
     def level_of(i, offset):
-        row = jnp.broadcast_to(held_ref[8 * i : 8 * i + 1, :], (8, COLS))
-        u = sub + offset
-        u = jnp.where(u < 0, u + sub_count, jnp.where(u >= sub_count, u - sub_count, u))
-        return gather_lanes(row, u)
+        first, middle, last = table[i]
+        return jnp.where(offset < 0, first, jnp.where(offset > 0, last, middle))
 
     return level_of
 
@@ -57,7 +61,14 @@
     return packed
 
 
-def own_kernel(levels_ref, fields_ref, lev, corner, cols_ref, held):
+def own_kernel(levels_hbm, fields_hbm, lev, lev_strips, corner, cols_ref, levels_ref, fields_ref, held, sems):
+    copies = [
+        pltpu.make_async_copy(levels_hbm, levels_ref, sems.at[0]),
+        pltpu.make_async_copy(fields_hbm, fields_ref, sems.at[1]),
+    ]
+    for copy in copies:
+        copy.start()
+    copies[0].wait()
     level_of = near_rows(levels_ref, held)
     p8 = lane(8)
     inner = (p8 < 64) | ((p8 >= 80) & (p8 < 112))
@@ -76,15 +87,22 @@
             for r in (16, 24, 32):
                 lev[first + r : first + r + 8, :] = centre_row
             lev[first + 40 : first + 48, :] = above_row
+    offset = jnp.where((p8 & 15) < 8, -1, 1)
+    below_row, centre_row, above_row = (level_of(i, offset) for i in range(3))
+    for first, count in ((0, 6), (48, 4), (80, 3)):
+        for r in range(count):
+            row = below_row if r == 0 else above_row if r == count - 1 else centre_row
+            lev_strips[first + 8 * r : first + 8 * r + 8, :] = row
     beside = lev[48:80, :]
     beside = jnp.maximum(beside, pltpu.roll(beside, 1, 1))
     corner[...] = jnp.maximum(beside, pltpu.roll(beside, 1, 0))
     own = lev[8:16, :]
+    copies[1].wait()
     for r in range(0, 32, 8):
         cols_ref[r : r + 8, :] = packed_cols(lambda f: fields_ref[f, r : r + 8, :], own)
 
 
-def cols_kernel(lev, cols_ref, far_ref, close_ref, out_ref, below_ref, above_ref):
+def cols_kernel(lev, cols_ref, close_ref, far_ref, out_ref, below_ref, above_ref):
     even = jnp.full((8, COLS), lax.rem(lax.axis_index("seg"), 2)) == 0
     below_level, above_level = lev[0:8, :], lev[40:48, :]
     for f in range(7):
@@ -128,12 +146,121 @@
     ]
 
 
+def doubled(part, tmp):
+    count = part.shape[0]
+    tmp[pl.ds(0, count, stride=2), :] = part
+    tmp[pl.ds(1, count, stride=2), :] = part
+    return tmp[0 : 2 * count, :]
+
+
+def rows_halved(ref, first, count, by_rows):
+    initial = ref[pl.ds(first, count, stride=2), :]
+    if not by_rows:
+        return initial
+    return 0.5 * (initial + ref[pl.ds(first + 1, count, stride=2), :])
+
+
+def cols_halved(value, by_cols):
+    return 0.5 * (value + pltpu.roll(value, 127, 1)) if by_cols else value
+
+
+def down_two(ref, firsts, by_rows, by_cols, tmp):
+    p = lane(24)
+    parts = [cols_halved(rows_halved(ref, first, 24, by_rows), by_cols) for first in firsts]
+    parts = [gather_lanes(part, (2 * p) & 127) for part in parts]
+    tmp[4:28, :] = parts[0] if len(parts) == 1 else jnp.where(p < 64, parts[0], parts[1])
+    return tmp[0:32, :]
+
+
+def down_one(ref, first, by_rows, by_cols, tmp):
+    part = cols_halved(rows_halved(ref, first, 16, by_rows), by_cols)
+    tmp[4:20, :] = gather_lanes(part, (2 * (lane(16) - 80)) & 127)
+    return tmp[0:32, :]
+
+
+def share_levels(win, lev, tmp, base, blocks):
+    p32, p24, p16 = lane(32), lane(24), lane(16)
+    coarse32 = (p32 >= 72) & (p32 < 120)
+    mid = base + 48
+    level_b = lev[48:80, :]
+    up_one = jnp.where(p16 < 72, 80 + (p16 >> 1), jnp.where(p16 >= 120, 16 + (p16 >> 1), p16))
+    up_two = (p24 >> 1, 64 + (p24 >> 1))
+    for f in range(7):
+        by_rows, by_cols = f != 6, f != 5
+        slots = [tmp.at[8 * f + k] for k in range(5)]
+        injected = doubled(gather_lanes(win[f, mid + 4 : mid + 20, :], up_one), slots[0])
+        value = jnp.where((level_b == 0) & ~coarse32, injected, win[f, mid : mid + 32, :])
+        win[f, mid : mid + 32, :] = value
+        part = win[f, mid + 4 : mid + 28, :]
+        for k, first in enumerate(blocks):
+            injected = doubled(gather_lanes(part, up_two[k]), slots[1 + k])
+            rows = slice(base + first, base + first + 48)
+            win[f, rows, :] = jnp.where(lev[first : first + 48, :] == 2, win[f, rows, :], injected)
+        firsts = [base + first for first in blocks]
+        halved = down_two(win.at[f], firsts, by_rows, by_cols, slots[3])
+        value = jnp.where((level_b == 2) & ~coarse32, halved, value)
+        win[f, mid : mid + 32, :] = value
+        halved = down_one(win.at[f], mid, by_rows, by_cols, slots[4])
+        win[f, mid : mid + 32, :] = jnp.where((level_b >= 1) & coarse32, halved, value)
+
+
+def rows_kernel(lev, fields_ref, below_ref, above_ref, win, tmp):
+    p8 = lane(8)
+    is_coarse = (p8 >= 72) & (p8 < 120)
+
+    def joined(fine, coarse):
+        return jnp.where(is_coarse, pltpu.roll(coarse, 80, 1), fine)
+
+    for f in range(7):
+        below, above = below_ref[f], above_ref[f]
+        initial, second = fields_ref[f, 0:8, :], fields_ref[f, 8:16, :]
+        win[f, 0:8, :] = below
+        win[f, 8:40, :] = fields_ref[f]
+        win[f, 40:48, :] = above
+        win[f, 48:56, :] = joined(below, below)
+        win[f, 56:64, :] = joined(initial, initial)
+        win[f, 64:72, :] = joined(second, above)
+        win[f, 72:80, :] = above
+    share_levels(win, lev, tmp, 0, (0,))
+
+
+def share_strips(strips, lev_strips, held, tmp):
+    p = lane(24)
+    k = p & 15
+    up = (p - k) + jnp.where(k < 8, 4 + (k >> 1), 8 + ((k - 8) >> 1))
+    down = (p - k) + ((2 * k - 8) & 15)
+    held[0:48, :] = strips
+    held[48:72, :] = strips[0:24]
+    held[72:80, :] = strips[40:48]
+    held[80:96, :] = strips[0:16]
+    held[96:104, :] = strips[40:48]
+    level_one = lev_strips[48:80, :]
+
+    def halved(first, count):
+        initial = held[pl.ds(first, count, stride=2), :]
+        mean = 0.5 * (initial + held[pl.ds(first + 1, count, stride=2), :])
+        f = lane(count) >> 4
+        value = jnp.where(f == 6, initial, mean)
+        value = jnp.where(f == 5, value, 0.5 * (value + pltpu.roll(value, 127, 1)))
+        return gather_lanes(value, down[0:count])
+
+    injected = doubled(gather_lanes(held[84:100, :], up[0:16]), tmp.at[0])
+    value = jnp.where(level_one == 0, injected, held[48:80, :])
+    held[48:80, :] = value
+    injected = doubled(gather_lanes(held[52:76, :], up), tmp.at[1])
+    held[0:48, :] = jnp.where(lev_strips[0:48, :] == 2, held[0:48, :], injected)
+    tmp[2, 4:28, :] = halved(0, 24)
+    held[48:80, :] = jnp.where(level_one == 2, tmp[2, 0:32, :], value)
+    tmp[3, 4:20, :] = halved(48, 16)
+    held[80:104, :] = jnp.where(lev_strips[80:104, :] >= 1, tmp[3, 0:24, :], held[80:104, :])
+
+
 def main_kernel(
     lev,
+    lev_strips,
     corner,
     fields_ref,
-    below_ref,
-    above_ref,
+    own_ref,
     right_ref,
     left_ref,
     out_ref,
@@ -147,91 +274,31 @@
     turned,
     leftx,
     fluxx,
+    held,
     tmp,
 ):
-    p32, p24, p16, p8 = lane(32), lane(24), lane(16), lane(8)
+    p32, p8 = lane(32), lane(8)
     coarse32 = (p32 >= 72) & (p32 < 120)
-
     is_coarse = (p8 >= 72) & (p8 < 120)
-    outer = ((p8 >= 64) & (p8 < 72)) | ((p8 >= 112) & (p8 < 120))
     own_level = lev[8:16, :]
 
     p48 = lane(48)
     strips = jnp.where((p48 & 15) < 8, left_ref[...], right_ref[...])
-    strip = ((p8 >= 64) & (p8 < 80)) | (p8 >= 112)
-    strip_index = (p8 & 7) + jnp.where(outer, 8, 0)
+    share_strips(strips, lev_strips, held, tmp)
+    strip_one = ((p32 >= 64) & (p32 < 72)) | (p32 >= 120)
+    strip_none = ((p32 >= 72) & (p32 < 80)) | ((p32 >= 112) & (p32 < 120))
+    right_side = ((p32 >= 64) & (p32 < 72)) | ((p32 >= 112) & (p32 < 120))
+    strip_index = (p32 & 7) + jnp.where(right_side, 8, 0)
     for f in range(7):
-        below, above = below_ref[f], above_ref[f]
-        win[f, PAD : PAD + 8, :] = below
-        win[f, PAD + 8 : PAD + 40, :] = fields_ref[f]
-        win[f, PAD + 40 : PAD + 48, :] = above
-        win[f, SIDE : SIDE + 48, :] = pltpu.roll(strips, (120 - 16 * f) % 128, 1)
         index = strip_index + 16 * f
-        packed = [gather_lanes(strips[r : r + 8], index) for r in (0, 8, 16, 40)]
-
-        def joined(fine, coarse):
-            return jnp.where(p8 < 72, fine, pltpu.roll(coarse, 80, 1))
-
-        initial, second = fields_ref[f, 0:8, :], fields_ref[f, 8:16, :]
-        win[f, MID : MID + 8, :] = jnp.where(strip, packed[0], joined(below, below))
-        win[f, MID + 8 : MID + 16, :] = jnp.where(strip, packed[1], joined(initial, initial))
-        win[f, MID + 16 : MID + 24, :] = jnp.where(
-            strip, jnp.where(is_coarse, packed[3], packed[2]), joined(second, above)
+        win[f, PAD : PAD + 48, :] = own_ref[f, 0:48, :]
+        win[f, SIDE : SIDE + 48, :] = pltpu.roll(held[0:48, :], (120 - 16 * f) % 128, 1)
+        fine = gather_lanes(held[48:80, :], index)
+        win[f, MID : MID + 32, :] = jnp.where(strip_one, fine, own_ref[f, 48:80, :])
+        coarse = gather_lanes(held[80:104, :], index[0:24])
+        win[f, MID : MID + 24, :] = jnp.where(
+            strip_none[0:24], coarse, win[f, MID : MID + 24, :]
         )
-        win[f, MID + 24 : MID + 32, :] = jnp.where(strip, packed[3], above)
-
-    index_up_one = jnp.where(p32 < 72, 80 + (p32 >> 1), jnp.where(p32 >= 120, 16 + (p32 >> 1), p32))
-    index_up_two = (p32 >> 1, 64 + (p32 >> 1))
-    index_down_two = (2 * p24) & 127
-    index_down_one = (2 * (p16 - 80)) & 127
-
-    def doubled(value, first, count, slot):
-        tmp[slot, 0:32, :] = value
-        part = tmp[slot, pl.ds(first, count), :]
-        tmp[slot + 1, pl.ds(0, count, stride=2), :] = part
-        tmp[slot + 1, pl.ds(1, count, stride=2), :] = part
-        return tmp[slot + 1, 0 : 2 * count, :]
-
-    def rows_halved(ref, first, count, by_rows):
-        initial = ref[pl.ds(first, count, stride=2), :]
-        if not by_rows:
-            return initial
-        return 0.5 * (initial + ref[pl.ds(first + 1, count, stride=2), :])
-
-    def cols_halved(value, by_cols):
-        return 0.5 * (value + pltpu.roll(value, 127, 1)) if by_cols else value
-
-    def down_two(ref, by_rows, by_cols, slot):
-        parts = [
-            cols_halved(rows_halved(ref, first, 24, by_rows), by_cols) for first in (PAD, SIDE)
-        ]
-        parts = [gather_lanes(part, index_down_two) for part in parts]
-        tmp[slot, 4:28, :] = jnp.where(p24 < 64, parts[0], parts[1])
-        return tmp[slot, 0:32, :]
-
-    def down_one(ref, by_rows, by_cols, slot):
-        part = cols_halved(rows_halved(ref, MID, 16, by_rows), by_cols)
-        tmp[slot, 4:20, :] = gather_lanes(part, index_down_one)
-        return tmp[slot, 0:32, :]
-
-    def share():
-        level_b = lev[48:80, :]
-        for f in range(7):
-            by_rows, by_cols = f != 6, f != 5
-            value = win[f, MID : MID + 32, :]
-            injected = doubled(gather_lanes(value, index_up_one), 4, 16, 0)
-            value = jnp.where((level_b == 0) & ~coarse32, injected, value)
-            for k, first in enumerate((0, 80)):
-                injected = doubled(gather_lanes(value, index_up_two[k]), 4, 24, 2 + 2 * k)
-                held_rows = slice(PAD + first, PAD + first + 48)
-                win[f, held_rows, :] = jnp.where(
-                    lev[first : first + 48, :] == 2, win[f, held_rows, :], injected
-                )
-            halved = down_two(win.at[f], by_rows, by_cols, 6)
-            value = jnp.where((level_b == 2) & ~coarse32, halved, value)
-            win[f, MID : MID + 32, :] = value
-            halved = down_one(win.at[f], by_rows, by_cols, 7)
-            win[f, MID : MID + 32, :] = jnp.where((level_b >= 1) & coarse32, halved, value)
 
     def swapped(value):
         outside = jnp.where(p8 < 48, pltpu.roll(value, 48, 1), pltpu.roll(value, 80, 1))
@@ -322,8 +389,8 @@
     def correct():
         value = edge[MID : MID + 32, :]
         finest = corner[...]
-        halved_two = down_two(edge, False, False, 6)
-        halved_one = down_one(edge, False, False, 7)
+        halved_two = down_two(edge, (PAD, SIDE), False, False, tmp.at[0])
+        halved_one = down_one(edge, MID, False, False, tmp.at[1])
         value = jnp.where((finest == 2) & ~coarse32, halved_two, value)
         edge[MID : MID + 32, :] = jnp.where((finest >= 1) & coarse32, halved_one, value)
 
@@ -343,8 +410,9 @@
                 win[5, part, :] = win[5, part, :] - ratio * diff_x
                 win[6, part, :] = win[6, part, :] + ratio * (other - value)
 
-    for _ in range(2):
-        share()
+    for section in range(2):
+        if section == 1:
+            share_levels(win, lev, tmp, PAD, (0, 80))
         primitives()
         sweep_x()
         sweep_y()
@@ -383,18 +451,24 @@
     params = pltpu.CompilerParams(vmem_limit_bytes=32 * 1024 * 1024)
     far = swapped_pairs(fields, "seg", 1)
     close = swapped_pairs(fields, "seg", 0)
-    lev, corner, cols = pl.pallas_call(
+    lev, lev_strips, corner, cols = pl.pallas_call(
         own_kernel,
         out_shape=(
             shape((128, COLS), jnp.int32),
+            shape((104, COLS), jnp.int32),
             shape((32, COLS), jnp.int32),
             shape((32, COLS), F32),
         ),
-        in_specs=[VMEM] * 2,
-        out_specs=(VMEM,) * 3,
-        scratch_shapes=[pltpu.VMEM((24, COLS), jnp.int32)],
+        in_specs=[HBM] * 2,
+        out_specs=(VMEM,) * 4,
+        scratch_shapes=[
+            pltpu.VMEM(region_levels.shape[::-1], jnp.int32),
+            pltpu.VMEM(fields.shape, F32),
+            pltpu.VMEM((24, COLS), jnp.int32),
+            pltpu.SemaphoreType.DMA((2,)),
+        ],
         compiler_params=params,
-    )(region_levels, fields)
+    )(*(pltpu.with_memory_space_constraint(x, pltpu.HBM) for x in (region_levels.T, fields)))
     rows = shape((7, 8, COLS), F32)
     packed, below, above = pl.pallas_call(
         cols_kernel,
@@ -402,9 +476,17 @@
         in_specs=[VMEM] * 4,
         out_specs=(VMEM,) * 3,
         compiler_params=params,
-    )(lev, cols, far, close)
+    )(lev, cols, close, far)
     right = moved(packed, "sub", -1)
     left = moved(packed, "sub", 1)
+    own = pl.pallas_call(
+        rows_kernel,
+        out_shape=shape((7, 128, COLS), F32),
+        in_specs=[VMEM] * 4,
+        out_specs=VMEM,
+        scratch_shapes=[pltpu.VMEM((56, 48, COLS), F32)],
+        compiler_params=params,
+    )(lev, fields, below, above)
 
     def window(*lead):
         return pltpu.VMEM((*lead, PAD + 136, COLS), F32)
@@ -428,10 +510,11 @@
             across(7),
             across(6),
             across(6),
-            pltpu.VMEM((8, 48, COLS), F32),
+            pltpu.VMEM((104, COLS), F32),
+            pltpu.VMEM((56, 48, COLS), F32),
         ],
         compiler_params=params,
-    )(lev, corner, fields, below, above, right, left)
+    )(lev, lev_strips, corner, fields, own, right, left)
 
 
 def solution(mesh):

time: 34.5 us -> 33.4 us (0.968)
  local copies, waits for them, and re-layouts: 1.69 us -> 0.01 us
  Pallas kernels: 4.87 us -> 5.99 us
  waiting for transfers between devices: 0.92 us -> 0.41 us
    unnamed x5 -> x2, local copies, waits for them, and re-layouts: 1.69 us -> 0.01 us
    pallas_call x1, Pallas kernels: 0.19 us -> 1.04 us  [on_device(): pl.pallas_call(own_kernel, out_shape=(shape((128, COLS), jnp.int32), shap...]
    ppermute x2, waiting for transfers between devices: 0.92 us -> 0.31 us  [moved(): lax.ppermute(value, axis, [(i, (i + step) % size) for i in range(size)])]
    pallas_call x0 -> x1, Pallas kernels: none -> 0.59 us  [on_device(): pl.pallas_call(rows_kernel, out_shape=shape((7, 128, COLS), F32), in_spec...]
  transfers between devices with their start and end apart: 4 -> 4, of which waited for: 1 -> 2; matrix products, arithmetic and copies ran while one was open for 2% -> 0% of each run, Pallas kernels for 1% -> 5%
where the time goes in v4:
time: 33.4 us; the launch traced here: 33.1 us
  starting transfers between devices  26.6 us (80%)
  Pallas kernels  5.99 us (18%)
  waiting for transfers between devices  0.41 us (1%)
    ppermute x2, starting transfers between devices, swapped_pairs(): return lax.ppermute(value, axis, pairs + [(j, i) for i, j in pairs])  14.3 us
    ppermute x2, starting transfers between devices, moved(): lax.ppermute(value, axis, [(i, (i + step) % size) for i in range(size)])  12.3 us
    pallas_call x1, Pallas kernels, on_device(): pl.pallas_call(main_kernel, out_shape=shape(fields.shape, F32), in_specs=...  4.29 us
    pallas_call x1, Pallas kernels, on_device(): pl.pallas_call(own_kernel, out_shape=(shape((128, COLS), jnp.int32), shap...  1.04 us
  transfers between devices with their start and end apart: 4, of which 2 were waited for; matrix products, arithmetic and copies ran while one was open for 0% of the time, Pallas kernels for 5%

profile of v4, /device:TPU:1, one launch (start us, length us, event | category | flops | bytes accessed | tf_op | source)
XLA Modules:
  0.0 33.1 jit_solution(17314535780859076291)
XLA Ops:
  0.0 4.6 %collective-permute-start.1 = (f32[7,32,128]{2,1,0:T(8,128)}, f32[7,32,128]{2,1,0:T(8,128)S(1)}, u32[]{:S(2)}, u32[]{:S(2)}) collective-permute-start(f32[7,32,128]{2,1,0:T(8,128)} %fields_ref.3), channel_id=1, source_target_pairs={{12,24},{36,48},{60,72},{84,96},{108,120},{132,144},{156,168},{180... | collective-permute-start | bytes 344072 | tf_op jit(solution)/shard_map/ppermute | solution.py:446
  4.6 9.8 %collective-permute-start = (f32[7,32,128]{2,1,0:T(8,128)}, f32[7,32,128]{2,1,0:T(8,128)S(1)}, u32[]{:S(2)}, u32[]{:S(2)}) collective-permute-start(f32[7,32,128]{2,1,0:T(8,128)} %fields_ref.3), channel_id=1, source_target_pairs={{0,12},{24,36},{48,60},{72,84},{96,108},{120,132},{144,156},{168,1... | collective-permute-start | bytes 344072 | tf_op jit(solution)/shard_map/ppermute | solution.py:446
  14.4 1.0 %shard_map.28 = (s32[128,128]{1,0:T(8,128)S(1)}, s32[104,128]{1,0:T(8,128)S(1)}, s32[32,128]{1,0:T(8,128)S(1)}, f32[32,128]{1,0:T(8,128)S(1)}) custom-call(s32[12,64]{1,0:T(8,128)} %bitcast.1, f32[7,32,128]{2,1,0:T(8,128)} %fields_ref.3), custom_call_target="tpu_custom_call" | custom-call | tf_op jit(solution)/shard_map/pallas_call | solution.py:454
  15.4 0.0 collective-permute-done.1.far_ref
  15.4 0.1 collective-permute-done.close_ref
  15.5 0.0 copy-start
  15.5 0.1 shard_map.29
  15.6 1.9 %collective-permute-start.3 = (f32[48,128]{1,0:T(8,128)S(1)}, f32[48,128]{1,0:T(8,128)S(1)}, u32[]{:S(2)}, u32[]{:S(2)}) collective-permute-start(f32[48,128]{1,0:T(8,128)S(1)} %get-tuple-element.18), channel_id=1, source_target_pairs={{0,1},{1,2},{2,3},{3,4},{4,5},{5,6},{6,7},{7,8},{8,9},{9,10},{10,1... | collective-permute-start | bytes 73736 | tf_op jit(solution)/shard_map/ppermute | solution.py:440
  17.5 10.4 %collective-permute-start.2 = (f32[48,128]{1,0:T(8,128)S(1)}, f32[48,128]{1,0:T(8,128)S(1)}, u32[]{:S(2)}, u32[]{:S(2)}) collective-permute-start(f32[48,128]{1,0:T(8,128)S(1)} %get-tuple-element.18), channel_id=1, source_target_pairs={{0,11},{1,0},{2,1},{3,2},{4,3},{5,4},{6,5},{7,6},{8,7},{9,8},{10,9... | collective-permute-start | bytes 73736 | tf_op jit(solution)/shard_map/ppermute | solution.py:440
  27.9 0.0 copy-done
  27.9 0.6 %shard_map.30.own_ref = f32[7,128,128]{2,1,0:T(8,128)S(1)} custom-call(s32[128,128]{1,0:T(8,128)S(1)} %get-tuple-element.12.lev, f32[7,32,128]{2,1,0:T(8,128)S(1)} %copy-done, f32[7,8,128]{2,1,0:T(8,128)S(1)} %get-tuple-element.16.below_ref, f32[7,8,128]{2,1,0:T(8,128)S(1)} %get-tuple-element.17.above_ref), custom_call_target="tpu_custom_call" | custom-call | tf_op jit(solution)/shard_map/pallas_call | solution.py:482
  28.5 0.0 collective-permute-done.3.left_ref
  28.5 0.3 collective-permute-done.2.right_ref
  28.8 4.3 %shard_map.31 = f32[7,32,128]{2,1,0:T(8,128)} custom-call(s32[128,128]{1,0:T(8,128)S(1)} %get-tuple-element.12.lev, s32[104,128]{1,0:T(8,128)S(1)} %get-tuple-element.13.lev_strips, s32[32,128]{1,0:T(8,128)S(1)} %get-tuple-element.14.corner, f32[7,32,128]{2,1,0:T(8,128)S(1)} %copy-done, f32[7,128,128]{2,1,0:T(8,128)S(1)} %shard_map.30.own_ref, ...), custom_call_target="tpu_custom_call" | custom-call | tf_op jit(solution)/shard_map/pallas_call | solution.py:497
Async XLA Ops:
  0.0 15.4 %collective-permute-start.1 = (f32[7,32,128]{2,1,0:T(8,128)}, f32[7,32,128]{2,1,0:T(8,128)S(1)}, u32[]{:S(2)}, u32[]{:S(2)}) collective-permute-start(f32[7,32,128]{2,1,0:T(8,128)} %fields_ref.3), channel_id=1, source_target_pairs={{12,24},{36,48},{60,72},{84,96},{108,120},{132,144},{156,168},{180... | collective-permute-start | bytes 344072 | tf_op jit(solution)/shard_map/ppermute | solution.py:446
  4.6 10.9 %collective-permute-start = (f32[7,32,128]{2,1,0:T(8,128)}, f32[7,32,128]{2,1,0:T(8,128)S(1)}, u32[]{:S(2)}, u32[]{:S(2)}) collective-permute-start(f32[7,32,128]{2,1,0:T(8,128)} %fields_ref.3), channel_id=1, source_target_pairs={{0,12},{24,36},{48,60},{72,84},{96,108},{120,132},{144,156},{168,1... | collective-permute-start | bytes 344072 | tf_op jit(solution)/shard_map/ppermute | solution.py:446
  15.5 12.4 %copy-start = (f32[7,32,128]{2,1,0:T(8,128)S(1)}, f32[7,32,128]{2,1,0:T(8,128)}, u32[]{:S(2)}) copy-start(f32[7,32,128]{2,1,0:T(8,128)} %fields_ref.3) | copy-start | bytes 344068
  15.6 12.9 %collective-permute-start.3 = (f32[48,128]{1,0:T(8,128)S(1)}, f32[48,128]{1,0:T(8,128)S(1)}, u32[]{:S(2)}, u32[]{:S(2)}) collective-permute-start(f32[48,128]{1,0:T(8,128)S(1)} %get-tuple-element.18), channel_id=1, source_target_pairs={{0,1},{1,2},{2,3},{3,4},{4,5},{5,6},{6,7},{7,8},{8,9},{9,10},{10,1... | collective-permute-start | bytes 73736 | tf_op jit(solution)/shard_map/ppermute | solution.py:440
  17.5 11.3 %collective-permute-start.2 = (f32[48,128]{1,0:T(8,128)S(1)}, f32[48,128]{1,0:T(8,128)S(1)}, u32[]{:S(2)}, u32[]{:S(2)}) collective-permute-start(f32[48,128]{1,0:T(8,128)S(1)} %get-tuple-element.18), channel_id=1, source_target_pairs={{0,11},{1,0},{2,1},{3,2},{4,3},{5,4},{6,5},{7,6},{8,7},{9,8},{10,9... | collective-permute-start | bytes 73736 | tf_op jit(solution)/shard_map/ppermute | solution.py:440

commit v5 on v4

v5 whole, which is shorter than its diff:
```python
from functools import partial

import jax
import jax.numpy as jnp
from jax import lax
from jax.experimental import pallas as pl
from jax.experimental.pallas import tpu as pltpu
from jax.sharding import PartitionSpec as P

STEP_SIZE = 0.08
ROWS, COLS = 32, 128
F32 = jnp.float32
VMEM = pl.BlockSpec(memory_space=pltpu.VMEM)
HBM = pl.BlockSpec(memory_space=pltpu.HBM)

PAD = 8
TPAD = 16
MID, SIDE = PAD + 48, PAD + 80


def lane(rows):
    return lax.broadcasted_iota(jnp.int32, (rows, COLS), 1)


def gather_lanes(value, index):
    return jnp.take_along_axis(value, index, axis=1, mode="promise_in_bounds")


def near_rows(levels_ref, held_ref):
    sub_count, seg_count = levels_ref.shape
    for j in range(3):
        u = lax.rem(lax.axis_index("sub") + (j - 1 + sub_count), sub_count)
        held_ref[8 * j : 8 * j + 1, 0:seg_count] = levels_ref[pl.ds(u, 1), :]
    table = []
    for i in range(3):
        s = lax.rem(lax.axis_index("seg") + (i - 1 + seg_count), seg_count)
        s = jnp.full((8, COLS), s, jnp.int32)
        rows = [jnp.broadcast_to(held_ref[8 * j : 8 * j + 1, :], (8, COLS)) for j in range(3)]
        table.append([gather_lanes(row, s) for row in rows])

    def level_of(i, offset):
        first, middle, last = table[i]
        return jnp.where(offset < 0, first, jnp.where(offset > 0, last, middle))

    return level_of


def last_rows(ref, f, level):
    return jnp.where(
        level == 2, ref[f, 24:32, :], jnp.where(level == 1, ref[f, 8:16, :], ref[f, 0:8, :])
    )


def packed_cols(read, level):
    p = lane(8)
    first = jnp.where(level == 2, 120, jnp.where(level == 1, 56, 24))
    index = (p & 7) + jnp.where((p & 15) < 8, first, 0)
    packed = gather_lanes(read(0), index)
    for f in range(1, 7):
        packed = jnp.where((p >> 4) == f, gather_lanes(read(f), index), packed)
    return packed


def own_kernel(levels_hbm, fields_hbm, lev, lev_strips, corner, cols_ref, levels_ref, fields_ref, held, sems):
    copies = [
        pltpu.make_async_copy(levels_hbm, levels_ref, sems.at[0]),
        pltpu.make_async_copy(fields_hbm, fields_ref, sems.at[1]),
    ]
    for copy in copies:
        copy.start()
    copies[0].wait()
    level_of = near_rows(levels_ref, held)
    p8 = lane(8)
    inner = (p8 < 64) | ((p8 >= 80) & (p8 < 112))
    outer = ((p8 >= 64) & (p8 < 72)) | ((p8 >= 112) & (p8 < 120))
    middle = jnp.zeros((8, COLS), jnp.int32)
    offsets = (middle, jnp.where(inner, 0, jnp.where(outer, 1, -1)), jnp.where(p8 < 64, 1, -1))
    is_coarse = (p8 >= 72) & (p8 < 120)
    for kind, first in enumerate((0, 48, 80)):
        below_row, centre_row, above_row = (level_of(i, offsets[kind]) for i in range(3))
        lev[first : first + 8, :] = below_row
        lev[first + 8 : first + 16, :] = centre_row
        if kind == 1:
            lev[first + 16 : first + 24, :] = jnp.where(is_coarse, above_row, centre_row)
            lev[first + 24 : first + 32, :] = above_row
        else:
            for r in (16, 24, 32):
                lev[first + r : first + r + 8, :] = centre_row
            lev[first + 40 : first + 48, :] = above_row
    offset = jnp.where((p8 & 15) < 8, -1, 1)
    below_row, centre_row, above_row = (level_of(i, offset) for i in range(3))
    for first, count in ((0, 6), (48, 4), (80, 3)):
        for r in range(count):
            row = below_row if r == 0 else above_row if r == count - 1 else centre_row
            lev_strips[first + 8 * r : first + 8 * r + 8, :] = row
    beside = lev[48:80, :]
    beside = jnp.maximum(beside, pltpu.roll(beside, 1, 1))
    corner[0] = jnp.maximum(beside, pltpu.roll(beside, 1, 0))
    corner[1] = pltpu.roll(corner[0], 127, 1)
    own = lev[8:16, :]
    copies[1].wait()
    for r in range(0, 32, 8):
        cols_ref[r : r + 8, :] = packed_cols(lambda f: fields_ref[f, r : r + 8, :], own)


def cols_kernel(lev, cols_ref, close_ref, far_ref, out_ref, below_ref, above_ref):
    even = jnp.full((8, COLS), lax.rem(lax.axis_index("seg"), 2)) == 0
    below_level, above_level = lev[0:8, :], lev[40:48, :]
    for f in range(7):
        far, close = (last_rows(ref, f, below_level) for ref in (far_ref, close_ref))
        below_ref[f] = jnp.where(even, far, close)
        above_ref[f] = jnp.where(even, close_ref[f, 0:8, :], far_ref[f, 0:8, :])
    out_ref[0:8, :] = packed_cols(lambda f: below_ref[f], below_level)
    out_ref[8:40, :] = cols_ref[...]
    out_ref[40:48, :] = packed_cols(lambda f: above_ref[f], above_level)


def minmod(a, b):
    return jnp.minimum(jnp.maximum(b, jnp.minimum(a, 0.0)), jnp.maximum(a, 0.0))


def riemann(left, right, normal):
    rho_l, vn_l, vt_l, vz_l, bt_l, bz_l = left
    rho_r, vn_r, vt_r, vz_r, bt_r, bz_r = right
    normal_square = normal * normal

    def signal(density, speed, square):
        total = density + (square + normal_square)
        return jnp.abs(speed) + jnp.abs(total) * lax.rsqrt(density * total)

    square_l = bt_l * bt_l + bz_l * bz_l
    square_r = bt_r * bt_r + bz_r * bz_r
    fastest = jnp.maximum(signal(rho_l, vn_l, square_l), signal(rho_r, vn_r, square_r))
    mn_l, mt_l, mz_l = rho_l * vn_l, rho_l * vt_l, rho_l * vz_l
    mn_r, mt_r, mz_r = rho_r * vn_r, rho_r * vt_r, rho_r * vz_r

    def carried(value_l, value_r, pull):
        return (value_l * vn_l + value_r * vn_r - pull) - fastest * (value_r - value_l)

    pressure = (rho_l + rho_r) + 0.5 * (square_l + square_r)
    return [
        (mn_l + mn_r) - fastest * (rho_r - rho_l),
        carried(mn_l, mn_r, normal_square - pressure),
        carried(mt_l, mt_r, normal * (bt_l + bt_r)),
        carried(mz_l, mz_r, normal * (bz_l + bz_r)),
        carried(bt_l, bt_r, normal * (vt_l + vt_r)),
        carried(bz_l, bz_r, normal * (vz_l + vz_r)),
    ]


def doubled(part):
    low = lax.broadcasted_iota(jnp.int32, (8, COLS), 0) >> 1
    rows = []
    for r in range(0, part.shape[0], 8):
        for index in (low, low + 4):
            rows.append(
                jnp.take_along_axis(part[r : r + 8], index, axis=0, mode="promise_in_bounds")
            )
    return jnp.concatenate(rows, axis=0)


def rows_halved(ref, first, by_rows):
    initial = ref[pl.ds(first - 8, 32, stride=2), :]
    if not by_rows:
        return initial
    return 0.5 * (initial + ref[pl.ds(first - 7, 32, stride=2), :])


def paired_lanes(value, index, by_cols):
    initial = gather_lanes(value, index)
    return 0.5 * (initial + gather_lanes(value, index + 1)) if by_cols else initial


def down_two(ref, firsts, by_rows, by_cols, step=0):
    p = lane(32) + step
    index = (2 * p) & 127
    parts = [paired_lanes(rows_halved(ref, first, by_rows), index, by_cols) for first in firsts]
    return parts[0] if len(parts) == 1 else jnp.where((p & 127) < 64, parts[0], parts[1])


def down_one(ref, first, by_rows, by_cols, step=0):
    return paired_lanes(
        rows_halved(ref, first, by_rows), (2 * (lane(32) + step - 80)) & 127, by_cols
    )


def share_levels(win, out, lev, blocks, fields):
    p32, p24, p16 = lane(32), lane(24), lane(16)
    coarse32 = (p32 >= 72) & (p32 < 120)
    level_b = lev[48:80, :]
    up_one = jnp.where(p16 < 72, 80 + (p16 >> 1), jnp.where(p16 >= 120, 16 + (p16 >> 1), p16))
    up_two = (p24 >> 1, 64 + (p24 >> 1))
    for f in fields:
        by_rows, by_cols = f != 6, f != 5
        value = win[f, MID : MID + 32, :]
        up = doubled(gather_lanes(win[f, MID + 4 : MID + 20, :], up_one))
        part = win[f, MID + 4 : MID + 28, :]
        ups = [doubled(gather_lanes(part, up_two[k])) for k in range(len(blocks))]
        down = down_two(win.at[f], [PAD + first for first in blocks], by_rows, by_cols)
        last = down_one(win.at[f], MID, by_rows, by_cols)
        medium = jnp.where(level_b == 0, up, jnp.where(level_b == 2, down, value))
        coarse = jnp.where(level_b >= 1, last, value)
        for first, injected in zip(blocks, ups):
            rows = slice(PAD + first, PAD + first + 48)
            out[f, rows, :] = jnp.where(lev[first : first + 48, :] == 2, win[f, rows, :], injected)
        out[f, MID : MID + 32, :] = jnp.where(coarse32, coarse, medium)


def rows_kernel(lev, fields_ref, below_ref, above_ref, out_ref, win):
    p8 = lane(8)
    is_coarse = (p8 >= 72) & (p8 < 120)

    def joined(fine, coarse):
        return jnp.where(is_coarse, pltpu.roll(coarse, 80, 1), fine)

    for f in range(7):
        below, above = below_ref[f], above_ref[f]
        initial, second = fields_ref[f, 0:8, :], fields_ref[f, 8:16, :]
        win[f, PAD : PAD + 8, :] = below
        win[f, PAD + 8 : PAD + 40, :] = fields_ref[f]
        win[f, PAD + 40 : PAD + 48, :] = above
        win[f, MID : MID + 8, :] = joined(below, below)
        win[f, MID + 8 : MID + 16, :] = joined(initial, initial)
        win[f, MID + 16 : MID + 24, :] = joined(second, above)
        win[f, MID + 24 : MID + 32, :] = above
    share_levels(win, out_ref, lev, (0,), range(7))


def share_strips(strips, lev_strips, held):
    p = lane(32)
    k = p & 15
    up = (p - k) + jnp.where(k < 8, 4 + (k >> 1), 8 + ((k - 8) >> 1))
    down = (p - k) + ((2 * k - 8) & 15)
    held[8:56, :] = strips
    held[56:80, :] = strips[0:24]
    held[80:88, :] = strips[40:48]
    held[88:104, :] = strips[0:16]
    held[104:112, :] = strips[40:48]

    def halved(first, count):
        initial = held[pl.ds(first - 8, count, stride=2), :]
        mean = 0.5 * (initial + held[pl.ds(first - 7, count, stride=2), :])
        f = lane(count) >> 4
        value = jnp.where(f == 6, initial, mean)
        even, odd = (gather_lanes(value, down[0:count] + k) for k in range(2))
        return jnp.where(f == 5, even, 0.5 * (even + odd))

    levels = [lev_strips[first : first + count, :] for first, count in ((0, 48), (48, 32), (80, 24))]
    up_one = doubled(gather_lanes(held[92:108, :], up[0:16]))
    up_two = doubled(gather_lanes(held[60:84, :], up[0:24]))
    down_to_one, down_to_none = halved(8, 32), halved(56, 24)
    fine = jnp.where(levels[0] == 2, held[8:56, :], up_two)
    medium = jnp.where(levels[1] == 2, down_to_one, held[56:88, :])
    medium = jnp.where(levels[1] == 0, up_one, medium)
    coarse = jnp.where(levels[2] >= 1, down_to_none, held[88:112, :])
    return fine, medium, coarse


def main_kernel(
    lev,
    lev_strips,
    corner,
    fields_ref,
    own_ref,
    right_ref,
    left_ref,
    out_ref,
    win,
    base,
    prim,
    lefty,
    fluxy,
    gx,
    diffx,
    edge,
    fixed,
    turned,
    leftx,
    fluxx,
    held,
    result,
    sems,
):
    p32, p8 = lane(32), lane(8)
    is_coarse = (p8 >= 72) & (p8 < 120)
    own_level = lev[8:16, :]

    p48 = lane(48)
    strips = jnp.where((p48 & 15) < 8, left_ref[...], right_ref[...])
    fine, medium, coarse = share_strips(strips, lev_strips, held)
    strip_one = ((p32 >= 64) & (p32 < 72)) | (p32 >= 120)
    strip_none = ((p32 >= 72) & (p32 < 80)) | ((p32 >= 112) & (p32 < 120))
    right_side = ((p32 >= 64) & (p32 < 72)) | ((p32 >= 112) & (p32 < 120))
    strip_index = (p32 & 7) + jnp.where(right_side, 8, 0)
    for f in range(7):
        index = strip_index + 16 * f
        base[f, PAD : PAD + 48, :] = own_ref[f, PAD : PAD + 48, :]
        base[f, SIDE : SIDE + 48, :] = pltpu.roll(fine, (120 - 16 * f) % 128, 1)
        value = jnp.where(strip_one, gather_lanes(medium, index), own_ref[f, MID : MID + 32, :])
        base[f, MID + 24 : MID + 32, :] = value[24:32]
        base[f, MID : MID + 24, :] = jnp.where(
            strip_none[0:24], gather_lanes(coarse, index[0:24]), value[0:24]
        )

    def swapped(value):
        outside = jnp.where(p8 < 48, pltpu.roll(value, 48, 1), pltpu.roll(value, 80, 1))
        return jnp.where((p8 >= 48) & (p8 < 80), value, outside)

    def turn(slot, value):
        value = value.T
        turned[slot, TPAD : TPAD + 128, :] = value
        turned[slot, TPAD - 8 : TPAD, :] = swapped(value[120:128])
        turned[slot, TPAD + 128 : TPAD + 136, :] = swapped(value[0:8])

    chunks = [PAD + 16 * c for c in range(8)]

    def primitives():
        for row in chunks:
            rows = slice(row, row + 16)
            inverse = 1.0 / base[0, rows, :]
            for i in range(3):
                prim[i, rows, :] = base[1 + i, rows, :] * inverse
            prim[3, rows, :] = 0.5 * (base[6, rows, :] + base[6, row + 1 : row + 17, :])
        for rows in row_sets:
            faces = [base[5, row : row + 8, :] for row in rows]
            for row, face, other in zip(rows, faces, beside_cols(faces, False)):
                prim[4, row : row + 8, :] = 0.5 * (face + other)
        sources = [(base, 0), (prim, 0), (prim, 1), (prim, 2), (prim, 3), (base, 4), (base, 5)]
        for slot, (ref, i) in enumerate(sources):
            turn(slot, ref[i, PAD : PAD + 128, :])

    def sweep(items, lefts, row, count, normal):
        def at(item, step):
            ref, i = item
            return ref[i, row + step : row + step + count, :]

        left, right = [], []
        for i, item in enumerate(items):
            value = at(item, 0)
            slope = 0.5 * minmod(value - at(item, -1), at(item, 1) - value)
            lefts[i, row : row + count, :] = value + slope
            if normal is not None:
                left.append(lefts[i, row - 1 : row - 1 + count, :])
                right.append(value - slope)
        if normal is None:
            return None
        return riemann(left, right, at(normal, 0))

    def sweep_x():
        items = [(turned, i) for i in range(6)]
        sweep(items, leftx, TPAD - 8, 8, None)
        for row in [TPAD + 16 * c for c in range(9)]:
            count = 8 if row == TPAD + 128 else 16
            flux = sweep(items, leftx, row, count, (turned, 6))
            for i, value in enumerate(flux):
                fluxx[i, row : row + count, :] = value
        gx[PAD : PAD + 128, :] = fluxx[4, TPAD : TPAD + 128, :].T
        for i, n in enumerate((0, 1, 2, 3, 5)):
            value = fluxx[n, TPAD + 1 : TPAD + 129, :] - fluxx[n, TPAD : TPAD + 128, :]
            diffx[i, PAD : PAD + 128, :] = value.T

    def sweep_y():
        items = [(base, 0), (prim, 1), (prim, 0), (prim, 2), (prim, 4), (base, 4)]
        for row in chunks:
            flux = sweep(items, lefty, row, 16, (base, 6))
            for i, n in enumerate((0, 2, 1, 3, 5, 4)):
                fluxy[i, row : row + 16, :] = flux[n]

    def beside_cols(parts, back):
        parts = [pltpu.roll(part, 1 if back else 127, 1) for part in parts]
        edge_lane = p8 == (0 if back else 127)
        return [
            jnp.where(edge_lane, parts[1], parts[0]),
            jnp.where(edge_lane, parts[0], parts[1]),
        ] + parts[2:]

    row_sets = [
        (PAD + 8 * c, SIDE + 8 * c) + ((MID + 8 * c,) if c < 4 else ()) for c in range(6)
    ]

    def edges():
        for rows in row_sets:
            shifted = beside_cols([fluxy[5, row : row + 8, :] for row in rows], True)
            for row, other in zip(rows, shifted):
                value = (fluxy[5, row : row + 8, :] + other) - (
                    gx[row : row + 8, :] + gx[row - 1 : row + 7, :]
                )
                edge[row : row + 8, :] = 0.125 * value

    def correct():
        value = edge[MID : MID + 32, :]
        values = (value, pltpu.roll(value, 127, 1))
        for step in range(2):
            finest = corner[step]
            coarse = (p32 + step >= 72) & (p32 + step < 120)
            halved_two = down_two(edge, (PAD, SIDE), False, False, step)
            halved_one = down_one(edge, MID, False, False, step)
            value = jnp.where((finest == 2) & ~coarse, halved_two, values[step])
            fixed[step, 0:32, :] = jnp.where((finest >= 1) & coarse, halved_one, value)

    def update_cells(i):
        for rows in row_sets:
            for k, row in enumerate(rows):
                part = slice(row, row + 8)
                change = diffx[i, part, :] + (fluxy[i, row + 1 : row + 9, :] - fluxy[i, part, :])
                win[i, part, :] = base[i, part, :] - 0.5 * ratios[k] * change

    def update_faces():
        for rows in row_sets:
            values = [edge[row : row + 8, :] for row in rows[:2]]
            above = [edge[row + 1 : row + 9, :] for row in rows[:2]]
            others = beside_cols(values, False)
            for row in rows[2:]:
                first = row - MID
                values.append(fixed[0, first : first + 8, :])
                above.append(fixed[0, first + 1 : first + 9, :])
                others.append(fixed[1, first : first + 8, :])
            for row, ratio, value, up, other in zip(rows, ratios, values, above, others):
                part = slice(row, row + 8)
                win[5, part, :] = base[5, part, :] - ratio * (up - value)
                win[6, part, :] = base[6, part, :] + ratio * (other - value)

    ratios = (STEP_SIZE, STEP_SIZE, jnp.where(is_coarse, STEP_SIZE / 4, STEP_SIZE / 2))

    def shared(fields):
        share_levels(win, base, lev, (0, 80), fields)

    def finish(fields):
        zero = jnp.zeros((8, COLS), F32)
        for f in fields:
            for c in range(4):
                value = win[f, PAD + 8 + 8 * c : PAD + 16 + 8 * c, :]
                if c < 2:
                    medium = win[f, MID + 8 + 8 * c : MID + 16 + 8 * c, :]
                    coarse = pltpu.roll(medium, 48, 1) if c == 0 else zero
                    lower = jnp.where(own_level == 1, medium, coarse)
                    value = jnp.where(own_level == 2, value, lower)
                used = p8 < jnp.where(own_level == 2, 128, jnp.where(own_level == 1, 64, 32))
                used = used & (own_level >= (0, 1, 2, 2)[c])
                blend = 0.5 * (fields_ref[f, 8 * c : 8 * c + 8, :] + value)
                result[f, 8 * c : 8 * c + 8, :] = jnp.where(used, blend, 0.0)
            pltpu.make_async_copy(result.at[f], out_ref.at[f], sems.at[f]).start()

    for section in range(2):
        then = (shared, finish)[section]
        primitives()
        sweep_x()
        sweep_y()
        edges()
        update_cells(0)
        then((0,))
        correct()
        for i in range(1, 5):
            update_cells(i)
            then((i,))
            if i == 2:
                update_faces()
        then((5, 6))
    for f in range(7):
        pltpu.make_async_copy(result.at[f], out_ref.at[f], sems.at[f]).wait()


def moved(value, axis, step):
    size = lax.axis_size(axis)
    return lax.ppermute(value, axis, [(i, (i + step) % size) for i in range(size)])


def swapped_pairs(value, axis, first):
    size = lax.axis_size(axis)
    pairs = [(i, (i + 1) % size) for i in range(first, size, 2)]
    return lax.ppermute(value, axis, pairs + [(j, i) for i, j in pairs])


def on_device(fields, region_levels):
    shape = jax.ShapeDtypeStruct
    params = pltpu.CompilerParams(vmem_limit_bytes=32 * 1024 * 1024)
    far = swapped_pairs(fields, "seg", 1)
    close = swapped_pairs(fields, "seg", 0)
    lev, lev_strips, corner, cols = pl.pallas_call(
        own_kernel,
        out_shape=(
            shape((128, COLS), jnp.int32),
            shape((104, COLS), jnp.int32),
            shape((2, 32, COLS), jnp.int32),
            shape((32, COLS), F32),
        ),
        in_specs=[HBM] * 2,
        out_specs=(VMEM,) * 4,
        scratch_shapes=[
            pltpu.VMEM(region_levels.shape[::-1], jnp.int32),
            pltpu.VMEM(fields.shape, F32),
            pltpu.VMEM((24, COLS), jnp.int32),
            pltpu.SemaphoreType.DMA((2,)),
        ],
        compiler_params=params,
    )(*(pltpu.with_memory_space_constraint(x, pltpu.HBM) for x in (region_levels.T, fields)))
    rows = shape((7, 8, COLS), F32)
    packed, below, above = pl.pallas_call(
        cols_kernel,
        out_shape=(shape((48, COLS), F32), rows, rows),
        in_specs=[VMEM] * 4,
        out_specs=(VMEM,) * 3,
        compiler_params=params,
    )(lev, cols, close, far)
    right = moved(packed, "sub", -1)
    left = moved(packed, "sub", 1)
    own = pl.pallas_call(
        rows_kernel,
        out_shape=shape((7, PAD + 136, COLS), F32),
        in_specs=[VMEM] * 4,
        out_specs=VMEM,
        scratch_shapes=[pltpu.VMEM((7, PAD + 136, COLS), F32)],
        compiler_params=params,
    )(lev, fields, below, above)

    def window(*lead):
        return pltpu.VMEM((*lead, PAD + 136, COLS), F32)

    def across(*lead):
        return pltpu.VMEM((*lead, TPAD + 144, COLS), F32)

    return pl.pallas_call(
        main_kernel,
        out_shape=shape(fields.shape, F32),
        in_specs=[VMEM] * 7,
        out_specs=HBM,
        scratch_shapes=[
            window(7),
            window(7),
            window(5),
            window(6),
            window(6),
            window(),
            window(5),
            window(),
            pltpu.VMEM((2, 40, COLS), F32),
            across(7),
            across(6),
            across(6),
            pltpu.VMEM((112, COLS), F32),
            pltpu.VMEM(fields.shape, F32),
            pltpu.SemaphoreType.DMA((7,)),
        ],
        compiler_params=params,
    )(lev, lev_strips, corner, fields, own, right, left)


def solution(mesh):
    placed = (P(None, "seg", "sub"), P())
    return jax.shard_map(
        on_device, mesh=mesh, in_specs=placed, out_specs=P(None, "seg", "sub"), check_vma=False
    )
```

time: 33.4 us -> 32.6 us (0.976)
  Pallas kernels: 5.99 us -> 5.02 us
    pallas_call x1, Pallas kernels: 4.29 us -> 3.49 us  [on_device(): pl.pallas_call(main_kernel, out_shape=shape(fields.shape, F32), in_specs=...]
  transfers between devices with their start and end apart: 4 -> 4, of which waited for: 2 -> 2; matrix products, arithmetic and copies ran while one was open for 0% -> 0% of each run, Pallas kernels for 5% -> 4%
where the time goes in v5:
time: 32.6 us; the launch traced here: 32.3 us
  starting transfers between devices  26.6 us (82%)
  Pallas kernels  5.02 us (15%)
  waiting for transfers between devices  0.59 us (2%)
    ppermute x2, starting transfers between devices, swapped_pairs(): return lax.ppermute(value, axis, pairs + [(j, i) for i, j in pairs])  14.3 us
    ppermute x2, starting transfers between devices, moved(): lax.ppermute(value, axis, [(i, (i + step) % size) for i in range(size)])  12.3 us
    pallas_call x1, Pallas kernels, on_device(): pl.pallas_call(main_kernel, out_shape=shape(fields.shape, F32), in_specs=...  3.49 us
    pallas_call x1, Pallas kernels, on_device(): pl.pallas_call(own_kernel, out_shape=(shape((128, COLS), jnp.int32), shap...  1.05 us
  transfers between devices with their start and end apart: 4, of which 2 were waited for; matrix products, arithmetic and copies ran while one was open for 0% of the time, Pallas kernels for 4%

profile of v5, /device:TPU:1, one launch (start us, length us, event | category | flops | bytes accessed | tf_op | source)
XLA Modules:
  0.0 32.3 jit_solution(7788781798392229490)
XLA Ops:
  0.0 4.6 %collective-permute-start.1 = (f32[7,32,128]{2,1,0:T(8,128)}, f32[7,32,128]{2,1,0:T(8,128)S(1)}, u32[]{:S(2)}, u32[]{:S(2)}) collective-permute-start(f32[7,32,128]{2,1,0:T(8,128)} %fields_ref.3), channel_id=1, source_target_pairs={{12,24},{36,48},{60,72},{84,96},{108,120},{132,144},{156,168},{180... | collective-permute-start | bytes 344072 | tf_op jit(solution)/shard_map/ppermute | solution.py:471
  4.6 9.8 %collective-permute-start = (f32[7,32,128]{2,1,0:T(8,128)}, f32[7,32,128]{2,1,0:T(8,128)S(1)}, u32[]{:S(2)}, u32[]{:S(2)}) collective-permute-start(f32[7,32,128]{2,1,0:T(8,128)} %fields_ref.3), channel_id=1, source_target_pairs={{0,12},{24,36},{48,60},{72,84},{96,108},{120,132},{144,156},{168,1... | collective-permute-start | bytes 344072 | tf_op jit(solution)/shard_map/ppermute | solution.py:471
  14.4 1.1 %shard_map.28 = (s32[128,128]{1,0:T(8,128)S(1)}, s32[104,128]{1,0:T(8,128)S(1)}, s32[2,32,128]{2,1,0:T(8,128)S(1)}, f32[32,128]{1,0:T(8,128)S(1)}) custom-call(s32[12,64]{1,0:T(8,128)} %bitcast.1, f32[7,32,128]{2,1,0:T(8,128)} %fields_ref.3), custom_call_target="tpu_custom_call" | custom-call | tf_op jit(solution)/shard_map/pallas_call | solution.py:479
  15.4 0.0 collective-permute-done.1.far_ref
  15.4 0.1 collective-permute-done.close_ref
  15.5 0.0 copy-start
  15.5 0.1 shard_map.29
  15.6 1.9 %collective-permute-start.3 = (f32[48,128]{1,0:T(8,128)S(1)}, f32[48,128]{1,0:T(8,128)S(1)}, u32[]{:S(2)}, u32[]{:S(2)}) collective-permute-start(f32[48,128]{1,0:T(8,128)S(1)} %get-tuple-element.18), channel_id=1, source_target_pairs={{0,1},{1,2},{2,3},{3,4},{4,5},{5,6},{6,7},{7,8},{8,9},{9,10},{10,1... | collective-permute-start | bytes 73736 | tf_op jit(solution)/shard_map/ppermute | solution.py:465
  17.5 10.4 %collective-permute-start.2 = (f32[48,128]{1,0:T(8,128)S(1)}, f32[48,128]{1,0:T(8,128)S(1)}, u32[]{:S(2)}, u32[]{:S(2)}) collective-permute-start(f32[48,128]{1,0:T(8,128)S(1)} %get-tuple-element.18), channel_id=1, source_target_pairs={{0,11},{1,0},{2,1},{3,2},{4,3},{5,4},{6,5},{7,6},{8,7},{9,8},{10,9... | collective-permute-start | bytes 73736 | tf_op jit(solution)/shard_map/ppermute | solution.py:465
  27.9 0.0 copy-done
  27.9 0.4 %shard_map.30.own_ref = f32[7,144,128]{2,1,0:T(8,128)S(1)} custom-call(s32[128,128]{1,0:T(8,128)S(1)} %get-tuple-element.12.lev, f32[7,32,128]{2,1,0:T(8,128)S(1)} %copy-done, f32[7,8,128]{2,1,0:T(8,128)S(1)} %get-tuple-element.16.below_ref, f32[7,8,128]{2,1,0:T(8,128)S(1)} %get-tuple-element.17.above_ref), custom_call_target="tpu_custom_call" | custom-call | tf_op jit(solution)/shard_map/pallas_call | solution.py:507
  28.3 0.0 collective-permute-done.3.left_ref
  28.3 0.5 %collective-permute-done.2.right_ref = f32[48,128]{1,0:T(8,128)S(1)} collective-permute-done((f32[48,128]{1,0:T(8,128)S(1)}, f32[48,128]{1,0:T(8,128)S(1)}, u32[]{:S(2)}, u32[]{:S(2)}) %collective-permute-start.2) | collective-permute-done | bytes 24608 | tf_op jit(solution)/shard_map/ppermute | solution.py:465
  28.8 3.5 %shard_map.31 = f32[7,32,128]{2,1,0:T(8,128)} custom-call(s32[128,128]{1,0:T(8,128)S(1)} %get-tuple-element.12.lev, s32[104,128]{1,0:T(8,128)S(1)} %get-tuple-element.13.lev_strips, s32[2,32,128]{2,1,0:T(8,128)S(1)} %get-tuple-element.14.corner, f32[7,32,128]{2,1,0:T(8,128)S(1)} %copy-done, f32[7,144,128]{2,1,0:T(8,128)S(1)} %shard_map.30.own_ref, ...), custom_call_target="tpu_custom_call" | custom-call | tf_op jit(solution)/shard_map/pallas_call | solution.py:522
Async XLA Ops:
  0.0 15.4 %collective-permute-start.1 = (f32[7,32,128]{2,1,0:T(8,128)}, f32[7,32,128]{2,1,0:T(8,128)S(1)}, u32[]{:S(2)}, u32[]{:S(2)}) collective-permute-start(f32[7,32,128]{2,1,0:T(8,128)} %fields_ref.3), channel_id=1, source_target_pairs={{12,24},{36,48},{60,72},{84,96},{108,120},{132,144},{156,168},{180... | collective-permute-start | bytes 344072 | tf_op jit(solution)/shard_map/ppermute | solution.py:471
  4.6 10.9 %collective-permute-start = (f32[7,32,128]{2,1,0:T(8,128)}, f32[7,32,128]{2,1,0:T(8,128)S(1)}, u32[]{:S(2)}, u32[]{:S(2)}) collective-permute-start(f32[7,32,128]{2,1,0:T(8,128)} %fields_ref.3), channel_id=1, source_target_pairs={{0,12},{24,36},{48,60},{72,84},{96,108},{120,132},{144,156},{168,1... | collective-permute-start | bytes 344072 | tf_op jit(solution)/shard_map/ppermute | solution.py:471
  15.5 12.4 %copy-start = (f32[7,32,128]{2,1,0:T(8,128)S(1)}, f32[7,32,128]{2,1,0:T(8,128)}, u32[]{:S(2)}) copy-start(f32[7,32,128]{2,1,0:T(8,128)} %fields_ref.3) | copy-start | bytes 344068
  15.6 12.7 %collective-permute-start.3 = (f32[48,128]{1,0:T(8,128)S(1)}, f32[48,128]{1,0:T(8,128)S(1)}, u32[]{:S(2)}, u32[]{:S(2)}) collective-permute-start(f32[48,128]{1,0:T(8,128)S(1)} %get-tuple-element.18), channel_id=1, source_target_pairs={{0,1},{1,2},{2,3},{3,4},{4,5},{5,6},{6,7},{7,8},{8,9},{9,10},{10,1... | collective-permute-start | bytes 73736 | tf_op jit(solution)/shard_map/ppermute | solution.py:465
  17.5 11.3 %collective-permute-start.2 = (f32[48,128]{1,0:T(8,128)S(1)}, f32[48,128]{1,0:T(8,128)S(1)}, u32[]{:S(2)}, u32[]{:S(2)}) collective-permute-start(f32[48,128]{1,0:T(8,128)S(1)} %get-tuple-element.18), channel_id=1, source_target_pairs={{0,11},{1,0},{2,1},{3,2},{4,3},{5,4},{6,5},{7,6},{8,7},{9,8},{10,9... | collective-permute-start | bytes 73736 | tf_op jit(solution)/shard_map/ppermute | solution.py:465

commit v6 on v5

--- a/solution.py
+++ b/solution.py
@@ -103,13 +103,16 @@
         cols_ref[r : r + 8, :] = packed_cols(lambda f: fields_ref[f, r : r + 8, :], own)
 
 
-def cols_kernel(lev, cols_ref, close_ref, far_ref, out_ref, below_ref, above_ref):
-    even = jnp.full((8, COLS), lax.rem(lax.axis_index("seg"), 2)) == 0
+def cols_kernel(lev, cols_ref, wrap_ref, close_ref, far_ref, out_ref, below_ref, above_ref):
+    seg, last = lax.axis_index("seg"), lax.axis_size("seg") - 1
+    even = jnp.full((8, COLS), lax.rem(seg, 2)) == 0
+    ends = jnp.full((8, COLS), lax.rem(seg, last)) == 0
     below_level, above_level = lev[0:8, :], lev[40:48, :]
     for f in range(7):
-        far, close = (last_rows(ref, f, below_level) for ref in (far_ref, close_ref))
-        below_ref[f] = jnp.where(even, far, close)
-        above_ref[f] = jnp.where(even, close_ref[f, 0:8, :], far_ref[f, 0:8, :])
+        far, wrap, close = (last_rows(r, f, below_level) for r in (far_ref, wrap_ref, close_ref))
+        below_ref[f] = jnp.where(even, jnp.where(ends, wrap, far), close)
+        far = jnp.where(ends, wrap_ref[f, 0:8, :], far_ref[f, 0:8, :])
+        above_ref[f] = jnp.where(even, close_ref[f, 0:8, :], far)
     out_ref[0:8, :] = packed_cols(lambda f: below_ref[f], below_level)
     out_ref[8:40, :] = cols_ref[...]
     out_ref[40:48, :] = packed_cols(lambda f: above_ref[f], above_level)
@@ -131,20 +134,16 @@
     square_l = bt_l * bt_l + bz_l * bz_l
     square_r = bt_r * bt_r + bz_r * bz_r
     fastest = jnp.maximum(signal(rho_l, vn_l, square_l), signal(rho_r, vn_r, square_r))
-    mn_l, mt_l, mz_l = rho_l * vn_l, rho_l * vt_l, rho_l * vz_l
-    mn_r, mt_r, mz_r = rho_r * vn_r, rho_r * vt_r, rho_r * vz_r
-
-    def carried(value_l, value_r, pull):
-        return (value_l * vn_l + value_r * vn_r - pull) - fastest * (value_r - value_l)
-
+    ahead, back = vn_l + fastest, vn_r - fastest
+    mass_l, mass_r = rho_l * ahead, rho_r * back
     pressure = (rho_l + rho_r) + 0.5 * (square_l + square_r)
     return [
-        (mn_l + mn_r) - fastest * (rho_r - rho_l),
-        carried(mn_l, mn_r, normal_square - pressure),
-        carried(mt_l, mt_r, normal * (bt_l + bt_r)),
-        carried(mz_l, mz_r, normal * (bz_l + bz_r)),
-        carried(bt_l, bt_r, normal * (vt_l + vt_r)),
-        carried(bz_l, bz_r, normal * (vz_l + vz_r)),
+        mass_l + mass_r,
+        (mass_l * vn_l + mass_r * vn_r) + (pressure - normal_square),
+        (mass_l * vt_l + mass_r * vt_r) - normal * (bt_l + bt_r),
+        (mass_l * vz_l + mass_r * vz_r) - normal * (bz_l + bz_r),
+        (bt_l * ahead + bt_r * back) - normal * (vt_l + vt_r),
+        (bz_l * ahead + bz_r * back) - normal * (vz_l + vz_r),
     ]
 
 
@@ -465,17 +464,19 @@
     return lax.ppermute(value, axis, [(i, (i + step) % size) for i in range(size)])
 
 
-def swapped_pairs(value, axis, first):
+def swapped_pairs(value, axis, first, stop):
     size = lax.axis_size(axis)
-    pairs = [(i, (i + 1) % size) for i in range(first, size, 2)]
+    pairs = [(i, (i + 1) % size) for i in range(first, stop, 2)]
     return lax.ppermute(value, axis, pairs + [(j, i) for i, j in pairs])
 
 
 def on_device(fields, region_levels):
     shape = jax.ShapeDtypeStruct
     params = pltpu.CompilerParams(vmem_limit_bytes=32 * 1024 * 1024)
-    far = swapped_pairs(fields, "seg", 1)
-    close = swapped_pairs(fields, "seg", 0)
+    size = lax.axis_size("seg")
+    wrap = swapped_pairs(fields, "seg", size - 1, size)
+    close = swapped_pairs(fields, "seg", 0, size)
+    far = swapped_pairs(fields, "seg", 1, size - 1)
     lev, lev_strips, corner, cols = pl.pallas_call(
         own_kernel,
         out_shape=(
@@ -498,10 +499,10 @@
     packed, below, above = pl.pallas_call(
         cols_kernel,
         out_shape=(shape((48, COLS), F32), rows, rows),
-        in_specs=[VMEM] * 4,
+        in_specs=[VMEM] * 5,
         out_specs=(VMEM,) * 3,
         compiler_params=params,
-    )(lev, cols, close, far)
+    )(lev, cols, wrap, close, far)
     right = moved(packed, "sub", -1)
     left = moved(packed, "sub", 1)
     own = pl.pallas_call(

time: 32.6 us -> 35.8 us (1.098)
  the two profiles are of different devices: /device:TPU:1 before, /device:TPU:63 now
where the time goes in v6:
time: 35.8 us; the launch traced here: 35.6 us
  starting transfers between devices  28.5 us (80%)
  Pallas kernels  4.91 us (14%)
  waiting for transfers between devices  2.09 us (6%)
    ppermute x2, starting transfers between devices, moved(): lax.ppermute(value, axis, [(i, (i + step) % size) for i in range(size)])  15 us
    ppermute x3, starting transfers between devices, swapped_pairs(): return lax.ppermute(value, axis, pairs + [(j, i) for i, j in pairs])  13.5 us
    pallas_call x1, Pallas kernels, on_device(): pl.pallas_call(main_kernel, out_shape=shape(fields.shape, F32), in_specs=...  3.35 us
    ppermute x3, waiting for transfers between devices, swapped_pairs(): return lax.ppermute(value, axis, pairs + [(j, i) for i, j in pairs])  1.58 us
    pallas_call x1, Pallas kernels, on_device(): pl.pallas_call(own_kernel, out_shape=(shape((128, COLS), jnp.int32), shap...  1.07 us
  transfers between devices with their start and end apart: 5, of which 2 were waited for; matrix products, arithmetic and copies ran while one was open for 0% of the time, Pallas kernels for 4%

profile of v6, /device:TPU:63, one launch (start us, length us, event | category | flops | bytes accessed | tf_op | source)
XLA Modules:
  0.0 35.6 jit_solution(13649831124742284701)
XLA Ops:
  0.0 0.7 %collective-permute-start.2 = (f32[7,32,128]{2,1,0:T(8,128)}, f32[7,32,128]{2,1,0:T(8,128)S(1)}, u32[]{:S(2)}, u32[]{:S(2)}) collective-permute-start(f32[7,32,128]{2,1,0:T(8,128)} %fields_ref.3), channel_id=1, source_target_pairs={{12,24},{36,48},{60,72},{84,96},{108,120},{132,144},{156,168},{180... | collective-permute-start | bytes 344072 | tf_op jit(solution)/shard_map/ppermute | solution.py:470
  0.7 4.6 %collective-permute-start.1 = (f32[7,32,128]{2,1,0:T(8,128)}, f32[7,32,128]{2,1,0:T(8,128)S(1)}, u32[]{:S(2)}, u32[]{:S(2)}) collective-permute-start(f32[7,32,128]{2,1,0:T(8,128)} %fields_ref.3), channel_id=1, source_target_pairs={{0,12},{24,36},{48,60},{72,84},{96,108},{120,132},{144,156},{168,1... | collective-permute-start | bytes 344072 | tf_op jit(solution)/shard_map/ppermute | solution.py:470
  5.3 8.2 %collective-permute-start = (f32[7,32,128]{2,1,0:T(8,128)}, f32[7,32,128]{2,1,0:T(8,128)S(1)}, u32[]{:S(2)}, u32[]{:S(2)}) collective-permute-start(f32[7,32,128]{2,1,0:T(8,128)} %fields_ref.3), channel_id=1, source_target_pairs={{756,0},{0,756},{757,1},{1,757},{758,2},{2,758},{759,3},{3,759},{7... | collective-permute-start | bytes 344072 | tf_op jit(solution)/shard_map/ppermute | solution.py:470
  13.5 1.1 %shard_map.28 = (s32[128,128]{1,0:T(8,128)S(1)}, s32[104,128]{1,0:T(8,128)S(1)}, s32[2,32,128]{2,1,0:T(8,128)S(1)}, f32[32,128]{1,0:T(8,128)S(1)}) custom-call(s32[12,64]{1,0:T(8,128)} %bitcast.1, f32[7,32,128]{2,1,0:T(8,128)} %fields_ref.3), custom_call_target="tpu_custom_call" | custom-call | tf_op jit(solution)/shard_map/pallas_call | solution.py:480
  14.6 0.0 collective-permute-done.2.far_ref
  14.6 0.0 collective-permute-done.1.close_ref
  14.6 1.6 %collective-permute-done.wrap_ref = f32[7,32,128]{2,1,0:T(8,128)S(1)} collective-permute-done((f32[7,32,128]{2,1,0:T(8,128)}, f32[7,32,128]{2,1,0:T(8,128)S(1)}, u32[]{:S(2)}, u32[]{:S(2)}) %collective-permute-start) | collective-permute-done | bytes 114720 | tf_op jit(solution)/shard_map/ppermute | solution.py:470
  16.2 0.0 copy-start
  16.2 0.1 shard_map.29
  16.3 2.8 %collective-permute-start.4 = (f32[48,128]{1,0:T(8,128)S(1)}, f32[48,128]{1,0:T(8,128)S(1)}, u32[]{:S(2)}, u32[]{:S(2)}) collective-permute-start(f32[48,128]{1,0:T(8,128)S(1)} %get-tuple-element.18), channel_id=1, source_target_pairs={{0,1},{1,2},{2,3},{3,4},{4,5},{5,6},{6,7},{7,8},{8,9},{9,10},{10,1... | collective-permute-start | bytes 73736 | tf_op jit(solution)/shard_map/ppermute | solution.py:464
  19.0 12.2 %collective-permute-start.3 = (f32[48,128]{1,0:T(8,128)S(1)}, f32[48,128]{1,0:T(8,128)S(1)}, u32[]{:S(2)}, u32[]{:S(2)}) collective-permute-start(f32[48,128]{1,0:T(8,128)S(1)} %get-tuple-element.18), channel_id=1, source_target_pairs={{0,11},{1,0},{2,1},{3,2},{4,3},{5,4},{6,5},{7,6},{8,7},{9,8},{10,9... | collective-permute-start | bytes 73736 | tf_op jit(solution)/shard_map/ppermute | solution.py:464
  31.3 0.0 copy-done
  31.3 0.4 %shard_map.30.own_ref = f32[7,144,128]{2,1,0:T(8,128)S(1)} custom-call(s32[128,128]{1,0:T(8,128)S(1)} %get-tuple-element.12.lev, f32[7,32,128]{2,1,0:T(8,128)S(1)} %copy-done, f32[7,8,128]{2,1,0:T(8,128)S(1)} %get-tuple-element.16.below_ref, f32[7,8,128]{2,1,0:T(8,128)S(1)} %get-tuple-element.17.above_ref), custom_call_target="tpu_custom_call" | custom-call | tf_op jit(solution)/shard_map/pallas_call | solution.py:508
  31.7 0.0 collective-permute-done.4.left_ref
  31.7 0.5 %collective-permute-done.3.right_ref = f32[48,128]{1,0:T(8,128)S(1)} collective-permute-done((f32[48,128]{1,0:T(8,128)S(1)}, f32[48,128]{1,0:T(8,128)S(1)}, u32[]{:S(2)}, u32[]{:S(2)}) %collective-permute-start.3) | collective-permute-done | bytes 24608 | tf_op jit(solution)/shard_map/ppermute | solution.py:464
  32.2 3.4 %shard_map.31 = f32[7,32,128]{2,1,0:T(8,128)} custom-call(s32[128,128]{1,0:T(8,128)S(1)} %get-tuple-element.12.lev, s32[104,128]{1,0:T(8,128)S(1)} %get-tuple-element.13.lev_strips, s32[2,32,128]{2,1,0:T(8,128)S(1)} %get-tuple-element.14.corner, f32[7,32,128]{2,1,0:T(8,128)S(1)} %copy-done, f32[7,144,128]{2,1,0:T(8,128)S(1)} %shard_map.30.own_ref, ...), custom_call_target="tpu_custom_call" | custom-call | tf_op jit(solution)/shard_map/pallas_call | solution.py:523
Async XLA Ops:
  0.0 14.6 %collective-permute-start.2 = (f32[7,32,128]{2,1,0:T(8,128)}, f32[7,32,128]{2,1,0:T(8,128)S(1)}, u32[]{:S(2)}, u32[]{:S(2)}) collective-permute-start(f32[7,32,128]{2,1,0:T(8,128)} %fields_ref.3), channel_id=1, source_target_pairs={{12,24},{36,48},{60,72},{84,96},{108,120},{132,144},{156,168},{180... | collective-permute-start | bytes 344072 | tf_op jit(solution)/shard_map/ppermute | solution.py:470
  0.7 13.9 %collective-permute-start.1 = (f32[7,32,128]{2,1,0:T(8,128)}, f32[7,32,128]{2,1,0:T(8,128)S(1)}, u32[]{:S(2)}, u32[]{:S(2)}) collective-permute-start(f32[7,32,128]{2,1,0:T(8,128)} %fields_ref.3), channel_id=1, source_target_pairs={{0,12},{24,36},{48,60},{72,84},{96,108},{120,132},{144,156},{168,1... | collective-permute-start | bytes 344072 | tf_op jit(solution)/shard_map/ppermute | solution.py:470
  5.3 10.9 %collective-permute-start = (f32[7,32,128]{2,1,0:T(8,128)}, f32[7,32,128]{2,1,0:T(8,128)S(1)}, u32[]{:S(2)}, u32[]{:S(2)}) collective-permute-start(f32[7,32,128]{2,1,0:T(8,128)} %fields_ref.3), channel_id=1, source_target_pairs={{756,0},{0,756},{757,1},{1,757},{758,2},{2,758},{759,3},{3,759},{7... | collective-permute-start | bytes 344072 | tf_op jit(solution)/shard_map/ppermute | solution.py:470
  16.2 15.1 %copy-start = (f32[7,32,128]{2,1,0:T(8,128)S(1)}, f32[7,32,128]{2,1,0:T(8,128)}, u32[]{:S(2)}) copy-start(f32[7,32,128]{2,1,0:T(8,128)} %fields_ref.3) | copy-start | bytes 344068
  16.3 15.4 %collective-permute-start.4 = (f32[48,128]{1,0:T(8,128)S(1)}, f32[48,128]{1,0:T(8,128)S(1)}, u32[]{:S(2)}, u32[]{:S(2)}) collective-permute-start(f32[48,128]{1,0:T(8,128)S(1)} %get-tuple-element.18), channel_id=1, source_target_pairs={{0,1},{1,2},{2,3},{3,4},{4,5},{5,6},{6,7},{7,8},{8,9},{9,10},{10,1... | collective-permute-start | bytes 73736 | tf_op jit(solution)/shard_map/ppermute | solution.py:464
  19.0 13.2 %collective-permute-start.3 = (f32[48,128]{1,0:T(8,128)S(1)}, f32[48,128]{1,0:T(8,128)S(1)}, u32[]{:S(2)}, u32[]{:S(2)}) collective-permute-start(f32[48,128]{1,0:T(8,128)S(1)} %get-tuple-element.18), channel_id=1, source_target_pairs={{0,11},{1,0},{2,1},{3,2},{4,3},{5,4},{6,5},{7,6},{8,7},{9,8},{10,9... | collective-permute-start | bytes 73736 | tf_op jit(solution)/shard_map/ppermute | solution.py:464

commit v7 on v6

--- a/solution.py
+++ b/solution.py
@@ -103,16 +103,16 @@
         cols_ref[r : r + 8, :] = packed_cols(lambda f: fields_ref[f, r : r + 8, :], own)
 
 
-def cols_kernel(lev, cols_ref, wrap_ref, close_ref, far_ref, out_ref, below_ref, above_ref):
-    seg, last = lax.axis_index("seg"), lax.axis_size("seg") - 1
+def cols_kernel(lev, cols_ref, close_ref, far_ref, first_ref, out_ref, below_ref, above_ref):
+    seg = lax.axis_index("seg")
     even = jnp.full((8, COLS), lax.rem(seg, 2)) == 0
-    ends = jnp.full((8, COLS), lax.rem(seg, last)) == 0
+    early = jnp.full((8, COLS), seg) < 2
     below_level, above_level = lev[0:8, :], lev[40:48, :]
     for f in range(7):
-        far, wrap, close = (last_rows(r, f, below_level) for r in (far_ref, wrap_ref, close_ref))
-        below_ref[f] = jnp.where(even, jnp.where(ends, wrap, far), close)
-        far = jnp.where(ends, wrap_ref[f, 0:8, :], far_ref[f, 0:8, :])
-        above_ref[f] = jnp.where(even, close_ref[f, 0:8, :], far)
+        far, close, first = (last_rows(r, f, below_level) for r in (far_ref, close_ref, first_ref))
+        below_ref[f] = jnp.where(even, far, jnp.where(early, first, close))
+        close = jnp.where(early, first_ref[f, 0:8, :], close_ref[f, 0:8, :])
+        above_ref[f] = jnp.where(even, close, far_ref[f, 0:8, :])
     out_ref[0:8, :] = packed_cols(lambda f: below_ref[f], below_level)
     out_ref[8:40, :] = cols_ref[...]
     out_ref[40:48, :] = packed_cols(lambda f: above_ref[f], above_level)
@@ -474,9 +474,9 @@
     shape = jax.ShapeDtypeStruct
     params = pltpu.CompilerParams(vmem_limit_bytes=32 * 1024 * 1024)
     size = lax.axis_size("seg")
-    wrap = swapped_pairs(fields, "seg", size - 1, size)
-    close = swapped_pairs(fields, "seg", 0, size)
-    far = swapped_pairs(fields, "seg", 1, size - 1)
+    close = swapped_pairs(fields, "seg", 2, size)
+    far = swapped_pairs(fields, "seg", 1, size)
+    first = swapped_pairs(fields, "seg", 0, 2)
     lev, lev_strips, corner, cols = pl.pallas_call(
         own_kernel,
         out_shape=(
@@ -502,7 +502,7 @@
         in_specs=[VMEM] * 5,
         out_specs=(VMEM,) * 3,
         compiler_params=params,
-    )(lev, cols, wrap, close, far)
+    )(lev, cols, close, far, first)
     right = moved(packed, "sub", -1)
     left = moved(packed, "sub", 1)
     own = pl.pallas_call(

time: 35.8 us -> 31.2 us (0.87)
  starting transfers between devices: 28.5 us -> 25 us
  waiting for transfers between devices: 2.09 us -> 0.93 us
    ppermute x2, starting transfers between devices: 15 us -> 10.3 us  [moved(): lax.ppermute(value, axis, [(i, (i + step) % size) for i in range(size)])]
    ppermute x3, starting transfers between devices: 13.5 us -> 14.7 us  [swapped_pairs(): return lax.ppermute(value, axis, pairs + [(j, i) for i, j in pairs])]
    ppermute x3, waiting for transfers between devices: 1.58 us -> 0.42 us  [swapped_pairs(): return lax.ppermute(value, axis, pairs + [(j, i) for i, j in pairs])]
  transfers between devices with their start and end apart: 5 -> 5, of which waited for: 2 -> 2; matrix products, arithmetic and copies ran while one was open for 0% -> 0% of each run, Pallas kernels for 4% -> 5%
where the time goes in v7:
time: 31.2 us; the launch traced here: 30.9 us
  starting transfers between devices  25 us (80%)
  Pallas kernels  4.89 us (16%)
  waiting for transfers between devices  0.93 us (3%)
    ppermute x3, starting transfers between devices, swapped_pairs(): return lax.ppermute(value, axis, pairs + [(j, i) for i, j in pairs])  14.7 us
    ppermute x2, starting transfers between devices, moved(): lax.ppermute(value, axis, [(i, (i + step) % size) for i in range(size)])  10.3 us
    pallas_call x1, Pallas kernels, on_device(): pl.pallas_call(main_kernel, out_shape=shape(fields.shape, F32), in_specs=...  3.35 us
    pallas_call x1, Pallas kernels, on_device(): pl.pallas_call(own_kernel, out_shape=(shape((128, COLS), jnp.int32), shap...  1.05 us
  transfers between devices with their start and end apart: 5, of which 2 were waited for; matrix products, arithmetic and copies ran while one was open for 0% of the time, Pallas kernels for 5%

profile of v7, /device:TPU:63, one launch (start us, length us, event | category | flops | bytes accessed | tf_op | source)
XLA Modules:
  0.0 30.9 jit_solution(835082056083751405)
XLA Ops:
  0.0 0.7 %collective-permute-start.2 = (f32[7,32,128]{2,1,0:T(8,128)}, f32[7,32,128]{2,1,0:T(8,128)S(1)}, u32[]{:S(2)}, u32[]{:S(2)}) collective-permute-start(f32[7,32,128]{2,1,0:T(8,128)} %fields_ref.3), channel_id=1, source_target_pairs={{0,12},{12,0},{1,13},{13,1},{2,14},{14,2},{3,15},{15,3},{4,16},{16... | collective-permute-start | bytes 344072 | tf_op jit(solution)/shard_map/ppermute | solution.py:470
  0.7 12.1 %collective-permute-start.1 = (f32[7,32,128]{2,1,0:T(8,128)}, f32[7,32,128]{2,1,0:T(8,128)S(1)}, u32[]{:S(2)}, u32[]{:S(2)}) collective-permute-start(f32[7,32,128]{2,1,0:T(8,128)} %fields_ref.3), channel_id=1, source_target_pairs={{12,24},{36,48},{60,72},{84,96},{108,120},{132,144},{156,168},{180... | collective-permute-start | bytes 344072 | tf_op jit(solution)/shard_map/ppermute | solution.py:470
  12.8 1.9 %collective-permute-start = (f32[7,32,128]{2,1,0:T(8,128)}, f32[7,32,128]{2,1,0:T(8,128)S(1)}, u32[]{:S(2)}, u32[]{:S(2)}) collective-permute-start(f32[7,32,128]{2,1,0:T(8,128)} %fields_ref.3), channel_id=1, source_target_pairs={{24,36},{48,60},{72,84},{96,108},{120,132},{144,156},{168,180},{19... | collective-permute-start | bytes 344072 | tf_op jit(solution)/shard_map/ppermute | solution.py:470
  14.7 1.1 %shard_map.28 = (s32[128,128]{1,0:T(8,128)S(1)}, s32[104,128]{1,0:T(8,128)S(1)}, s32[2,32,128]{2,1,0:T(8,128)S(1)}, f32[32,128]{1,0:T(8,128)S(1)}) custom-call(s32[12,64]{1,0:T(8,128)} %bitcast.1, f32[7,32,128]{2,1,0:T(8,128)} %fields_ref.3), custom_call_target="tpu_custom_call" | custom-call | tf_op jit(solution)/shard_map/pallas_call | solution.py:480
  15.8 0.0 collective-permute-done.2.first_ref
  15.8 0.0 collective-permute-done.1.far_ref
  15.8 0.4 %collective-permute-done.close_ref = f32[7,32,128]{2,1,0:T(8,128)S(1)} collective-permute-done((f32[7,32,128]{2,1,0:T(8,128)}, f32[7,32,128]{2,1,0:T(8,128)S(1)}, u32[]{:S(2)}, u32[]{:S(2)}) %collective-permute-start) | collective-permute-done | bytes 114720 | tf_op jit(solution)/shard_map/ppermute | solution.py:470
  16.2 0.0 copy-start
  16.2 0.1 shard_map.29
  16.3 1.9 %collective-permute-start.4 = (f32[48,128]{1,0:T(8,128)S(1)}, f32[48,128]{1,0:T(8,128)S(1)}, u32[]{:S(2)}, u32[]{:S(2)}) collective-permute-start(f32[48,128]{1,0:T(8,128)S(1)} %get-tuple-element.18), channel_id=1, source_target_pairs={{0,1},{1,2},{2,3},{3,4},{4,5},{5,6},{6,7},{7,8},{8,9},{9,10},{10,1... | collective-permute-start | bytes 73736 | tf_op jit(solution)/shard_map/ppermute | solution.py:464
  18.3 8.4 %collective-permute-start.3 = (f32[48,128]{1,0:T(8,128)S(1)}, f32[48,128]{1,0:T(8,128)S(1)}, u32[]{:S(2)}, u32[]{:S(2)}) collective-permute-start(f32[48,128]{1,0:T(8,128)S(1)} %get-tuple-element.18), channel_id=1, source_target_pairs={{0,11},{1,0},{2,1},{3,2},{4,3},{5,4},{6,5},{7,6},{8,7},{9,8},{10,9... | collective-permute-start | bytes 73736 | tf_op jit(solution)/shard_map/ppermute | solution.py:464
  26.6 0.0 copy-done
  26.7 0.4 %shard_map.30.own_ref = f32[7,144,128]{2,1,0:T(8,128)S(1)} custom-call(s32[128,128]{1,0:T(8,128)S(1)} %get-tuple-element.12.lev, f32[7,32,128]{2,1,0:T(8,128)S(1)} %copy-done, f32[7,8,128]{2,1,0:T(8,128)S(1)} %get-tuple-element.16.below_ref, f32[7,8,128]{2,1,0:T(8,128)S(1)} %get-tuple-element.17.above_ref), custom_call_target="tpu_custom_call" | custom-call | tf_op jit(solution)/shard_map/pallas_call | solution.py:508
  27.1 0.0 collective-permute-done.4.left_ref
  27.1 0.5 %collective-permute-done.3.right_ref = f32[48,128]{1,0:T(8,128)S(1)} collective-permute-done((f32[48,128]{1,0:T(8,128)S(1)}, f32[48,128]{1,0:T(8,128)S(1)}, u32[]{:S(2)}, u32[]{:S(2)}) %collective-permute-start.3) | collective-permute-done | bytes 24608 | tf_op jit(solution)/shard_map/ppermute | solution.py:464
  27.6 3.4 %shard_map.31 = f32[7,32,128]{2,1,0:T(8,128)} custom-call(s32[128,128]{1,0:T(8,128)S(1)} %get-tuple-element.12.lev, s32[104,128]{1,0:T(8,128)S(1)} %get-tuple-element.13.lev_strips, s32[2,32,128]{2,1,0:T(8,128)S(1)} %get-tuple-element.14.corner, f32[7,32,128]{2,1,0:T(8,128)S(1)} %copy-done, f32[7,144,128]{2,1,0:T(8,128)S(1)} %shard_map.30.own_ref, ...), custom_call_target="tpu_custom_call" | custom-call | tf_op jit(solution)/shard_map/pallas_call | solution.py:523
Async XLA Ops:
  0.0 15.8 %collective-permute-start.2 = (f32[7,32,128]{2,1,0:T(8,128)}, f32[7,32,128]{2,1,0:T(8,128)S(1)}, u32[]{:S(2)}, u32[]{:S(2)}) collective-permute-start(f32[7,32,128]{2,1,0:T(8,128)} %fields_ref.3), channel_id=1, source_target_pairs={{0,12},{12,0},{1,13},{13,1},{2,14},{14,2},{3,15},{15,3},{4,16},{16... | collective-permute-start | bytes 344072 | tf_op jit(solution)/shard_map/ppermute | solution.py:470
  0.7 15.2 %collective-permute-start.1 = (f32[7,32,128]{2,1,0:T(8,128)}, f32[7,32,128]{2,1,0:T(8,128)S(1)}, u32[]{:S(2)}, u32[]{:S(2)}) collective-permute-start(f32[7,32,128]{2,1,0:T(8,128)} %fields_ref.3), channel_id=1, source_target_pairs={{12,24},{36,48},{60,72},{84,96},{108,120},{132,144},{156,168},{180... | collective-permute-start | bytes 344072 | tf_op jit(solution)/shard_map/ppermute | solution.py:470
  12.8 3.4 %collective-permute-start = (f32[7,32,128]{2,1,0:T(8,128)}, f32[7,32,128]{2,1,0:T(8,128)S(1)}, u32[]{:S(2)}, u32[]{:S(2)}) collective-permute-start(f32[7,32,128]{2,1,0:T(8,128)} %fields_ref.3), channel_id=1, source_target_pairs={{24,36},{48,60},{72,84},{96,108},{120,132},{144,156},{168,180},{19... | collective-permute-start | bytes 344072 | tf_op jit(solution)/shard_map/ppermute | solution.py:470
  16.2 10.4 %copy-start = (f32[7,32,128]{2,1,0:T(8,128)S(1)}, f32[7,32,128]{2,1,0:T(8,128)}, u32[]{:S(2)}) copy-start(f32[7,32,128]{2,1,0:T(8,128)} %fields_ref.3) | copy-start | bytes 344068
  16.3 10.7 %collective-permute-start.4 = (f32[48,128]{1,0:T(8,128)S(1)}, f32[48,128]{1,0:T(8,128)S(1)}, u32[]{:S(2)}, u32[]{:S(2)}) collective-permute-start(f32[48,128]{1,0:T(8,128)S(1)} %get-tuple-element.18), channel_id=1, source_target_pairs={{0,1},{1,2},{2,3},{3,4},{4,5},{5,6},{6,7},{7,8},{8,9},{9,10},{10,1... | collective-permute-start | bytes 73736 | tf_op jit(solution)/shard_map/ppermute | solution.py:464
  18.3 9.3 %collective-permute-start.3 = (f32[48,128]{1,0:T(8,128)S(1)}, f32[48,128]{1,0:T(8,128)S(1)}, u32[]{:S(2)}, u32[]{:S(2)}) collective-permute-start(f32[48,128]{1,0:T(8,128)S(1)} %get-tuple-element.18), channel_id=1, source_target_pairs={{0,11},{1,0},{2,1},{3,2},{4,3},{5,4},{6,5},{7,6},{8,7},{9,8},{10,9... | collective-permute-start | bytes 73736 | tf_op jit(solution)/shard_map/ppermute | solution.py:464

commit v8 on v7

--- a/solution.py
+++ b/solution.py
@@ -261,8 +261,9 @@
     corner,
     fields_ref,
     own_ref,
-    right_ref,
-    left_ref,
+    last_ref,
+    far_ref,
+    near_ref,
     out_ref,
     win,
     base,
@@ -285,7 +286,10 @@
     own_level = lev[8:16, :]
 
     p48 = lane(48)
-    strips = jnp.where((p48 & 15) < 8, left_ref[...], right_ref[...])
+    sub, count = lax.axis_index("sub"), lax.axis_size("sub")
+    even = jnp.full((48, COLS), lax.rem(sub, 2)) == 0
+    near = jnp.where(jnp.full((48, COLS), sub) >= count - 2, last_ref[...], near_ref[...])
+    strips = jnp.where(((p48 & 15) < 8) == even, far_ref[...], near)
     fine, medium, coarse = share_strips(strips, lev_strips, held)
     strip_one = ((p32 >= 64) & (p32 < 72)) | (p32 >= 120)
     strip_none = ((p32 >= 72) & (p32 < 80)) | ((p32 >= 112) & (p32 < 120))
@@ -358,12 +362,13 @@
             value = fluxx[n, TPAD + 1 : TPAD + 129, :] - fluxx[n, TPAD : TPAD + 128, :]
             diffx[i, PAD : PAD + 128, :] = value.T
 
-    def sweep_y():
+    def sweep_y(last):
         items = [(base, 0), (prim, 1), (prim, 0), (prim, 2), (prim, 4), (base, 4)]
         for row in chunks:
             flux = sweep(items, lefty, row, 16, (base, 6))
             for i, n in enumerate((0, 2, 1, 3, 5, 4)):
-                fluxy[i, row : row + 16, :] = flux[n]
+                if i == 5 or row < SIDE or not last:
+                    fluxy[i, row : row + 16, :] = flux[n]
 
     def beside_cols(parts, back):
         parts = [pltpu.roll(part, 1 if back else 127, 1) for part in parts]
@@ -397,14 +402,19 @@
             value = jnp.where((finest == 2) & ~coarse, halved_two, values[step])
             fixed[step, 0:32, :] = jnp.where((finest >= 1) & coarse, halved_one, value)
 
-    def update_cells(i):
+    def is_own(row):
+        return PAD + 8 <= row < PAD + 40 or MID + 8 <= row < MID + 24
+
+    def update_cells(i, last):
         for rows in row_sets:
             for k, row in enumerate(rows):
+                if last and not is_own(row):
+                    continue
                 part = slice(row, row + 8)
                 change = diffx[i, part, :] + (fluxy[i, row + 1 : row + 9, :] - fluxy[i, part, :])
                 win[i, part, :] = base[i, part, :] - 0.5 * ratios[k] * change
 
-    def update_faces():
+    def update_faces(last):
         for rows in row_sets:
             values = [edge[row : row + 8, :] for row in rows[:2]]
             above = [edge[row + 1 : row + 9, :] for row in rows[:2]]
@@ -415,6 +425,8 @@
                 above.append(fixed[0, first + 1 : first + 9, :])
                 others.append(fixed[1, first : first + 8, :])
             for row, ratio, value, up, other in zip(rows, ratios, values, above, others):
+                if last and not is_own(row):
+                    continue
                 part = slice(row, row + 8)
                 win[5, part, :] = base[5, part, :] - ratio * (up - value)
                 win[6, part, :] = base[6, part, :] + ratio * (other - value)
@@ -441,27 +453,24 @@
             pltpu.make_async_copy(result.at[f], out_ref.at[f], sems.at[f]).start()
 
     for section in range(2):
+        last = section == 1
         then = (shared, finish)[section]
         primitives()
+        sweep_y(last)
         sweep_x()
-        sweep_y()
         edges()
-        update_cells(0)
+        correct()
+        update_cells(0, last)
         then((0,))
-        correct()
-        for i in range(1, 5):
-            update_cells(i)
+        update_faces(last)
+        update_cells(1, last)
+        then((1,))
+        then((5, 6))
+        for i in range(2, 5):
+            update_cells(i, last)
             then((i,))
-            if i == 2:
-                update_faces()
-        then((5, 6))
     for f in range(7):
         pltpu.make_async_copy(result.at[f], out_ref.at[f], sems.at[f]).wait()
-
-
-def moved(value, axis, step):
-    size = lax.axis_size(axis)
-    return lax.ppermute(value, axis, [(i, (i + step) % size) for i in range(size)])
 
 
 def swapped_pairs(value, axis, first, stop):
@@ -503,8 +512,10 @@
         out_specs=(VMEM,) * 3,
         compiler_params=params,
     )(lev, cols, close, far, first)
-    right = moved(packed, "sub", -1)
-    left = moved(packed, "sub", 1)
+    count = lax.axis_size("sub")
+    end = swapped_pairs(packed, "sub", count - 2, count)
+    far = swapped_pairs(packed, "sub", 1, count)
+    near = swapped_pairs(packed, "sub", 0, count - 2)
     own = pl.pallas_call(
         rows_kernel,
         out_shape=shape((7, PAD + 136, COLS), F32),
@@ -523,7 +534,7 @@
     return pl.pallas_call(
         main_kernel,
         out_shape=shape(fields.shape, F32),
-        in_specs=[VMEM] * 7,
+        in_specs=[VMEM] * 8,
         out_specs=HBM,
         scratch_shapes=[
             window(7),
@@ -543,7 +554,7 @@
             pltpu.SemaphoreType.DMA((7,)),
         ],
         compiler_params=params,
-    )(lev, lev_strips, corner, fields, own, right, left)
+    )(lev, lev_strips, corner, fields, own, end, far, near)
 
 
 def solution(mesh):

time: 31.2 us -> 31.5 us (level)
  the two profiles are of different devices: /device:TPU:63 before, /device:TPU:64 now
where the time goes in v8:
time: 31.5 us; the launch traced here: 31.3 us
  starting transfers between devices  21.5 us (68%)
  waiting for transfers between devices  4.84 us (15%)
  Pallas kernels  4.82 us (15%)
    ppermute x6, starting transfers between devices, swapped_pairs(): return lax.ppermute(value, axis, pairs + [(j, i) for i, j in pairs])  21.5 us
    ppermute x6, waiting for transfers between devices, swapped_pairs(): return lax.ppermute(value, axis, pairs + [(j, i) for i, j in pairs])  4.84 us
    pallas_call x1, Pallas kernels, on_device(): pl.pallas_call(main_kernel, out_shape=shape(fields.shape, F32), in_specs=...  3.29 us
    pallas_call x1, Pallas kernels, on_device(): pl.pallas_call(own_kernel, out_shape=(shape((128, COLS), jnp.int32), shap...  1.05 us
  transfers between devices with their start and end apart: 6, of which 2 were waited for; matrix products, arithmetic and copies ran while one was open for 0% of the time, Pallas kernels for 5%

profile of v8, /device:TPU:64, one launch (start us, length us, event | category | flops | bytes accessed | tf_op | source)
XLA Modules:
  0.0 31.3 jit_solution(6584912518916124049)
XLA Ops:
  0.0 1.9 %collective-permute-start.2 = (f32[7,32,128]{2,1,0:T(8,128)}, f32[7,32,128]{2,1,0:T(8,128)S(1)}, u32[]{:S(2)}, u32[]{:S(2)}) collective-permute-start(f32[7,32,128]{2,1,0:T(8,128)} %fields_ref.3), channel_id=1, source_target_pairs={{0,12},{12,0},{1,13},{13,1},{2,14},{14,2},{3,15},{15,3},{4,16},{16... | collective-permute-start | bytes 344072 | tf_op jit(solution)/shard_map/ppermute | solution.py:479
  1.9 5.8 %collective-permute-start.1 = (f32[7,32,128]{2,1,0:T(8,128)}, f32[7,32,128]{2,1,0:T(8,128)S(1)}, u32[]{:S(2)}, u32[]{:S(2)}) collective-permute-start(f32[7,32,128]{2,1,0:T(8,128)} %fields_ref.3), channel_id=1, source_target_pairs={{12,24},{36,48},{60,72},{84,96},{108,120},{132,144},{156,168},{180... | collective-permute-start | bytes 344072 | tf_op jit(solution)/shard_map/ppermute | solution.py:479
  7.7 0.7 %collective-permute-start = (f32[7,32,128]{2,1,0:T(8,128)}, f32[7,32,128]{2,1,0:T(8,128)S(1)}, u32[]{:S(2)}, u32[]{:S(2)}) collective-permute-start(f32[7,32,128]{2,1,0:T(8,128)} %fields_ref.3), channel_id=1, source_target_pairs={{24,36},{48,60},{72,84},{96,108},{120,132},{144,156},{168,180},{19... | collective-permute-start | bytes 344072 | tf_op jit(solution)/shard_map/ppermute | solution.py:479
  8.4 1.1 %shard_map.28 = (s32[128,128]{1,0:T(8,128)S(1)}, s32[104,128]{1,0:T(8,128)S(1)}, s32[2,32,128]{2,1,0:T(8,128)S(1)}, f32[32,128]{1,0:T(8,128)S(1)}) custom-call(s32[12,64]{1,0:T(8,128)} %bitcast.1, f32[7,32,128]{2,1,0:T(8,128)} %fields_ref.3), custom_call_target="tpu_custom_call" | custom-call | tf_op jit(solution)/shard_map/pallas_call | solution.py:489
  9.4 0.0 collective-permute-done.2.first_ref
  9.4 2.1 %collective-permute-done.1.far_ref = f32[7,32,128]{2,1,0:T(8,128)S(1)} collective-permute-done((f32[7,32,128]{2,1,0:T(8,128)}, f32[7,32,128]{2,1,0:T(8,128)S(1)}, u32[]{:S(2)}, u32[]{:S(2)}) %collective-permute-start.1) | collective-permute-done | bytes 114720 | tf_op jit(solution)/shard_map/ppermute | solution.py:479
  11.6 0.0 collective-permute-done.close_ref
  11.6 0.0 copy-start
  11.6 0.1 shard_map.29
  11.7 10.6 %collective-permute-start.5 = (f32[48,128]{1,0:T(8,128)S(1)}, f32[48,128]{1,0:T(8,128)S(1)}, u32[]{:S(2)}, u32[]{:S(2)}) collective-permute-start(f32[48,128]{1,0:T(8,128)S(1)} %get-tuple-element.18), channel_id=1, source_target_pairs={{0,1},{2,3},{4,5},{6,7},{8,9},{1,0},{3,2},{5,4},{7,6},{9,8},{12,13... | collective-permute-start | bytes 73736 | tf_op jit(solution)/shard_map/ppermute | solution.py:479
  22.2 1.9 %collective-permute-start.4 = (f32[48,128]{1,0:T(8,128)S(1)}, f32[48,128]{1,0:T(8,128)S(1)}, u32[]{:S(2)}, u32[]{:S(2)}) collective-permute-start(f32[48,128]{1,0:T(8,128)S(1)} %get-tuple-element.18), channel_id=1, source_target_pairs={{1,2},{3,4},{5,6},{7,8},{9,10},{11,0},{2,1},{4,3},{6,5},{8,7},{10,... | collective-permute-start | bytes 73736 | tf_op jit(solution)/shard_map/ppermute | solution.py:479
  24.2 0.7 %collective-permute-start.3 = (f32[48,128]{1,0:T(8,128)S(1)}, f32[48,128]{1,0:T(8,128)S(1)}, u32[]{:S(2)}, u32[]{:S(2)}) collective-permute-start(f32[48,128]{1,0:T(8,128)S(1)} %get-tuple-element.18), channel_id=1, source_target_pairs={{10,11},{11,10},{22,23},{23,22},{34,35},{35,34},{46,47},{47,46},{5... | collective-permute-start | bytes 73736 | tf_op jit(solution)/shard_map/ppermute | solution.py:479
  24.8 0.0 copy-done
  24.8 0.4 %shard_map.30.own_ref = f32[7,144,128]{2,1,0:T(8,128)S(1)} custom-call(s32[128,128]{1,0:T(8,128)S(1)} %get-tuple-element.12.lev, f32[7,32,128]{2,1,0:T(8,128)S(1)} %copy-done, f32[7,8,128]{2,1,0:T(8,128)S(1)} %get-tuple-element.16.below_ref, f32[7,8,128]{2,1,0:T(8,128)S(1)} %get-tuple-element.17.above_ref), custom_call_target="tpu_custom_call" | custom-call | tf_op jit(solution)/shard_map/pallas_call | solution.py:519
  25.2 0.0 collective-permute-done.5.near_ref
  25.3 2.7 %collective-permute-done.4.far_ref = f32[48,128]{1,0:T(8,128)S(1)} collective-permute-done((f32[48,128]{1,0:T(8,128)S(1)}, f32[48,128]{1,0:T(8,128)S(1)}, u32[]{:S(2)}, u32[]{:S(2)}) %collective-permute-start.4) | collective-permute-done | bytes 24608 | tf_op jit(solution)/shard_map/ppermute | solution.py:479
  28.0 0.0 collective-permute-done.3.last_ref
  28.0 3.3 %shard_map.31 = f32[7,32,128]{2,1,0:T(8,128)} custom-call(s32[128,128]{1,0:T(8,128)S(1)} %get-tuple-element.12.lev, s32[104,128]{1,0:T(8,128)S(1)} %get-tuple-element.13.lev_strips, s32[2,32,128]{2,1,0:T(8,128)S(1)} %get-tuple-element.14.corner, f32[7,32,128]{2,1,0:T(8,128)S(1)} %copy-done, f32[7,144,128]{2,1,0:T(8,128)S(1)} %shard_map.30.own_ref, ...), custom_call_target="tpu_custom_call" | custom-call | tf_op jit(solution)/shard_map/pallas_call | solution.py:534
Async XLA Ops:
  0.0 9.4 %collective-permute-start.2 = (f32[7,32,128]{2,1,0:T(8,128)}, f32[7,32,128]{2,1,0:T(8,128)S(1)}, u32[]{:S(2)}, u32[]{:S(2)}) collective-permute-start(f32[7,32,128]{2,1,0:T(8,128)} %fields_ref.3), channel_id=1, source_target_pairs={{0,12},{12,0},{1,13},{13,1},{2,14},{14,2},{3,15},{15,3},{4,16},{16... | collective-permute-start | bytes 344072 | tf_op jit(solution)/shard_map/ppermute | solution.py:479
  1.9 9.6 %collective-permute-start.1 = (f32[7,32,128]{2,1,0:T(8,128)}, f32[7,32,128]{2,1,0:T(8,128)S(1)}, u32[]{:S(2)}, u32[]{:S(2)}) collective-permute-start(f32[7,32,128]{2,1,0:T(8,128)} %fields_ref.3), channel_id=1, source_target_pairs={{12,24},{36,48},{60,72},{84,96},{108,120},{132,144},{156,168},{180... | collective-permute-start | bytes 344072 | tf_op jit(solution)/shard_map/ppermute | solution.py:479
  7.7 3.9 %collective-permute-start = (f32[7,32,128]{2,1,0:T(8,128)}, f32[7,32,128]{2,1,0:T(8,128)S(1)}, u32[]{:S(2)}, u32[]{:S(2)}) collective-permute-start(f32[7,32,128]{2,1,0:T(8,128)} %fields_ref.3), channel_id=1, source_target_pairs={{24,36},{48,60},{72,84},{96,108},{120,132},{144,156},{168,180},{19... | collective-permute-start | bytes 344072 | tf_op jit(solution)/shard_map/ppermute | solution.py:479
  11.6 13.3 %copy-start = (f32[7,32,128]{2,1,0:T(8,128)S(1)}, f32[7,32,128]{2,1,0:T(8,128)}, u32[]{:S(2)}) copy-start(f32[7,32,128]{2,1,0:T(8,128)} %fields_ref.3) | copy-start | bytes 344068
  11.7 13.6 %collective-permute-start.5 = (f32[48,128]{1,0:T(8,128)S(1)}, f32[48,128]{1,0:T(8,128)S(1)}, u32[]{:S(2)}, u32[]{:S(2)}) collective-permute-start(f32[48,128]{1,0:T(8,128)S(1)} %get-tuple-element.18), channel_id=1, source_target_pairs={{0,1},{2,3},{4,5},{6,7},{8,9},{1,0},{3,2},{5,4},{7,6},{9,8},{12,13... | collective-permute-start | bytes 73736 | tf_op jit(solution)/shard_map/ppermute | solution.py:479
  22.2 5.7 %collective-permute-start.4 = (f32[48,128]{1,0:T(8,128)S(1)}, f32[48,128]{1,0:T(8,128)S(1)}, u32[]{:S(2)}, u32[]{:S(2)}) collective-permute-start(f32[48,128]{1,0:T(8,128)S(1)} %get-tuple-element.18), channel_id=1, source_target_pairs={{1,2},{3,4},{5,6},{7,8},{9,10},{11,0},{2,1},{4,3},{6,5},{8,7},{10,... | collective-permute-start | bytes 73736 | tf_op jit(solution)/shard_map/ppermute | solution.py:479
  24.2 3.8 %collective-permute-start.3 = (f32[48,128]{1,0:T(8,128)S(1)}, f32[48,128]{1,0:T(8,128)S(1)}, u32[]{:S(2)}, u32[]{:S(2)}) collective-permute-start(f32[48,128]{1,0:T(8,128)S(1)} %get-tuple-element.18), channel_id=1, source_target_pairs={{10,11},{11,10},{22,23},{23,22},{34,35},{35,34},{46,47},{47,46},{5... | collective-permute-start | bytes 73736 | tf_op jit(solution)/shard_map/ppermute | solution.py:479

commit v9 on v8

--- a/solution.py
+++ b/solution.py
@@ -61,7 +61,20 @@
     return packed
 
 
-def own_kernel(levels_hbm, fields_hbm, lev, lev_strips, corner, cols_ref, levels_ref, fields_ref, held, sems):
+def own_kernel(
+    levels_hbm,
+    fields_hbm,
+    lev,
+    lev_strips,
+    corner,
+    cols_ref,
+    far_ref,
+    close_ref,
+    levels_ref,
+    fields_ref,
+    held,
+    sems,
+):
     copies = [
         pltpu.make_async_copy(levels_hbm, levels_ref, sems.at[0]),
         pltpu.make_async_copy(fields_hbm, fields_ref, sems.at[1]),
@@ -99,6 +112,11 @@
     corner[1] = pltpu.roll(corner[0], 127, 1)
     own = lev[8:16, :]
     copies[1].wait()
+    even = jnp.full((8, COLS), lax.rem(lax.axis_index("seg"), 2)) == 0
+    for f in range(7):
+        first, last = fields_ref[f, 0:8, :], last_rows(fields_ref, f, own)
+        far_ref[f] = jnp.where(even, first, last)
+        close_ref[f] = jnp.where(even, last, first)
     for r in range(0, 32, 8):
         cols_ref[r : r + 8, :] = packed_cols(lambda f: fields_ref[f, r : r + 8, :], own)
 
@@ -109,10 +127,9 @@
     early = jnp.full((8, COLS), seg) < 2
     below_level, above_level = lev[0:8, :], lev[40:48, :]
     for f in range(7):
-        far, close, first = (last_rows(r, f, below_level) for r in (far_ref, close_ref, first_ref))
-        below_ref[f] = jnp.where(even, far, jnp.where(early, first, close))
-        close = jnp.where(early, first_ref[f, 0:8, :], close_ref[f, 0:8, :])
-        above_ref[f] = jnp.where(even, close, far_ref[f, 0:8, :])
+        close = jnp.where(early, first_ref[f], close_ref[f])
+        below_ref[f] = jnp.where(even, far_ref[f], close)
+        above_ref[f] = jnp.where(even, close, far_ref[f])
     out_ref[0:8, :] = packed_cols(lambda f: below_ref[f], below_level)
     out_ref[8:40, :] = cols_ref[...]
     out_ref[40:48, :] = packed_cols(lambda f: above_ref[f], above_level)
@@ -482,20 +499,19 @@
 def on_device(fields, region_levels):
     shape = jax.ShapeDtypeStruct
     params = pltpu.CompilerParams(vmem_limit_bytes=32 * 1024 * 1024)
-    size = lax.axis_size("seg")
-    close = swapped_pairs(fields, "seg", 2, size)
-    far = swapped_pairs(fields, "seg", 1, size)
-    first = swapped_pairs(fields, "seg", 0, 2)
-    lev, lev_strips, corner, cols = pl.pallas_call(
+    rows = shape((7, 8, COLS), F32)
+    lev, lev_strips, corner, cols, to_far, to_close = pl.pallas_call(
         own_kernel,
         out_shape=(
             shape((128, COLS), jnp.int32),
             shape((104, COLS), jnp.int32),
             shape((2, 32, COLS), jnp.int32),
             shape((32, COLS), F32),
+            rows,
+            rows,
         ),
         in_specs=[HBM] * 2,
-        out_specs=(VMEM,) * 4,
+        out_specs=(VMEM,) * 6,
         scratch_shapes=[
             pltpu.VMEM(region_levels.shape[::-1], jnp.int32),
             pltpu.VMEM(fields.shape, F32),
@@ -504,7 +520,10 @@
         ],
         compiler_params=params,
     )(*(pltpu.with_memory_space_constraint(x, pltpu.HBM) for x in (region_levels.T, fields)))
-    rows = shape((7, 8, COLS), F32)
+    size = lax.axis_size("seg")
+    close = swapped_pairs(to_close, "seg", 2, size)
+    far = swapped_pairs(to_far, "seg", 1, size)
+    first = swapped_pairs(to_close, "seg", 0, 2)
     packed, below, above = pl.pallas_call(
         cols_kernel,
         out_shape=(shape((48, COLS), F32), rows, rows),

time: 31.5 us -> 32.3 us (1.025)
  the two profiles are of different devices: /device:TPU:64 before, /device:TPU:1 now
where the time goes in v9:
time: 32.3 us; the launch traced here: 32 us
  starting transfers between devices  26.9 us (83%)
  Pallas kernels  4.82 us (15%)
    ppermute x6, starting transfers between devices, swapped_pairs(): return lax.ppermute(value, axis, pairs + [(j, i) for i, j in pairs])  26.9 us
    pallas_call x1, Pallas kernels, on_device(): pl.pallas_call(main_kernel, out_shape=shape(fields.shape, F32), in_specs=...  3.29 us
    pallas_call x1, Pallas kernels, on_device(): pl.pallas_call(own_kernel, out_shape=(shape((128, COLS), jnp.int32), shap...  1.05 us
  transfers between devices with their start and end apart: 6, of which 2 were waited for; matrix products, arithmetic and copies ran while one was open for 0% of the time, Pallas kernels for 1%

profile of v9, /device:TPU:1, one launch (start us, length us, event | category | flops | bytes accessed | tf_op | source)
XLA Modules:
  0.0 32.0 jit_solution(12176865264755593074)
XLA Ops:
  0.0 1.0 %shard_map.28 = (s32[128,128]{1,0:T(8,128)S(1)}, s32[104,128]{1,0:T(8,128)S(1)}, s32[2,32,128]{2,1,0:T(8,128)S(1)}, f32[32,128]{1,0:T(8,128)S(1)}, f32[7,8,128]{2,1,0:T(8,128)S(1)}, /*index=5*/f32[7,8,128]{2,1,0:T(8,128)S(1)}) custom-call(s32[12,64]{1,0:T(8,128)} %bitcast.1, f32[7,32,128]{2,1,0:T(8,128)} %fields_ref.3), custom_call_target="tpu_custom_call" | custom-call | tf_op jit(solution)/shard_map/pallas_call | solution.py:503
  1.1 0.0 copy-start
  1.1 4.7 %collective-permute-start.1 = (f32[7,8,128]{2,1,0:T(8,128)S(1)}, f32[7,8,128]{2,1,0:T(8,128)S(1)}, u32[]{:S(2)}, u32[]{:S(2)}) collective-permute-start(f32[7,8,128]{2,1,0:T(8,128)S(1)} %get-tuple-element.19), channel_id=1, source_target_pairs={{12,24},{36,48},{60,72},{84,96},{108,120},{132,144},{156,168},{180... | collective-permute-start | bytes 86024 | tf_op jit(solution)/shard_map/ppermute | solution.py:496
  5.8 9.8 %collective-permute-start.2 = (f32[7,8,128]{2,1,0:T(8,128)S(1)}, f32[7,8,128]{2,1,0:T(8,128)S(1)}, u32[]{:S(2)}, u32[]{:S(2)}) collective-permute-start(f32[7,8,128]{2,1,0:T(8,128)S(1)} %get-tuple-element.18), channel_id=1, source_target_pairs={{0,12},{12,0},{1,13},{13,1},{2,14},{14,2},{3,15},{15,3},{4,16},{16... | collective-permute-start | bytes 86024 | tf_op jit(solution)/shard_map/ppermute | solution.py:496
  15.6 0.7 %collective-permute-start = (f32[7,8,128]{2,1,0:T(8,128)S(1)}, f32[7,8,128]{2,1,0:T(8,128)S(1)}, u32[]{:S(2)}, u32[]{:S(2)}) collective-permute-start(f32[7,8,128]{2,1,0:T(8,128)S(1)} %get-tuple-element.18), channel_id=1, source_target_pairs={{24,36},{48,60},{72,84},{96,108},{120,132},{144,156},{168,180},{19... | collective-permute-start | bytes 86024 | tf_op jit(solution)/shard_map/ppermute | solution.py:496
  16.2 0.0 collective-permute-done.1.far_ref
  16.2 0.2 collective-permute-done.2.first_ref
  16.4 0.0 collective-permute-done.close_ref
  16.4 0.1 shard_map.29
  16.5 1.9 %collective-permute-start.5 = (f32[48,128]{1,0:T(8,128)S(1)}, f32[48,128]{1,0:T(8,128)S(1)}, u32[]{:S(2)}, u32[]{:S(2)}) collective-permute-start(f32[48,128]{1,0:T(8,128)S(1)} %get-tuple-element.22), channel_id=1, source_target_pairs={{0,1},{2,3},{4,5},{6,7},{8,9},{1,0},{3,2},{5,4},{7,6},{9,8},{12,13... | collective-permute-start | bytes 73736 | tf_op jit(solution)/shard_map/ppermute | solution.py:496
  18.4 9.1 %collective-permute-start.4 = (f32[48,128]{1,0:T(8,128)S(1)}, f32[48,128]{1,0:T(8,128)S(1)}, u32[]{:S(2)}, u32[]{:S(2)}) collective-permute-start(f32[48,128]{1,0:T(8,128)S(1)} %get-tuple-element.22), channel_id=1, source_target_pairs={{1,2},{3,4},{5,6},{7,8},{9,10},{11,0},{2,1},{4,3},{6,5},{8,7},{10,... | collective-permute-start | bytes 73736 | tf_op jit(solution)/shard_map/ppermute | solution.py:496
  27.5 0.7 %collective-permute-start.3 = (f32[48,128]{1,0:T(8,128)S(1)}, f32[48,128]{1,0:T(8,128)S(1)}, u32[]{:S(2)}, u32[]{:S(2)}) collective-permute-start(f32[48,128]{1,0:T(8,128)S(1)} %get-tuple-element.22), channel_id=1, source_target_pairs={{10,11},{11,10},{22,23},{23,22},{34,35},{35,34},{46,47},{47,46},{5... | collective-permute-start | bytes 73736 | tf_op jit(solution)/shard_map/ppermute | solution.py:496
  28.2 0.0 copy-done
  28.2 0.4 %shard_map.30.own_ref = f32[7,144,128]{2,1,0:T(8,128)S(1)} custom-call(s32[128,128]{1,0:T(8,128)S(1)} %get-tuple-element.14.lev, f32[7,32,128]{2,1,0:T(8,128)S(1)} %copy-done, f32[7,8,128]{2,1,0:T(8,128)S(1)} %get-tuple-element.20.below_ref, f32[7,8,128]{2,1,0:T(8,128)S(1)} %get-tuple-element.21.above_ref), custom_call_target="tpu_custom_call" | custom-call | tf_op jit(solution)/shard_map/pallas_call | solution.py:538
  28.6 0.0 collective-permute-done.5.near_ref
  28.6 0.1 collective-permute-done.4.far_ref
  28.7 0.0 collective-permute-done.3.last_ref
  28.8 3.3 %shard_map.31 = f32[7,32,128]{2,1,0:T(8,128)} custom-call(s32[128,128]{1,0:T(8,128)S(1)} %get-tuple-element.14.lev, s32[104,128]{1,0:T(8,128)S(1)} %get-tuple-element.15.lev_strips, s32[2,32,128]{2,1,0:T(8,128)S(1)} %get-tuple-element.16.corner, f32[7,32,128]{2,1,0:T(8,128)S(1)} %copy-done, f32[7,144,128]{2,1,0:T(8,128)S(1)} %shard_map.30.own_ref, ...), custom_call_target="tpu_custom_call" | custom-call | tf_op jit(solution)/shard_map/pallas_call | solution.py:553
Async XLA Ops:
  1.1 27.2 %copy-start = (f32[7,32,128]{2,1,0:T(8,128)S(1)}, f32[7,32,128]{2,1,0:T(8,128)}, u32[]{:S(2)}) copy-start(f32[7,32,128]{2,1,0:T(8,128)} %fields_ref.3) | copy-start | bytes 344068
  1.1 15.2 %collective-permute-start.1 = (f32[7,8,128]{2,1,0:T(8,128)S(1)}, f32[7,8,128]{2,1,0:T(8,128)S(1)}, u32[]{:S(2)}, u32[]{:S(2)}) collective-permute-start(f32[7,8,128]{2,1,0:T(8,128)S(1)} %get-tuple-element.19), channel_id=1, source_target_pairs={{12,24},{36,48},{60,72},{84,96},{108,120},{132,144},{156,168},{180... | collective-permute-start | bytes 86024 | tf_op jit(solution)/shard_map/ppermute | solution.py:496
  5.8 10.6 %collective-permute-start.2 = (f32[7,8,128]{2,1,0:T(8,128)S(1)}, f32[7,8,128]{2,1,0:T(8,128)S(1)}, u32[]{:S(2)}, u32[]{:S(2)}) collective-permute-start(f32[7,8,128]{2,1,0:T(8,128)S(1)} %get-tuple-element.18), channel_id=1, source_target_pairs={{0,12},{12,0},{1,13},{13,1},{2,14},{14,2},{3,15},{15,3},{4,16},{16... | collective-permute-start | bytes 86024 | tf_op jit(solution)/shard_map/ppermute | solution.py:496
  15.6 0.8 %collective-permute-start = (f32[7,8,128]{2,1,0:T(8,128)S(1)}, f32[7,8,128]{2,1,0:T(8,128)S(1)}, u32[]{:S(2)}, u32[]{:S(2)}) collective-permute-start(f32[7,8,128]{2,1,0:T(8,128)S(1)} %get-tuple-element.18), channel_id=1, source_target_pairs={{24,36},{48,60},{72,84},{96,108},{120,132},{144,156},{168,180},{19... | collective-permute-start | bytes 86024 | tf_op jit(solution)/shard_map/ppermute | solution.py:496
  16.5 12.1 %collective-permute-start.5 = (f32[48,128]{1,0:T(8,128)S(1)}, f32[48,128]{1,0:T(8,128)S(1)}, u32[]{:S(2)}, u32[]{:S(2)}) collective-permute-start(f32[48,128]{1,0:T(8,128)S(1)} %get-tuple-element.22), channel_id=1, source_target_pairs={{0,1},{2,3},{4,5},{6,7},{8,9},{1,0},{3,2},{5,4},{7,6},{9,8},{12,13... | collective-permute-start | bytes 73736 | tf_op jit(solution)/shard_map/ppermute | solution.py:496
  18.4 10.3 %collective-permute-start.4 = (f32[48,128]{1,0:T(8,128)S(1)}, f32[48,128]{1,0:T(8,128)S(1)}, u32[]{:S(2)}, u32[]{:S(2)}) collective-permute-start(f32[48,128]{1,0:T(8,128)S(1)} %get-tuple-element.22), channel_id=1, source_target_pairs={{1,2},{3,4},{5,6},{7,8},{9,10},{11,0},{2,1},{4,3},{6,5},{8,7},{10,... | collective-permute-start | bytes 73736 | tf_op jit(solution)/shard_map/ppermute | solution.py:496
  27.5 1.2 %collective-permute-start.3 = (f32[48,128]{1,0:T(8,128)S(1)}, f32[48,128]{1,0:T(8,128)S(1)}, u32[]{:S(2)}, u32[]{:S(2)}) collective-permute-start(f32[48,128]{1,0:T(8,128)S(1)} %get-tuple-element.22), channel_id=1, source_target_pairs={{10,11},{11,10},{22,23},{23,22},{34,35},{35,34},{46,47},{47,46},{5... | collective-permute-start | bytes 73736 | tf_op jit(solution)/shard_map/ppermute | solution.py:496

commit v10 on v8

--- a/solution.py
+++ b/solution.py
@@ -287,8 +287,11 @@
 
     p48 = lane(48)
     sub, count = lax.axis_index("sub"), lax.axis_size("sub")
-    even = jnp.full((48, COLS), lax.rem(sub, 2)) == 0
-    near = jnp.where(jnp.full((48, COLS), sub) >= count - 2, last_ref[...], near_ref[...])
+    first_row = lax.axis_index("seg") == 0
+    sub = jnp.full((48, COLS), sub)
+    even = jnp.where(first_row, 1 - (sub & 1), sub & 1) == 0
+    third = jnp.where(first_row, jnp.where(sub == 0, count - 1, sub), sub + 1) >= count - 1
+    near = jnp.where(third, last_ref[...], near_ref[...])
     strips = jnp.where(((p48 & 15) < 8) == even, far_ref[...], near)
     fine, medium, coarse = share_strips(strips, lev_strips, held)
     strip_one = ((p32 >= 64) & (p32 < 72)) | (p32 >= 120)
@@ -477,6 +480,19 @@
     size = lax.axis_size(axis)
     pairs = [(i, (i + 1) % size) for i in range(first, stop, 2)]
     return lax.ppermute(value, axis, pairs + [(j, i) for i, j in pairs])
+
+
+def swapped_subs(value, turn):
+    rows, count = lax.axis_size("seg"), lax.axis_size("sub")
+    pairs = []
+    for s in range(rows):
+        first, stop = ((0, count - 2), (1, count), (count - 2, count))[turn]
+        if s == 0:
+            first, stop = ((1, count - 1), (0, count), (count - 1, count))[turn]
+        for u in range(first, stop, 2):
+            a, b = s * count + u, s * count + (u + 1) % count
+            pairs += [(a, b), (b, a)]
+    return lax.ppermute(value, ("seg", "sub"), pairs)
 
 
 def on_device(fields, region_levels):
@@ -512,10 +528,7 @@
         out_specs=(VMEM,) * 3,
         compiler_params=params,
     )(lev, cols, close, far, first)
-    count = lax.axis_size("sub")
-    end = swapped_pairs(packed, "sub", count - 2, count)
-    far = swapped_pairs(packed, "sub", 1, count)
-    near = swapped_pairs(packed, "sub", 0, count - 2)
+    end, far, near = (swapped_subs(packed, turn) for turn in (2, 1, 0))
     own = pl.pallas_call(
         rows_kernel,
         out_shape=shape((7, PAD + 136, COLS), F32),

time: 31.5 us -> 30.1 us (0.956)
  the two profiles are of different devices: /device:TPU:64 before, /device:TPU:1 now
where the time goes in v10:
time: 30.1 us; the launch traced here: 29.8 us
  starting transfers between devices  21.6 us (72%)
  Pallas kernels  4.82 us (16%)
  waiting for transfers between devices  3.3 us (11%)
    ppermute x3, starting transfers between devices, swapped_pairs(): return lax.ppermute(value, axis, pairs + [(j, i) for i, j in pairs])  15 us
    ppermute x3, starting transfers between devices, swapped_subs(): return lax.ppermute(value, ('seg', 'sub'), pairs)  6.62 us
    pallas_call x1, Pallas kernels, on_device(): pl.pallas_call(main_kernel, out_shape=shape(fields.shape, F32), in_specs=...  3.29 us
    ppermute x3, waiting for transfers between devices, swapped_pairs(): return lax.ppermute(value, axis, pairs + [(j, i) for i, j in pairs])  2.65 us
    pallas_call x1, Pallas kernels, on_device(): pl.pallas_call(own_kernel, out_shape=(shape((128, COLS), jnp.int32), shap...  1.05 us
    ppermute x3, waiting for transfers between devices, swapped_subs(): return lax.ppermute(value, ('seg', 'sub'), pairs)  0.65 us
  transfers between devices with their start and end apart: 6, of which 2 were waited for; matrix products, arithmetic and copies ran while one was open for 0% of the time, Pallas kernels for 5%

profile of v10, /device:TPU:1, one launch (start us, length us, event | category | flops | bytes accessed | tf_op | source)
XLA Modules:
  0.0 29.8 jit_solution(877011129406694085)
XLA Ops:
  0.0 12.4 %collective-permute-start.2 = (f32[7,32,128]{2,1,0:T(8,128)}, f32[7,32,128]{2,1,0:T(8,128)S(1)}, u32[]{:S(2)}, u32[]{:S(2)}) collective-permute-start(f32[7,32,128]{2,1,0:T(8,128)} %fields_ref.3), channel_id=1, source_target_pairs={{0,12},{12,0},{1,13},{13,1},{2,14},{14,2},{3,15},{15,3},{4,16},{16... | collective-permute-start | bytes 344072 | tf_op jit(solution)/shard_map/ppermute | solution.py:482
  12.4 1.9 %collective-permute-start.1 = (f32[7,32,128]{2,1,0:T(8,128)}, f32[7,32,128]{2,1,0:T(8,128)S(1)}, u32[]{:S(2)}, u32[]{:S(2)}) collective-permute-start(f32[7,32,128]{2,1,0:T(8,128)} %fields_ref.3), channel_id=1, source_target_pairs={{12,24},{36,48},{60,72},{84,96},{108,120},{132,144},{156,168},{180... | collective-permute-start | bytes 344072 | tf_op jit(solution)/shard_map/ppermute | solution.py:482
  14.4 0.7 %collective-permute-start = (f32[7,32,128]{2,1,0:T(8,128)}, f32[7,32,128]{2,1,0:T(8,128)S(1)}, u32[]{:S(2)}, u32[]{:S(2)}) collective-permute-start(f32[7,32,128]{2,1,0:T(8,128)} %fields_ref.3), channel_id=1, source_target_pairs={{24,36},{48,60},{72,84},{96,108},{120,132},{144,156},{168,180},{19... | collective-permute-start | bytes 344072 | tf_op jit(solution)/shard_map/ppermute | solution.py:482
  15.0 1.1 %shard_map.28 = (s32[128,128]{1,0:T(8,128)S(1)}, s32[104,128]{1,0:T(8,128)S(1)}, s32[2,32,128]{2,1,0:T(8,128)S(1)}, f32[32,128]{1,0:T(8,128)S(1)}) custom-call(s32[12,64]{1,0:T(8,128)} %bitcast.1, f32[7,32,128]{2,1,0:T(8,128)} %fields_ref.3), custom_call_target="tpu_custom_call" | custom-call | tf_op jit(solution)/shard_map/pallas_call | solution.py:505
  16.1 0.0 collective-permute-done.2.first_ref
  16.1 2.6 %collective-permute-done.1.far_ref = f32[7,32,128]{2,1,0:T(8,128)S(1)} collective-permute-done((f32[7,32,128]{2,1,0:T(8,128)}, f32[7,32,128]{2,1,0:T(8,128)S(1)}, u32[]{:S(2)}, u32[]{:S(2)}) %collective-permute-start.1) | collective-permute-done | bytes 114720 | tf_op jit(solution)/shard_map/ppermute | solution.py:482
  18.7 0.0 collective-permute-done.close_ref
  18.8 0.0 copy-start
  18.8 0.1 shard_map.29
  18.8 1.9 %collective-permute-start.5 = (f32[48,128]{1,0:T(8,128)S(1)}, f32[48,128]{1,0:T(8,128)S(1)}, u32[]{:S(2)}, u32[]{:S(2)}) collective-permute-start(f32[48,128]{1,0:T(8,128)S(1)} %get-tuple-element.18), channel_id=1, source_target_pairs={{1,2},{2,1},{3,4},{4,3},{5,6},{6,5},{7,8},{8,7},{9,10},{10,9},{12,... | collective-permute-start | bytes 73736 | tf_op jit(solution)/shard_map/ppermute | solution.py:495
  20.8 4.0 %collective-permute-start.4 = (f32[48,128]{1,0:T(8,128)S(1)}, f32[48,128]{1,0:T(8,128)S(1)}, u32[]{:S(2)}, u32[]{:S(2)}) collective-permute-start(f32[48,128]{1,0:T(8,128)S(1)} %get-tuple-element.18), channel_id=1, source_target_pairs={{0,1},{1,0},{2,3},{3,2},{4,5},{5,4},{6,7},{7,6},{8,9},{9,8},{10,11... | collective-permute-start | bytes 73736 | tf_op jit(solution)/shard_map/ppermute | solution.py:495
  24.8 0.7 %collective-permute-start.3 = (f32[48,128]{1,0:T(8,128)S(1)}, f32[48,128]{1,0:T(8,128)S(1)}, u32[]{:S(2)}, u32[]{:S(2)}) collective-permute-start(f32[48,128]{1,0:T(8,128)S(1)} %get-tuple-element.18), channel_id=1, source_target_pairs={{11,0},{0,11},{22,23},{23,22},{34,35},{35,34},{46,47},{47,46},{58,... | collective-permute-start | bytes 73736 | tf_op jit(solution)/shard_map/ppermute | solution.py:495
  25.5 0.0 copy-done
  25.5 0.4 %shard_map.30.own_ref = f32[7,144,128]{2,1,0:T(8,128)S(1)} custom-call(s32[128,128]{1,0:T(8,128)S(1)} %get-tuple-element.12.lev, f32[7,32,128]{2,1,0:T(8,128)S(1)} %copy-done, f32[7,8,128]{2,1,0:T(8,128)S(1)} %get-tuple-element.16.below_ref, f32[7,8,128]{2,1,0:T(8,128)S(1)} %get-tuple-element.17.above_ref), custom_call_target="tpu_custom_call" | custom-call | tf_op jit(solution)/shard_map/pallas_call | solution.py:532
  25.9 0.0 collective-permute-done.5.near_ref
  25.9 0.6 %collective-permute-done.4.far_ref = f32[48,128]{1,0:T(8,128)S(1)} collective-permute-done((f32[48,128]{1,0:T(8,128)S(1)}, f32[48,128]{1,0:T(8,128)S(1)}, u32[]{:S(2)}, u32[]{:S(2)}) %collective-permute-start.4) | collective-permute-done | bytes 24608 | tf_op jit(solution)/shard_map/ppermute | solution.py:495
  26.6 0.0 collective-permute-done.3.last_ref
  26.6 3.3 %shard_map.31 = f32[7,32,128]{2,1,0:T(8,128)} custom-call(s32[128,128]{1,0:T(8,128)S(1)} %get-tuple-element.12.lev, s32[104,128]{1,0:T(8,128)S(1)} %get-tuple-element.13.lev_strips, s32[2,32,128]{2,1,0:T(8,128)S(1)} %get-tuple-element.14.corner, f32[7,32,128]{2,1,0:T(8,128)S(1)} %copy-done, f32[7,144,128]{2,1,0:T(8,128)S(1)} %shard_map.30.own_ref, ...), custom_call_target="tpu_custom_call" | custom-call | tf_op jit(solution)/shard_map/pallas_call | solution.py:547
Async XLA Ops:
  0.0 16.1 %collective-permute-start.2 = (f32[7,32,128]{2,1,0:T(8,128)}, f32[7,32,128]{2,1,0:T(8,128)S(1)}, u32[]{:S(2)}, u32[]{:S(2)}) collective-permute-start(f32[7,32,128]{2,1,0:T(8,128)} %fields_ref.3), channel_id=1, source_target_pairs={{0,12},{12,0},{1,13},{13,1},{2,14},{14,2},{3,15},{15,3},{4,16},{16... | collective-permute-start | bytes 344072 | tf_op jit(solution)/shard_map/ppermute | solution.py:482
  12.4 6.3 %collective-permute-start.1 = (f32[7,32,128]{2,1,0:T(8,128)}, f32[7,32,128]{2,1,0:T(8,128)S(1)}, u32[]{:S(2)}, u32[]{:S(2)}) collective-permute-start(f32[7,32,128]{2,1,0:T(8,128)} %fields_ref.3), channel_id=1, source_target_pairs={{12,24},{36,48},{60,72},{84,96},{108,120},{132,144},{156,168},{180... | collective-permute-start | bytes 344072 | tf_op jit(solution)/shard_map/ppermute | solution.py:482
  14.4 4.4 %collective-permute-start = (f32[7,32,128]{2,1,0:T(8,128)}, f32[7,32,128]{2,1,0:T(8,128)S(1)}, u32[]{:S(2)}, u32[]{:S(2)}) collective-permute-start(f32[7,32,128]{2,1,0:T(8,128)} %fields_ref.3), channel_id=1, source_target_pairs={{24,36},{48,60},{72,84},{96,108},{120,132},{144,156},{168,180},{19... | collective-permute-start | bytes 344072 | tf_op jit(solution)/shard_map/ppermute | solution.py:482
  18.8 6.7 %copy-start = (f32[7,32,128]{2,1,0:T(8,128)S(1)}, f32[7,32,128]{2,1,0:T(8,128)}, u32[]{:S(2)}) copy-start(f32[7,32,128]{2,1,0:T(8,128)} %fields_ref.3) | copy-start | bytes 344068
  18.8 7.1 %collective-permute-start.5 = (f32[48,128]{1,0:T(8,128)S(1)}, f32[48,128]{1,0:T(8,128)S(1)}, u32[]{:S(2)}, u32[]{:S(2)}) collective-permute-start(f32[48,128]{1,0:T(8,128)S(1)} %get-tuple-element.18), channel_id=1, source_target_pairs={{1,2},{2,1},{3,4},{4,3},{5,6},{6,5},{7,8},{8,7},{9,10},{10,9},{12,... | collective-permute-start | bytes 73736 | tf_op jit(solution)/shard_map/ppermute | solution.py:495
  20.8 5.8 %collective-permute-start.4 = (f32[48,128]{1,0:T(8,128)S(1)}, f32[48,128]{1,0:T(8,128)S(1)}, u32[]{:S(2)}, u32[]{:S(2)}) collective-permute-start(f32[48,128]{1,0:T(8,128)S(1)} %get-tuple-element.18), channel_id=1, source_target_pairs={{0,1},{1,0},{2,3},{3,2},{4,5},{5,4},{6,7},{7,6},{8,9},{9,8},{10,11... | collective-permute-start | bytes 73736 | tf_op jit(solution)/shard_map/ppermute | solution.py:495
  24.8 1.7 %collective-permute-start.3 = (f32[48,128]{1,0:T(8,128)S(1)}, f32[48,128]{1,0:T(8,128)S(1)}, u32[]{:S(2)}, u32[]{:S(2)}) collective-permute-start(f32[48,128]{1,0:T(8,128)S(1)} %get-tuple-element.18), channel_id=1, source_target_pairs={{11,0},{0,11},{22,23},{23,22},{34,35},{35,34},{46,47},{47,46},{58,... | collective-permute-start | bytes 73736 | tf_op jit(solution)/shard_map/ppermute | solution.py:495

commit v11 on v10

--- a/solution.py
+++ b/solution.py
@@ -173,8 +173,14 @@
 def down_two(ref, firsts, by_rows, by_cols, step=0):
     p = lane(32) + step
     index = (2 * p) & 127
-    parts = [paired_lanes(rows_halved(ref, first, by_rows), index, by_cols) for first in firsts]
-    return parts[0] if len(parts) == 1 else jnp.where((p & 127) < 64, parts[0], parts[1])
+    parts = [rows_halved(ref, first, by_rows) for first in firsts]
+    if len(parts) == 1:
+        return paired_lanes(parts[0], index, by_cols)
+    inside = (p & 127) < 64
+    picks = []
+    for k in range(2 if by_cols else 1):
+        picks.append(jnp.where(inside, gather_lanes(parts[0], index + k), gather_lanes(parts[1], index + k)))
+    return 0.5 * (picks[0] + picks[1]) if by_cols else picks[0]
 
 
 def down_one(ref, first, by_rows, by_cols, step=0):
@@ -309,8 +315,7 @@
         )
 
     def swapped(value):
-        outside = jnp.where(p8 < 48, pltpu.roll(value, 48, 1), pltpu.roll(value, 80, 1))
-        return jnp.where((p8 >= 48) & (p8 < 80), value, outside)
+        return gather_lanes(value, jnp.where(p8 < 48, p8 + 80, jnp.where(p8 < 80, p8, p8 - 80)))
 
     def turn(slot, value):
         value = value.T
@@ -355,8 +360,8 @@
     def sweep_x():
         items = [(turned, i) for i in range(6)]
         sweep(items, leftx, TPAD - 8, 8, None)
-        for row in [TPAD + 16 * c for c in range(9)]:
-            count = 8 if row == TPAD + 128 else 16
+        for row in range(TPAD, TPAD + 136, 8):
+            count = min(8, TPAD + 136 - row)
             flux = sweep(items, leftx, row, count, (turned, 6))
             for i, value in enumerate(flux):
                 fluxx[i, row : row + count, :] = value
@@ -367,11 +372,11 @@
 
     def sweep_y(last):
         items = [(base, 0), (prim, 1), (prim, 0), (prim, 2), (prim, 4), (base, 4)]
-        for row in chunks:
-            flux = sweep(items, lefty, row, 16, (base, 6))
+        for row in range(PAD, PAD + 128, 8):
+            flux = sweep(items, lefty, row, 8, (base, 6))
             for i, n in enumerate((0, 2, 1, 3, 5, 4)):
                 if i == 5 or row < SIDE or not last:
-                    fluxy[i, row : row + 16, :] = flux[n]
+                    fluxy[i, row : row + 8, :] = flux[n]
 
     def beside_cols(parts, back):
         parts = [pltpu.roll(part, 1 if back else 127, 1) for part in parts]

time: 30.1 us -> 30 us (level)
  no operation moved by 1% of the time
where the time goes in v11:
time: 30 us; the launch traced here: 29.7 us
  starting transfers between devices  21.6 us (72%)
  Pallas kernels  4.71 us (16%)
  waiting for transfers between devices  3.3 us (11%)
    ppermute x3, starting transfers between devices, swapped_pairs(): return lax.ppermute(value, axis, pairs + [(j, i) for i, j in pairs])  15 us
    ppermute x3, starting transfers between devices, swapped_subs(): return lax.ppermute(value, ('seg', 'sub'), pairs)  6.62 us
    pallas_call x1, Pallas kernels, on_device(): pl.pallas_call(main_kernel, out_shape=shape(fields.shape, F32), in_specs=...  3.18 us
    ppermute x3, waiting for transfers between devices, swapped_pairs(): return lax.ppermute(value, axis, pairs + [(j, i) for i, j in pairs])  2.65 us
    pallas_call x1, Pallas kernels, on_device(): pl.pallas_call(own_kernel, out_shape=(shape((128, COLS), jnp.int32), shap...  1.05 us
    ppermute x3, waiting for transfers between devices, swapped_subs(): return lax.ppermute(value, ('seg', 'sub'), pairs)  0.65 us
  transfers between devices with their start and end apart: 6, of which 2 were waited for; matrix products, arithmetic and copies ran while one was open for 0% of the time, Pallas kernels for 5%

profile of v11, /device:TPU:1, one launch (start us, length us, event | category | flops | bytes accessed | tf_op | source)
XLA Modules:
  0.0 29.7 jit_solution(12155757716595840336)
XLA Ops:
  0.0 12.4 %collective-permute-start.2 = (f32[7,32,128]{2,1,0:T(8,128)}, f32[7,32,128]{2,1,0:T(8,128)S(1)}, u32[]{:S(2)}, u32[]{:S(2)}) collective-permute-start(f32[7,32,128]{2,1,0:T(8,128)} %fields_ref.3), channel_id=1, source_target_pairs={{0,12},{12,0},{1,13},{13,1},{2,14},{14,2},{3,15},{15,3},{4,16},{16... | collective-permute-start | bytes 344072 | tf_op jit(solution)/shard_map/ppermute | solution.py:487
  12.4 1.9 %collective-permute-start.1 = (f32[7,32,128]{2,1,0:T(8,128)}, f32[7,32,128]{2,1,0:T(8,128)S(1)}, u32[]{:S(2)}, u32[]{:S(2)}) collective-permute-start(f32[7,32,128]{2,1,0:T(8,128)} %fields_ref.3), channel_id=1, source_target_pairs={{12,24},{36,48},{60,72},{84,96},{108,120},{132,144},{156,168},{180... | collective-permute-start | bytes 344072 | tf_op jit(solution)/shard_map/ppermute | solution.py:487
  14.4 0.7 %collective-permute-start = (f32[7,32,128]{2,1,0:T(8,128)}, f32[7,32,128]{2,1,0:T(8,128)S(1)}, u32[]{:S(2)}, u32[]{:S(2)}) collective-permute-start(f32[7,32,128]{2,1,0:T(8,128)} %fields_ref.3), channel_id=1, source_target_pairs={{24,36},{48,60},{72,84},{96,108},{120,132},{144,156},{168,180},{19... | collective-permute-start | bytes 344072 | tf_op jit(solution)/shard_map/ppermute | solution.py:487
  15.0 1.1 %shard_map.28 = (s32[128,128]{1,0:T(8,128)S(1)}, s32[104,128]{1,0:T(8,128)S(1)}, s32[2,32,128]{2,1,0:T(8,128)S(1)}, f32[32,128]{1,0:T(8,128)S(1)}) custom-call(s32[12,64]{1,0:T(8,128)} %bitcast.1, f32[7,32,128]{2,1,0:T(8,128)} %fields_ref.3), custom_call_target="tpu_custom_call" | custom-call | tf_op jit(solution)/shard_map/pallas_call | solution.py:510
  16.1 0.0 collective-permute-done.2.first_ref
  16.1 2.6 %collective-permute-done.1.far_ref = f32[7,32,128]{2,1,0:T(8,128)S(1)} collective-permute-done((f32[7,32,128]{2,1,0:T(8,128)}, f32[7,32,128]{2,1,0:T(8,128)S(1)}, u32[]{:S(2)}, u32[]{:S(2)}) %collective-permute-start.1) | collective-permute-done | bytes 114720 | tf_op jit(solution)/shard_map/ppermute | solution.py:487
  18.7 0.0 collective-permute-done.close_ref
  18.8 0.0 copy-start
  18.8 0.1 shard_map.29
  18.8 1.9 %collective-permute-start.5 = (f32[48,128]{1,0:T(8,128)S(1)}, f32[48,128]{1,0:T(8,128)S(1)}, u32[]{:S(2)}, u32[]{:S(2)}) collective-permute-start(f32[48,128]{1,0:T(8,128)S(1)} %get-tuple-element.18), channel_id=1, source_target_pairs={{1,2},{2,1},{3,4},{4,3},{5,6},{6,5},{7,8},{8,7},{9,10},{10,9},{12,... | collective-permute-start | bytes 73736 | tf_op jit(solution)/shard_map/ppermute | solution.py:500
  20.8 4.0 %collective-permute-start.4 = (f32[48,128]{1,0:T(8,128)S(1)}, f32[48,128]{1,0:T(8,128)S(1)}, u32[]{:S(2)}, u32[]{:S(2)}) collective-permute-start(f32[48,128]{1,0:T(8,128)S(1)} %get-tuple-element.18), channel_id=1, source_target_pairs={{0,1},{1,0},{2,3},{3,2},{4,5},{5,4},{6,7},{7,6},{8,9},{9,8},{10,11... | collective-permute-start | bytes 73736 | tf_op jit(solution)/shard_map/ppermute | solution.py:500
  24.8 0.7 %collective-permute-start.3 = (f32[48,128]{1,0:T(8,128)S(1)}, f32[48,128]{1,0:T(8,128)S(1)}, u32[]{:S(2)}, u32[]{:S(2)}) collective-permute-start(f32[48,128]{1,0:T(8,128)S(1)} %get-tuple-element.18), channel_id=1, source_target_pairs={{11,0},{0,11},{22,23},{23,22},{34,35},{35,34},{46,47},{47,46},{58,... | collective-permute-start | bytes 73736 | tf_op jit(solution)/shard_map/ppermute | solution.py:500
  25.5 0.0 copy-done
  25.5 0.4 %shard_map.30.own_ref = f32[7,144,128]{2,1,0:T(8,128)S(1)} custom-call(s32[128,128]{1,0:T(8,128)S(1)} %get-tuple-element.12.lev, f32[7,32,128]{2,1,0:T(8,128)S(1)} %copy-done, f32[7,8,128]{2,1,0:T(8,128)S(1)} %get-tuple-element.16.below_ref, f32[7,8,128]{2,1,0:T(8,128)S(1)} %get-tuple-element.17.above_ref), custom_call_target="tpu_custom_call" | custom-call | tf_op jit(solution)/shard_map/pallas_call | solution.py:537
  25.9 0.0 collective-permute-done.5.near_ref
  25.9 0.6 %collective-permute-done.4.far_ref = f32[48,128]{1,0:T(8,128)S(1)} collective-permute-done((f32[48,128]{1,0:T(8,128)S(1)}, f32[48,128]{1,0:T(8,128)S(1)}, u32[]{:S(2)}, u32[]{:S(2)}) %collective-permute-start.4) | collective-permute-done | bytes 24608 | tf_op jit(solution)/shard_map/ppermute | solution.py:500
  26.6 0.0 collective-permute-done.3.last_ref
  26.6 3.2 %shard_map.31 = f32[7,32,128]{2,1,0:T(8,128)} custom-call(s32[128,128]{1,0:T(8,128)S(1)} %get-tuple-element.12.lev, s32[104,128]{1,0:T(8,128)S(1)} %get-tuple-element.13.lev_strips, s32[2,32,128]{2,1,0:T(8,128)S(1)} %get-tuple-element.14.corner, f32[7,32,128]{2,1,0:T(8,128)S(1)} %copy-done, f32[7,144,128]{2,1,0:T(8,128)S(1)} %shard_map.30.own_ref, ...), custom_call_target="tpu_custom_call" | custom-call | tf_op jit(solution)/shard_map/pallas_call | solution.py:552
Async XLA Ops:
  0.0 16.1 %collective-permute-start.2 = (f32[7,32,128]{2,1,0:T(8,128)}, f32[7,32,128]{2,1,0:T(8,128)S(1)}, u32[]{:S(2)}, u32[]{:S(2)}) collective-permute-start(f32[7,32,128]{2,1,0:T(8,128)} %fields_ref.3), channel_id=1, source_target_pairs={{0,12},{12,0},{1,13},{13,1},{2,14},{14,2},{3,15},{15,3},{4,16},{16... | collective-permute-start | bytes 344072 | tf_op jit(solution)/shard_map/ppermute | solution.py:487
  12.4 6.3 %collective-permute-start.1 = (f32[7,32,128]{2,1,0:T(8,128)}, f32[7,32,128]{2,1,0:T(8,128)S(1)}, u32[]{:S(2)}, u32[]{:S(2)}) collective-permute-start(f32[7,32,128]{2,1,0:T(8,128)} %fields_ref.3), channel_id=1, source_target_pairs={{12,24},{36,48},{60,72},{84,96},{108,120},{132,144},{156,168},{180... | collective-permute-start | bytes 344072 | tf_op jit(solution)/shard_map/ppermute | solution.py:487
  14.4 4.4 %collective-permute-start = (f32[7,32,128]{2,1,0:T(8,128)}, f32[7,32,128]{2,1,0:T(8,128)S(1)}, u32[]{:S(2)}, u32[]{:S(2)}) collective-permute-start(f32[7,32,128]{2,1,0:T(8,128)} %fields_ref.3), channel_id=1, source_target_pairs={{24,36},{48,60},{72,84},{96,108},{120,132},{144,156},{168,180},{19... | collective-permute-start | bytes 344072 | tf_op jit(solution)/shard_map/ppermute | solution.py:487
  18.8 6.7 %copy-start = (f32[7,32,128]{2,1,0:T(8,128)S(1)}, f32[7,32,128]{2,1,0:T(8,128)}, u32[]{:S(2)}) copy-start(f32[7,32,128]{2,1,0:T(8,128)} %fields_ref.3) | copy-start | bytes 344068
  18.8 7.1 %collective-permute-start.5 = (f32[48,128]{1,0:T(8,128)S(1)}, f32[48,128]{1,0:T(8,128)S(1)}, u32[]{:S(2)}, u32[]{:S(2)}) collective-permute-start(f32[48,128]{1,0:T(8,128)S(1)} %get-tuple-element.18), channel_id=1, source_target_pairs={{1,2},{2,1},{3,4},{4,3},{5,6},{6,5},{7,8},{8,7},{9,10},{10,9},{12,... | collective-permute-start | bytes 73736 | tf_op jit(solution)/shard_map/ppermute | solution.py:500
  20.8 5.8 %collective-permute-start.4 = (f32[48,128]{1,0:T(8,128)S(1)}, f32[48,128]{1,0:T(8,128)S(1)}, u32[]{:S(2)}, u32[]{:S(2)}) collective-permute-start(f32[48,128]{1,0:T(8,128)S(1)} %get-tuple-element.18), channel_id=1, source_target_pairs={{0,1},{1,0},{2,3},{3,2},{4,5},{5,4},{6,7},{7,6},{8,9},{9,8},{10,11... | collective-permute-start | bytes 73736 | tf_op jit(solution)/shard_map/ppermute | solution.py:500
  24.8 1.7 %collective-permute-start.3 = (f32[48,128]{1,0:T(8,128)S(1)}, f32[48,128]{1,0:T(8,128)S(1)}, u32[]{:S(2)}, u32[]{:S(2)}) collective-permute-start(f32[48,128]{1,0:T(8,128)S(1)} %get-tuple-element.18), channel_id=1, source_target_pairs={{11,0},{0,11},{22,23},{23,22},{34,35},{35,34},{46,47},{47,46},{58,... | collective-permute-start | bytes 73736 | tf_op jit(solution)/shard_map/ppermute | solution.py:500

commit v12 on v11

--- a/solution.py
+++ b/solution.py
@@ -103,16 +103,26 @@
         cols_ref[r : r + 8, :] = packed_cols(lambda f: fields_ref[f, r : r + 8, :], own)
 
 
-def cols_kernel(lev, cols_ref, close_ref, far_ref, first_ref, out_ref, below_ref, above_ref):
-    seg = lax.axis_index("seg")
-    even = jnp.full((8, COLS), lax.rem(seg, 2)) == 0
-    early = jnp.full((8, COLS), seg) < 2
+def cols_kernel(lev, cols_ref, third_ref, second_ref, first_ref, out_ref, below_ref, above_ref):
+    seg, size = lax.axis_index("seg"), lax.axis_size("seg")
+    seg = jnp.full((8, COLS), seg)
+    even = (seg & 1) == 0
+    head, tail = seg < 2, seg >= size - 1
+    far_second = head | tail | (seg == 2)
+    close_third = (seg == 2) | (seg == 3) | (seg >= size - 2)
     below_level, above_level = lev[0:8, :], lev[40:48, :]
+
+    def picked(values):
+        first, second, third = values
+        far = jnp.where(far_second, second, first)
+        return far, jnp.where(close_third, third, jnp.where(head, first, second))
+
     for f in range(7):
-        far, close, first = (last_rows(r, f, below_level) for r in (far_ref, close_ref, first_ref))
-        below_ref[f] = jnp.where(even, far, jnp.where(early, first, close))
-        close = jnp.where(early, first_ref[f, 0:8, :], close_ref[f, 0:8, :])
-        above_ref[f] = jnp.where(even, close, far_ref[f, 0:8, :])
+        refs = (first_ref, second_ref, third_ref)
+        far, close = picked([last_rows(ref, f, below_level) for ref in refs])
+        below_ref[f] = jnp.where(even, far, close)
+        far, close = picked([ref[f, 0:8, :] for ref in refs])
+        above_ref[f] = jnp.where(even, close, far)
     out_ref[0:8, :] = packed_cols(lambda f: below_ref[f], below_level)
     out_ref[8:40, :] = cols_ref[...]
     out_ref[40:48, :] = packed_cols(lambda f: above_ref[f], above_level)
@@ -481,10 +491,15 @@
         pltpu.make_async_copy(result.at[f], out_ref.at[f], sems.at[f]).wait()
 
 
-def swapped_pairs(value, axis, first, stop):
-    size = lax.axis_size(axis)
-    pairs = [(i, (i + 1) % size) for i in range(first, stop, 2)]
-    return lax.ppermute(value, axis, pairs + [(j, i) for i, j in pairs])
+def swapped_segs(value, turn):
+    size = lax.axis_size("seg")
+    starts = (
+        [0, *range(3, size - 2, 2)],
+        [size - 1, 1, *range(4, size - 2, 2)],
+        [2, size - 2] if size > 4 else [2],
+    )[turn]
+    pairs = [(i, (i + 1) % size) for i in starts]
+    return lax.ppermute(value, "seg", pairs + [(j, i) for i, j in pairs])
 
 
 def swapped_subs(value, turn):
@@ -503,10 +518,7 @@
 def on_device(fields, region_levels):
     shape = jax.ShapeDtypeStruct
     params = pltpu.CompilerParams(vmem_limit_bytes=32 * 1024 * 1024)
-    size = lax.axis_size("seg")
-    close = swapped_pairs(fields, "seg", 2, size)
-    far = swapped_pairs(fields, "seg", 1, size)
-    first = swapped_pairs(fields, "seg", 0, 2)
+    third, second, first = (swapped_segs(fields, turn) for turn in (2, 1, 0))
     lev, lev_strips, corner, cols = pl.pallas_call(
         own_kernel,
         out_shape=(
@@ -532,7 +544,7 @@
         in_specs=[VMEM] * 5,
         out_specs=(VMEM,) * 3,
         compiler_params=params,
-    )(lev, cols, close, far, first)
+    )(lev, cols, third, second, first)
     end, far, near = (swapped_subs(packed, turn) for turn in (2, 1, 0))
     own = pl.pallas_call(
         rows_kernel,

time: 30 us -> 30.1 us (level)
  no operation moved by 1% of the time
where the time goes in v12:
time: 30.1 us; the launch traced here: 29.7 us
  starting transfers between devices  21.6 us (72%)
  Pallas kernels  4.72 us (16%)
  waiting for transfers between devices  3.3 us (11%)
    ppermute x3, starting transfers between devices, swapped_segs(): return lax.ppermute(value, 'seg', pairs + [(j, i) for i, j in pairs])  15 us
    ppermute x3, starting transfers between devices, swapped_subs(): return lax.ppermute(value, ('seg', 'sub'), pairs)  6.62 us
    pallas_call x1, Pallas kernels, on_device(): pl.pallas_call(main_kernel, out_shape=shape(fields.shape, F32), in_specs=...  3.18 us
    ppermute x3, waiting for transfers between devices, swapped_segs(): return lax.ppermute(value, 'seg', pairs + [(j, i) for i, j in pairs])  2.65 us
    pallas_call x1, Pallas kernels, on_device(): pl.pallas_call(own_kernel, out_shape=(shape((128, COLS), jnp.int32), shap...  1.05 us
    ppermute x3, waiting for transfers between devices, swapped_subs(): return lax.ppermute(value, ('seg', 'sub'), pairs)  0.65 us
  transfers between devices with their start and end apart: 6, of which 2 were waited for; matrix products, arithmetic and copies ran while one was open for 0% of the time, Pallas kernels for 5%

profile of v12, /device:TPU:1, one launch (start us, length us, event | category | flops | bytes accessed | tf_op | source)
XLA Modules:
  0.0 29.7 jit_solution(13001776703958562946)
XLA Ops:
  0.0 12.4 %collective-permute-start.2 = (f32[7,32,128]{2,1,0:T(8,128)}, f32[7,32,128]{2,1,0:T(8,128)S(1)}, u32[]{:S(2)}, u32[]{:S(2)}) collective-permute-start(f32[7,32,128]{2,1,0:T(8,128)} %fields_ref.3), channel_id=1, source_target_pairs={{0,12},{36,48},{60,72},{84,96},{108,120},{132,144},{156,168},{180,... | collective-permute-start | bytes 344072 | tf_op jit(solution)/shard_map/ppermute | solution.py:502
  12.4 1.9 %collective-permute-start.1 = (f32[7,32,128]{2,1,0:T(8,128)}, f32[7,32,128]{2,1,0:T(8,128)S(1)}, u32[]{:S(2)}, u32[]{:S(2)}) collective-permute-start(f32[7,32,128]{2,1,0:T(8,128)} %fields_ref.3), channel_id=1, source_target_pairs={{756,0},{12,24},{48,60},{72,84},{96,108},{120,132},{144,156},{168,... | collective-permute-start | bytes 344072 | tf_op jit(solution)/shard_map/ppermute | solution.py:502
  14.4 0.7 %collective-permute-start = (f32[7,32,128]{2,1,0:T(8,128)}, f32[7,32,128]{2,1,0:T(8,128)S(1)}, u32[]{:S(2)}, u32[]{:S(2)}) collective-permute-start(f32[7,32,128]{2,1,0:T(8,128)} %fields_ref.3), channel_id=1, source_target_pairs={{24,36},{744,756},{36,24},{756,744},{25,37},{745,757},{37,25},{757... | collective-permute-start | bytes 344072 | tf_op jit(solution)/shard_map/ppermute | solution.py:502
  15.0 1.1 %shard_map.28 = (s32[128,128]{1,0:T(8,128)S(1)}, s32[104,128]{1,0:T(8,128)S(1)}, s32[2,32,128]{2,1,0:T(8,128)S(1)}, f32[32,128]{1,0:T(8,128)S(1)}) custom-call(s32[12,64]{1,0:T(8,128)} %bitcast.1, f32[7,32,128]{2,1,0:T(8,128)} %fields_ref.3), custom_call_target="tpu_custom_call" | custom-call | tf_op jit(solution)/shard_map/pallas_call | solution.py:522
  16.1 0.0 collective-permute-done.2.first_ref
  16.1 2.6 %collective-permute-done.1.second_ref = f32[7,32,128]{2,1,0:T(8,128)S(1)} collective-permute-done((f32[7,32,128]{2,1,0:T(8,128)}, f32[7,32,128]{2,1,0:T(8,128)S(1)}, u32[]{:S(2)}, u32[]{:S(2)}) %collective-permute-start.1) | collective-permute-done | bytes 114720 | tf_op jit(solution)/shard_map/ppermute | solution.py:502
  18.7 0.0 collective-permute-done.third_ref
  18.8 0.0 copy-start
  18.8 0.1 shard_map.29
  18.9 1.9 %collective-permute-start.5 = (f32[48,128]{1,0:T(8,128)S(1)}, f32[48,128]{1,0:T(8,128)S(1)}, u32[]{:S(2)}, u32[]{:S(2)}) collective-permute-start(f32[48,128]{1,0:T(8,128)S(1)} %get-tuple-element.18), channel_id=1, source_target_pairs={{1,2},{2,1},{3,4},{4,3},{5,6},{6,5},{7,8},{8,7},{9,10},{10,9},{12,... | collective-permute-start | bytes 73736 | tf_op jit(solution)/shard_map/ppermute | solution.py:515
  20.8 4.0 %collective-permute-start.4 = (f32[48,128]{1,0:T(8,128)S(1)}, f32[48,128]{1,0:T(8,128)S(1)}, u32[]{:S(2)}, u32[]{:S(2)}) collective-permute-start(f32[48,128]{1,0:T(8,128)S(1)} %get-tuple-element.18), channel_id=1, source_target_pairs={{0,1},{1,0},{2,3},{3,2},{4,5},{5,4},{6,7},{7,6},{8,9},{9,8},{10,11... | collective-permute-start | bytes 73736 | tf_op jit(solution)/shard_map/ppermute | solution.py:515
  24.8 0.7 %collective-permute-start.3 = (f32[48,128]{1,0:T(8,128)S(1)}, f32[48,128]{1,0:T(8,128)S(1)}, u32[]{:S(2)}, u32[]{:S(2)}) collective-permute-start(f32[48,128]{1,0:T(8,128)S(1)} %get-tuple-element.18), channel_id=1, source_target_pairs={{11,0},{0,11},{22,23},{23,22},{34,35},{35,34},{46,47},{47,46},{58,... | collective-permute-start | bytes 73736 | tf_op jit(solution)/shard_map/ppermute | solution.py:515
  25.5 0.0 copy-done
  25.5 0.4 %shard_map.30.own_ref = f32[7,144,128]{2,1,0:T(8,128)S(1)} custom-call(s32[128,128]{1,0:T(8,128)S(1)} %get-tuple-element.12.lev, f32[7,32,128]{2,1,0:T(8,128)S(1)} %copy-done, f32[7,8,128]{2,1,0:T(8,128)S(1)} %get-tuple-element.16.below_ref, f32[7,8,128]{2,1,0:T(8,128)S(1)} %get-tuple-element.17.above_ref), custom_call_target="tpu_custom_call" | custom-call | tf_op jit(solution)/shard_map/pallas_call | solution.py:549
  25.9 0.0 collective-permute-done.5.near_ref
  25.9 0.6 %collective-permute-done.4.far_ref = f32[48,128]{1,0:T(8,128)S(1)} collective-permute-done((f32[48,128]{1,0:T(8,128)S(1)}, f32[48,128]{1,0:T(8,128)S(1)}, u32[]{:S(2)}, u32[]{:S(2)}) %collective-permute-start.4) | collective-permute-done | bytes 24608 | tf_op jit(solution)/shard_map/ppermute | solution.py:515
  26.6 0.0 collective-permute-done.3.last_ref
  26.6 3.2 %shard_map.31 = f32[7,32,128]{2,1,0:T(8,128)} custom-call(s32[128,128]{1,0:T(8,128)S(1)} %get-tuple-element.12.lev, s32[104,128]{1,0:T(8,128)S(1)} %get-tuple-element.13.lev_strips, s32[2,32,128]{2,1,0:T(8,128)S(1)} %get-tuple-element.14.corner, f32[7,32,128]{2,1,0:T(8,128)S(1)} %copy-done, f32[7,144,128]{2,1,0:T(8,128)S(1)} %shard_map.30.own_ref, ...), custom_call_target="tpu_custom_call" | custom-call | tf_op jit(solution)/shard_map/pallas_call | solution.py:564
Async XLA Ops:
  0.0 16.1 %collective-permute-start.2 = (f32[7,32,128]{2,1,0:T(8,128)}, f32[7,32,128]{2,1,0:T(8,128)S(1)}, u32[]{:S(2)}, u32[]{:S(2)}) collective-permute-start(f32[7,32,128]{2,1,0:T(8,128)} %fields_ref.3), channel_id=1, source_target_pairs={{0,12},{36,48},{60,72},{84,96},{108,120},{132,144},{156,168},{180,... | collective-permute-start | bytes 344072 | tf_op jit(solution)/shard_map/ppermute | solution.py:502
  12.4 6.3 %collective-permute-start.1 = (f32[7,32,128]{2,1,0:T(8,128)}, f32[7,32,128]{2,1,0:T(8,128)S(1)}, u32[]{:S(2)}, u32[]{:S(2)}) collective-permute-start(f32[7,32,128]{2,1,0:T(8,128)} %fields_ref.3), channel_id=1, source_target_pairs={{756,0},{12,24},{48,60},{72,84},{96,108},{120,132},{144,156},{168,... | collective-permute-start | bytes 344072 | tf_op jit(solution)/shard_map/ppermute | solution.py:502
  14.4 4.4 %collective-permute-start = (f32[7,32,128]{2,1,0:T(8,128)}, f32[7,32,128]{2,1,0:T(8,128)S(1)}, u32[]{:S(2)}, u32[]{:S(2)}) collective-permute-start(f32[7,32,128]{2,1,0:T(8,128)} %fields_ref.3), channel_id=1, source_target_pairs={{24,36},{744,756},{36,24},{756,744},{25,37},{745,757},{37,25},{757... | collective-permute-start | bytes 344072 | tf_op jit(solution)/shard_map/ppermute | solution.py:502
  18.8 6.7 %copy-start = (f32[7,32,128]{2,1,0:T(8,128)S(1)}, f32[7,32,128]{2,1,0:T(8,128)}, u32[]{:S(2)}) copy-start(f32[7,32,128]{2,1,0:T(8,128)} %fields_ref.3) | copy-start | bytes 344068
  18.9 7.1 %collective-permute-start.5 = (f32[48,128]{1,0:T(8,128)S(1)}, f32[48,128]{1,0:T(8,128)S(1)}, u32[]{:S(2)}, u32[]{:S(2)}) collective-permute-start(f32[48,128]{1,0:T(8,128)S(1)} %get-tuple-element.18), channel_id=1, source_target_pairs={{1,2},{2,1},{3,4},{4,3},{5,6},{6,5},{7,8},{8,7},{9,10},{10,9},{12,... | collective-permute-start | bytes 73736 | tf_op jit(solution)/shard_map/ppermute | solution.py:515
  20.8 5.8 %collective-permute-start.4 = (f32[48,128]{1,0:T(8,128)S(1)}, f32[48,128]{1,0:T(8,128)S(1)}, u32[]{:S(2)}, u32[]{:S(2)}) collective-permute-start(f32[48,128]{1,0:T(8,128)S(1)} %get-tuple-element.18), channel_id=1, source_target_pairs={{0,1},{1,0},{2,3},{3,2},{4,5},{5,4},{6,7},{7,6},{8,9},{9,8},{10,11... | collective-permute-start | bytes 73736 | tf_op jit(solution)/shard_map/ppermute | solution.py:515
  24.8 1.7 %collective-permute-start.3 = (f32[48,128]{1,0:T(8,128)S(1)}, f32[48,128]{1,0:T(8,128)S(1)}, u32[]{:S(2)}, u32[]{:S(2)}) collective-permute-start(f32[48,128]{1,0:T(8,128)S(1)} %get-tuple-element.18), channel_id=1, source_target_pairs={{11,0},{0,11},{22,23},{23,22},{34,35},{35,34},{46,47},{47,46},{58,... | collective-permute-start | bytes 73736 | tf_op jit(solution)/shard_map/ppermute | solution.py:515

commit v13 on v12

--- a/solution.py
+++ b/solution.py
@@ -61,7 +61,7 @@
     return packed
 
 
-def own_kernel(levels_hbm, fields_hbm, lev, lev_strips, corner, cols_ref, levels_ref, fields_ref, held, sems):
+def own_kernel(levels_hbm, fields_hbm, lev, lev_strips, corner, cols_ref, fields_ref, levels_ref, held, sems):
     copies = [
         pltpu.make_async_copy(levels_hbm, levels_ref, sems.at[0]),
         pltpu.make_async_copy(fields_hbm, fields_ref, sems.at[1]),
@@ -103,7 +103,19 @@
         cols_ref[r : r + 8, :] = packed_cols(lambda f: fields_ref[f, r : r + 8, :], own)
 
 
-def cols_kernel(lev, cols_ref, third_ref, second_ref, first_ref, out_ref, below_ref, above_ref):
+def cols_kernel(
+    lev,
+    cols_ref,
+    fields_ref,
+    first_ref,
+    third_ref,
+    second_ref,
+    out_ref,
+    below_ref,
+    above_ref,
+    own_ref,
+    win,
+):
     seg, size = lax.axis_index("seg"), lax.axis_size("seg")
     seg = jnp.full((8, COLS), seg)
     even = (seg & 1) == 0
@@ -126,6 +138,10 @@
     out_ref[0:8, :] = packed_cols(lambda f: below_ref[f], below_level)
     out_ref[8:40, :] = cols_ref[...]
     out_ref[40:48, :] = packed_cols(lambda f: above_ref[f], above_level)
+
+    @pl.when(lax.axis_index("sub") == 0)
+    def _():
+        own_windows(lev, fields_ref, below_ref, above_ref, own_ref, win)
 
 
 def minmod(a, b):
@@ -221,7 +237,13 @@
         out[f, MID : MID + 32, :] = jnp.where(coarse32, coarse, medium)
 
 
-def rows_kernel(lev, fields_ref, below_ref, above_ref, out_ref, win):
+def rows_kernel(lev, fields_ref, below_ref, above_ref, held_ref, out_ref, win):
+    @pl.when(lax.axis_index("sub") != 0)
+    def _():
+        own_windows(lev, fields_ref, below_ref, above_ref, out_ref, win)
+
+
+def own_windows(lev, fields_ref, below_ref, above_ref, out_ref, win):
     p8 = lane(8)
     is_coarse = (p8 >= 72) & (p8 < 120)
 
@@ -519,41 +541,44 @@
     shape = jax.ShapeDtypeStruct
     params = pltpu.CompilerParams(vmem_limit_bytes=32 * 1024 * 1024)
     third, second, first = (swapped_segs(fields, turn) for turn in (2, 1, 0))
-    lev, lev_strips, corner, cols = pl.pallas_call(
+    lev, lev_strips, corner, cols, tile = pl.pallas_call(
         own_kernel,
         out_shape=(
             shape((128, COLS), jnp.int32),
             shape((104, COLS), jnp.int32),
             shape((2, 32, COLS), jnp.int32),
             shape((32, COLS), F32),
+            shape(fields.shape, F32),
         ),
         in_specs=[HBM] * 2,
-        out_specs=(VMEM,) * 4,
+        out_specs=(VMEM,) * 5,
         scratch_shapes=[
             pltpu.VMEM(region_levels.shape[::-1], jnp.int32),
-            pltpu.VMEM(fields.shape, F32),
             pltpu.VMEM((24, COLS), jnp.int32),
             pltpu.SemaphoreType.DMA((2,)),
         ],
         compiler_params=params,
     )(*(pltpu.with_memory_space_constraint(x, pltpu.HBM) for x in (region_levels.T, fields)))
     rows = shape((7, 8, COLS), F32)
-    packed, below, above = pl.pallas_call(
+    windows = shape((7, PAD + 136, COLS), F32)
+    packed, below, above, own = pl.pallas_call(
         cols_kernel,
-        out_shape=(shape((48, COLS), F32), rows, rows),
-        in_specs=[VMEM] * 5,
-        out_specs=(VMEM,) * 3,
+        out_shape=(shape((48, COLS), F32), rows, rows, windows),
+        in_specs=[VMEM] * 6,
+        out_specs=(VMEM,) * 4,
+        scratch_shapes=[pltpu.VMEM(windows.shape, F32)],
         compiler_params=params,
-    )(lev, cols, third, second, first)
+    )(lev, cols, tile, first, third, second)
     end, far, near = (swapped_subs(packed, turn) for turn in (2, 1, 0))
     own = pl.pallas_call(
         rows_kernel,
-        out_shape=shape((7, PAD + 136, COLS), F32),
-        in_specs=[VMEM] * 4,
+        out_shape=windows,
+        in_specs=[VMEM] * 5,
         out_specs=VMEM,
+        input_output_aliases={4: 0},
         scratch_shapes=[pltpu.VMEM((7, PAD + 136, COLS), F32)],
         compiler_params=params,
-    )(lev, fields, below, above)
+    )(lev, tile, below, above, own)
 
     def window(*lead):
         return pltpu.VMEM((*lead, PAD + 136, COLS), F32)
@@ -584,7 +609,7 @@
             pltpu.SemaphoreType.DMA((7,)),
         ],
         compiler_params=params,
-    )(lev, lev_strips, corner, fields, own, end, far, near)
+    )(lev, lev_strips, corner, tile, own, end, far, near)
 
 
 def solution(mesh):

time: 30.1 us -> 30.4 us (level)
  waiting for transfers between devices: 3.3 us -> 4.08 us
  starting transfers between devices: 21.6 us -> 21.2 us
    ppermute x3, waiting for transfers between devices: 0.65 us -> 1.43 us  [swapped_subs(): return lax.ppermute(value, ('seg', 'sub'), pairs)]
    pallas_call x1, Pallas kernels: 0.09 us -> 0.49 us  [on_device(): pl.pallas_call(cols_kernel, out_shape=(shape((48, COLS), F32), rows, rows...]
    ppermute x3, starting transfers between devices: 6.62 us -> 6.22 us  [swapped_subs(): return lax.ppermute(value, ('seg', 'sub'), pairs)]
    pallas_call x1, Pallas kernels: 0.39 us -> 0.02 us  [on_device(): pl.pallas_call(rows_kernel, out_shape=windows, in_specs=[VMEM] * 5, out_s...]
  transfers between devices with their start and end apart: 6 -> 6, of which waited for: 2 -> 2; matrix products, arithmetic and copies ran while one was open for 0% -> 0% of each run, Pallas kernels for 5% -> 4%
where the time goes in v13:
time: 30.4 us; the launch traced here: 30.1 us
  starting transfers between devices  21.2 us (70%)
  Pallas kernels  4.75 us (16%)
  waiting for transfers between devices  4.08 us (13%)
    ppermute x3, starting transfers between devices, swapped_segs(): return lax.ppermute(value, 'seg', pairs + [(j, i) for i, j in pairs])  15 us
    ppermute x3, starting transfers between devices, swapped_subs(): return lax.ppermute(value, ('seg', 'sub'), pairs)  6.22 us
    pallas_call x1, Pallas kernels, on_device(): pl.pallas_call(main_kernel, out_shape=shape(fields.shape, F32), in_specs=...  3.18 us
    ppermute x3, waiting for transfers between devices, swapped_segs(): return lax.ppermute(value, 'seg', pairs + [(j, i) for i, j in pairs])  2.65 us
    ppermute x3, waiting for transfers between devices, swapped_subs(): return lax.ppermute(value, ('seg', 'sub'), pairs)  1.43 us
    pallas_call x1, Pallas kernels, on_device(): pl.pallas_call(own_kernel, out_shape=(shape((128, COLS), jnp.int32), shap...  1.05 us
  transfers between devices with their start and end apart: 6, of which 2 were waited for; matrix products, arithmetic and copies ran while one was open for 0% of the time, Pallas kernels for 4%

profile of v13, /device:TPU:1, one launch (start us, length us, event | category | flops | bytes accessed | tf_op | source)
XLA Modules:
  0.0 30.1 jit_solution(7978285662852514726)
XLA Ops:
  0.0 12.4 %collective-permute-start = (f32[7,32,128]{2,1,0:T(8,128)}, f32[7,32,128]{2,1,0:T(8,128)S(1)}, u32[]{:S(2)}, u32[]{:S(2)}) collective-permute-start(f32[7,32,128]{2,1,0:T(8,128)} %fields_hbm.1), channel_id=1, source_target_pairs={{0,12},{36,48},{60,72},{84,96},{108,120},{132,144},{156,168},{180,... | collective-permute-start | bytes 344072 | tf_op jit(solution)/shard_map/ppermute | solution.py:524
  12.4 1.9 %collective-permute-start.2 = (f32[7,32,128]{2,1,0:T(8,128)}, f32[7,32,128]{2,1,0:T(8,128)S(1)}, u32[]{:S(2)}, u32[]{:S(2)}) collective-permute-start(f32[7,32,128]{2,1,0:T(8,128)} %fields_hbm.1), channel_id=1, source_target_pairs={{756,0},{12,24},{48,60},{72,84},{96,108},{120,132},{144,156},{168,... | collective-permute-start | bytes 344072 | tf_op jit(solution)/shard_map/ppermute | solution.py:524
  14.3 0.7 %collective-permute-start.1 = (f32[7,32,128]{2,1,0:T(8,128)}, f32[7,32,128]{2,1,0:T(8,128)S(1)}, u32[]{:S(2)}, u32[]{:S(2)}) collective-permute-start(f32[7,32,128]{2,1,0:T(8,128)} %fields_hbm.1), channel_id=1, source_target_pairs={{24,36},{744,756},{36,24},{756,744},{25,37},{745,757},{37,25},{757... | collective-permute-start | bytes 344072 | tf_op jit(solution)/shard_map/ppermute | solution.py:524
  15.0 1.1 %shard_map.28 = (s32[128,128]{1,0:T(8,128)S(1)}, s32[104,128]{1,0:T(8,128)S(1)}, s32[2,32,128]{2,1,0:T(8,128)S(1)}, f32[32,128]{1,0:T(8,128)S(1)}, f32[7,32,128]{2,1,0:T(8,128)S(1)}) custom-call(s32[12,64]{1,0:T(8,128)} %bitcast.1, f32[7,32,128]{2,1,0:T(8,128)} %fields_hbm.1), custom_call_target="tpu_custom_call" | custom-call | tf_op jit(solution)/shard_map/pallas_call | solution.py:544
  16.1 0.0 collective-permute-done.first_ref
  16.1 2.6 %collective-permute-done.2.second_ref = f32[7,32,128]{2,1,0:T(8,128)S(1)} collective-permute-done((f32[7,32,128]{2,1,0:T(8,128)}, f32[7,32,128]{2,1,0:T(8,128)S(1)}, u32[]{:S(2)}, u32[]{:S(2)}) %collective-permute-start.2) | collective-permute-done | bytes 114720 | tf_op jit(solution)/shard_map/ppermute | solution.py:524
  18.7 0.0 collective-permute-done.1.third_ref
  18.7 0.5 %shard_map.29 = (f32[48,128]{1,0:T(8,128)S(1)}, f32[7,8,128]{2,1,0:T(8,128)S(1)}, f32[7,8,128]{2,1,0:T(8,128)S(1)}, f32[7,144,128]{2,1,0:T(8,128)S(1)}) custom-call(s32[128,128]{1,0:T(8,128)S(1)} %get-tuple-element.14.lev, f32[32,128]{1,0:T(8,128)S(1)} %get-tuple-element.18.cols_ref, f32[7,32,128]{2,1,0:T(8,128)S(1)} %get-tuple-element.17.fields_ref, ...), custom_call_target="tpu_custom_call" | custom-call | tf_op jit(solution)/shard_map/pallas_call | solution.py:564
  19.2 1.9 %collective-permute-start.5 = (f32[48,128]{1,0:T(8,128)S(1)}, f32[48,128]{1,0:T(8,128)S(1)}, u32[]{:S(2)}, u32[]{:S(2)}) collective-permute-start(f32[48,128]{1,0:T(8,128)S(1)} %get-tuple-element.22), channel_id=1, source_target_pairs={{1,2},{2,1},{3,4},{4,3},{5,6},{6,5},{7,8},{8,7},{9,10},{10,9},{12,... | collective-permute-start | bytes 73736 | tf_op jit(solution)/shard_map/ppermute | solution.py:537
  21.2 3.6 %collective-permute-start.4 = (f32[48,128]{1,0:T(8,128)S(1)}, f32[48,128]{1,0:T(8,128)S(1)}, u32[]{:S(2)}, u32[]{:S(2)}) collective-permute-start(f32[48,128]{1,0:T(8,128)S(1)} %get-tuple-element.22), channel_id=1, source_target_pairs={{0,1},{1,0},{2,3},{3,2},{4,5},{5,4},{6,7},{7,6},{8,9},{9,8},{10,11... | collective-permute-start | bytes 73736 | tf_op jit(solution)/shard_map/ppermute | solution.py:537
  24.8 0.7 %collective-permute-start.3 = (f32[48,128]{1,0:T(8,128)S(1)}, f32[48,128]{1,0:T(8,128)S(1)}, u32[]{:S(2)}, u32[]{:S(2)}) collective-permute-start(f32[48,128]{1,0:T(8,128)S(1)} %get-tuple-element.22), channel_id=1, source_target_pairs={{11,0},{0,11},{22,23},{23,22},{34,35},{35,34},{46,47},{47,46},{58,... | collective-permute-start | bytes 73736 | tf_op jit(solution)/shard_map/ppermute | solution.py:537
  25.5 0.0 collective-permute-done.5.near_ref
  25.5 1.4 %collective-permute-done.4.far_ref = f32[48,128]{1,0:T(8,128)S(1)} collective-permute-done((f32[48,128]{1,0:T(8,128)S(1)}, f32[48,128]{1,0:T(8,128)S(1)}, u32[]{:S(2)}, u32[]{:S(2)}) %collective-permute-start.4) | collective-permute-done | bytes 24608 | tf_op jit(solution)/shard_map/ppermute | solution.py:537
  27.0 0.0 collective-permute-done.3.last_ref
  27.0 3.2 %shard_map.31 = f32[7,32,128]{2,1,0:T(8,128)} custom-call(s32[128,128]{1,0:T(8,128)S(1)} %get-tuple-element.14.lev, s32[104,128]{1,0:T(8,128)S(1)} %get-tuple-element.15.lev_strips, s32[2,32,128]{2,1,0:T(8,128)S(1)} %get-tuple-element.16.corner, f32[7,32,128]{2,1,0:T(8,128)S(1)} %get-tuple-element.17.fields_ref, f32[7,144,128]{2,1,0:T(8,128)S(1)} %shard_map.30.own_ref, ...), custom_call_target="tpu_custom_call" | custom-call | tf_op jit(solution)/shard_map/pallas_call | solution.py:589
  (1 shorter events, 0.0 us)
Async XLA Ops:
  0.0 16.1 %collective-permute-start = (f32[7,32,128]{2,1,0:T(8,128)}, f32[7,32,128]{2,1,0:T(8,128)S(1)}, u32[]{:S(2)}, u32[]{:S(2)}) collective-permute-start(f32[7,32,128]{2,1,0:T(8,128)} %fields_hbm.1), channel_id=1, source_target_pairs={{0,12},{36,48},{60,72},{84,96},{108,120},{132,144},{156,168},{180,... | collective-permute-start | bytes 344072 | tf_op jit(solution)/shard_map/ppermute | solution.py:524
  12.4 6.3 %collective-permute-start.2 = (f32[7,32,128]{2,1,0:T(8,128)}, f32[7,32,128]{2,1,0:T(8,128)S(1)}, u32[]{:S(2)}, u32[]{:S(2)}) collective-permute-start(f32[7,32,128]{2,1,0:T(8,128)} %fields_hbm.1), channel_id=1, source_target_pairs={{756,0},{12,24},{48,60},{72,84},{96,108},{120,132},{144,156},{168,... | collective-permute-start | bytes 344072 | tf_op jit(solution)/shard_map/ppermute | solution.py:524
  14.3 4.4 %collective-permute-start.1 = (f32[7,32,128]{2,1,0:T(8,128)}, f32[7,32,128]{2,1,0:T(8,128)S(1)}, u32[]{:S(2)}, u32[]{:S(2)}) collective-permute-start(f32[7,32,128]{2,1,0:T(8,128)} %fields_hbm.1), channel_id=1, source_target_pairs={{24,36},{744,756},{36,24},{756,744},{25,37},{745,757},{37,25},{757... | collective-permute-start | bytes 344072 | tf_op jit(solution)/shard_map/ppermute | solution.py:524
  19.2 6.3 %collective-permute-start.5 = (f32[48,128]{1,0:T(8,128)S(1)}, f32[48,128]{1,0:T(8,128)S(1)}, u32[]{:S(2)}, u32[]{:S(2)}) collective-permute-start(f32[48,128]{1,0:T(8,128)S(1)} %get-tuple-element.22), channel_id=1, source_target_pairs={{1,2},{2,1},{3,4},{4,3},{5,6},{6,5},{7,8},{8,7},{9,10},{10,9},{12,... | collective-permute-start | bytes 73736 | tf_op jit(solution)/shard_map/ppermute | solution.py:537
  21.2 5.8 %collective-permute-start.4 = (f32[48,128]{1,0:T(8,128)S(1)}, f32[48,128]{1,0:T(8,128)S(1)}, u32[]{:S(2)}, u32[]{:S(2)}) collective-permute-start(f32[48,128]{1,0:T(8,128)S(1)} %get-tuple-element.22), channel_id=1, source_target_pairs={{0,1},{1,0},{2,3},{3,2},{4,5},{5,4},{6,7},{7,6},{8,9},{9,8},{10,11... | collective-permute-start | bytes 73736 | tf_op jit(solution)/shard_map/ppermute | solution.py:537
  24.8 2.1 %collective-permute-start.3 = (f32[48,128]{1,0:T(8,128)S(1)}, f32[48,128]{1,0:T(8,128)S(1)}, u32[]{:S(2)}, u32[]{:S(2)}) collective-permute-start(f32[48,128]{1,0:T(8,128)S(1)} %get-tuple-element.22), channel_id=1, source_target_pairs={{11,0},{0,11},{22,23},{23,22},{34,35},{35,34},{46,47},{47,46},{58,... | collective-permute-start | bytes 73736 | tf_op jit(solution)/shard_map/ppermute | solution.py:537
